TPU v7x, 256 devices: a whole 4x4x8 slice. The times are simulated.
256 devices in a mesh: ctx: 32 (over y, x, core), tp: 4 (over z_hi), dp: 2 (over z_lo).
Axes of the slice: x: 4, y: 4, z: 8 (z_hi: 4, z_lo: 2; z = z_hi * 2 + z_lo), core: 2. Of those that a mesh axis runs over, the one named last changes fastest.
Arguments:
- head_input: float32 [2, 7168, 2560], P('dp', 'ctx', 'tp'), may hold values from -24 to 24
- gate_input: float32 [2, 7168, 2560], P('dp', 'ctx', 'tp'), may hold values from -5 to 5
- log_decay: float32 [2, 40, 7168], P('dp', 'tp', 'ctx'), may hold values from -0.8 to 0, as said below
- in_b: float32 [2, 7168, 128], P('dp', 'ctx'), may hold values from -0.5 to 0.5
- in_c: float32 [2, 7168, 128], P('dp', 'ctx'), may hold values from -0.1875 to 0.1875
- skip: float32 [40], P('tp'), may hold values from 0.5 to 2
- norm_gain: float32 [2560], P('tp'), may hold values from 0.25 to 1.75
- w_out: float32 [2560, 2560], P('tp'), may hold values from -0.125 to 0.125
- d_out: float32 [2, 7168, 2560], P('dp', ('ctx', 'tp')), may hold values from -24 to 24
Outputs:
- out: float32 [2, 7168, 2560], P('dp', ('ctx', 'tp'))
- grad_input: float32 [2, 7168, 2560], P('dp', 'ctx', 'tp')
- grad_w_out_t: float32 [2560, 2560], P(('ctx', 'dp'), 'tp')
Inputs may be any that keep to these rules, and one draw needn't show every extreme that they name: `log_decay`: every entry is negative.
All inputs are finite; a program needn't handle non-finite values.
Results may differ from a plain program's by a relative error of at most 0.00023.
Values sent between devices are 32-bit elements; how exact they have to be, the bound alone decides.
No kernel may reach another device: no remote copies, remote signals or barrier semaphores. Data moves between devices by JAX's collectives and lax.ppermute only.
A program may use at most 128 MiB of HBM per device.

v0:
```python
import jax
import jax.numpy as jnp
from jax import lax
from jax.sharding import PartitionSpec as P

GROUP = 640


highest = lax.Precision.HIGHEST


def prefix(value, axis, join, neutral, backward):
    count, mine = (lax.axis_size(axis), lax.axis_index(axis))
    pieces = jax.tree.map(lambda part: lax.all_gather(part, axis), value)
    if backward:
        pieces = jax.tree.map(lambda part: part[::-1], pieces)
        mine = count - 1 - mine
    so_far = jax.tree.map(
        lambda part, zero: jnp.full_like(part, 0) + jnp.asarray(zero, part.dtype), value, neutral
    )

    def step(position, so_far):
        longer = join(so_far, jax.tree.map(lambda part: part[position], pieces))
        return jax.tree.map(lambda new, old: jnp.where(position < mine, new, old), longer, so_far)

    return lax.fori_loop(0, count - 1, step, so_far)


def ssd_output(x_heads, cum_decay, b_mat, c_mat, skip, state_in):
    length = x_heads.shape[0]
    causal = jnp.arange(length)[:, None] >= jnp.arange(length)[None, :]
    exponent = jnp.where(causal[None], cum_decay[:, :, None] - cum_decay[:, None, :], -1e30)
    scores = jnp.dot(c_mat, b_mat.T, precision=highest)
    weights = jnp.exp(exponent) * scores[None]
    result = jnp.einsum("hts,shp->thp", weights, x_heads, precision=highest)
    carried = jnp.einsum("tn,hnp->thp", c_mat, state_in, precision=highest)
    result = result + carried * jnp.exp(cum_decay).T[:, :, None]
    return result + skip[None, :, None] * x_heads


def span_state(x_heads, cum_decay, b_mat):
    to_end = jnp.exp(cum_decay[:, -1:] - cum_decay)
    return jnp.einsum("sn,hs,shp->hnp", b_mat, to_end, x_heads, precision=highest)


def gate_norm(values, gate, gain):
    gated = values * jax.nn.silu(gate)
    rows = gated.shape[0]
    grouped = gated.reshape(rows, -1, GROUP)
    scale = lax.rsqrt(jnp.mean(grouped * grouped, axis=2, keepdims=True) + 1e-05)
    return (grouped * scale).reshape(rows, -1) * gain[None, :]


def chain_combine(earlier, later):
    decay_early, state_early = earlier
    trailing_decay, state_late = later
    return (decay_early * trailing_decay, trailing_decay[:, None, None] * state_early + state_late)


def per_device(head_input, gate_input, log_decay, in_b, in_c, skip, norm_gain, w_out, d_out):
    heads = log_decay.shape[1]
    length = head_input.shape[1]
    width = head_input.shape[2]
    x_heads = head_input[0].reshape(length, heads, width // heads)
    cum_decay = jnp.cumsum(log_decay[0], axis=1)
    totals = cum_decay[:, -1]
    b_mat = in_b[0]
    c_mat = in_c[0]
    state_loc, state_vjp = jax.vjp(lambda inner: span_state(inner, cum_decay, b_mat), x_heads)
    identity = (jnp.ones_like(totals), jnp.zeros_like(state_loc))
    state_in = prefix((jnp.exp(totals), state_loc), "ctx", chain_combine, identity, False)[1]
    y_heads, output_vjp = jax.vjp(
        lambda inner: ssd_output(inner, cum_decay, b_mat, c_mat, skip, state_in), x_heads
    )
    y_flat = y_heads.reshape(length, width)
    normed, norm_vjp = jax.vjp(lambda values: gate_norm(values, gate_input[0], norm_gain), y_flat)
    out_share = lax.psum_scatter(
        jnp.dot(normed, w_out, precision=highest), "tp", scatter_dimension=0, tiled=True
    )
    d_full = lax.all_gather(d_out[0], "tp", axis=0, tiled=True)
    grad_share = lax.psum_scatter(
        lax.dot_general(d_full, normed, (((0,), (0,)), ((), ())), precision=highest),
        ("ctx", "dp"),
        scatter_dimension=0,
        tiled=True,
    )
    d_normed = lax.dot_general(d_full, w_out, (((1,), (1,)), ((), ())), precision=highest)
    d_heads = norm_vjp(d_normed)[0].reshape(length, heads, width // heads)
    grad_loc = jnp.einsum("tn,ht,thp->hnp", c_mat, jnp.exp(cum_decay), d_heads, precision=highest)
    back_identity = (jnp.ones_like(totals), jnp.zeros_like(grad_loc))
    grad_in = prefix((jnp.exp(totals), grad_loc), "ctx", chain_combine, back_identity, True)[1]
    grad_heads = output_vjp(d_heads)[0] + state_vjp(grad_in)[0]
    return (out_share[None], grad_heads.reshape(1, length, width), grad_share)


def solution(mesh):
    placed = (
        P("dp", "ctx", "tp"),
        P("dp", "ctx", "tp"),
        P("dp", "tp", "ctx"),
        P("dp", "ctx", None),
        P("dp", "ctx", None),
        P("tp"),
        P("tp"),
        P("tp", None),
        P("dp", ("ctx", "tp"), None),
    )
    return jax.shard_map(
        per_device,
        mesh=mesh,
        in_specs=placed,
        out_specs=(P("dp", ("ctx", "tp"), None), P("dp", "ctx", "tp"), P(("ctx", "dp"), "tp")),
        check_vma=False,
    )
```

profile of v0, /device:TPU:2, one launch (start us, length us, event | category | flops | bytes accessed | tf_op | source)
XLA Modules:
  0.0 891.4 jit_solution(2987644311405601738)
XLA Ops:
  9.3 1.3 copy.53
  10.6 2.3 convolution_bitcast_fusion.4
  15.3 63.2 %all-reduce.1 = f32[320]{0:T(512)S(1)} all-reduce(f32[320]{0:T(512)S(1)} %dynamic-update-slice), channel_id=2, replica_groups=mesh['ctx'=32,'tp'=4,'dp'=2] {'ctx'}, use_global_device_ids=true, to_apply=%add.1 | all-reduce | flops 320 | bytes 2560
  79.0 1.1 copy.57
  80.0 3.8 fusion.7
  83.8 44.5 %while.28 = (s32[]{:T(128)}, f32[10,128,64]{2,1,0:T(8,128)S(1)}, s32[]{:T(128)}, f32[32,10]{1,0:T(8,128)S(1)}, f32[32,10,128,64]{2,3,1,0:T(8,128)}, /*index=5*/s32[]{:T(128)}, s32[]{:T(128)}) while((s32[]{:T(128)}, f32[10,128,64]{2,1,0:T(8,128)S(1)}, s32[]{:T(128)}, f32[32,10]{1,0:T(8,128)S(1)}, f32[32,10,128,64]{2,3,1,0:T(8,128)}, ...), condition=%wide.region_3.4_spmd.clone, body=%wide.region_2.3_spmd.clone.sunk | while | flops 327684 | bytes 2293993 | solution.py:26
  83.9 1.0 constant_dynamic-slice_fusion.3
  85.3 1.0 constant_dynamic-slice_fusion.3
  86.7 1.0 constant_dynamic-slice_fusion.3
  89.6 1.0 constant_dynamic-slice_fusion.3
  91.0 1.0 constant_dynamic-slice_fusion.3
  92.5 1.0 constant_dynamic-slice_fusion.3
  93.9 1.0 constant_dynamic-slice_fusion.3
  101.1 1.0 constant_dynamic-slice_fusion.3
  102.6 1.0 constant_dynamic-slice_fusion.3
  106.9 1.0 constant_dynamic-slice_fusion.3
  128.4 3.6 multiply_reduce_fusion
  132.0 1.3 copy.56
  133.3 2.0 all-gather.10.cloned.1.call-done
  135.2 10.3 %multiply_reduce_fusion.1 = (f32[224]{0:T(256)S(1)}, f32[224,640]{1,0:T(8,128)S(1)}, f32[224,640]{1,0:T(8,128)S(1)}) fusion(f32[224,640]{1,0:T(8,128)S(1)} %copy.56, f32[1,224,640]{2,1,0:T(8,128)S(1)} %copy-done.5, f32[640]{0:T(1024)S(1)} %copy-done.9, f32[640,2560]{1,0:T(8,128)} %param.20, f32[1,224,2560]{2,1,0:T(8,128)} %all-gather.10.cloned.1.call-done), kind=kOutput, calls=%fused_computation.50 | convolution fusion | flops 4405166080 | bytes 11144576 | tf_op jit(solution)/shard_map/dot_general | solution.py:87
  145.6 7.7 convolution_bitcast_fusion
  153.6 1.1 copy.58
  154.7 2.7 convolution_bitcast_fusion.3
  158.8 4.9 fusion.17
  163.8 7.4 fusion.36
  171.2 570.7 %all-reduce.5.cloned.1.call-done = f32[2560,640]{0,1:T(8,128)} async-done(((f32[2560,640]{0,1:T(8,128)}), f32[2560,640]{0,1:T(8,128)}) %all-reduce.5.cloned.1.call-update) | async-done | bytes 6553616
  741.8 1.2 constant_dynamic-slice_fusion.1
  743.9 67.7 %all-gather.12.cloned.1.call-done = f32[320,128,64]{1,2,0:T(8,128)} async-done(((f32[10,128,64]{1,2,0:T(8,128)}), f32[320,128,64]{1,2,0:T(8,128)}) %all-gather.12.cloned.1.call-update) | async-done | bytes 10485776 | tf_op jit(solution)/shard_map/all_gather | solution.py:14
  811.5 15.0 %copy.59 = f32[32,10,128,64]{3,2,1,0:T(8,128)} copy(f32[32,10,128,64]{2,3,1,0:T(8,128)} %bitcast.121) | data formatting | bytes 20971520 | tf_op jit(solution)/shard_map/all_gather | solution.py:14
  826.5 16.3 %rev.7 = f32[32,10,128,64]{3,2,1,0:T(8,128)} reverse(f32[32,10,128,64]{3,2,1,0:T(8,128)} %copy.59), dimensions={0} | reverse | bytes 20971520 | tf_op jit(solution)/shard_map/rev | solution.py:16
  842.8 39.8 %while.29 = (s32[]{:T(128)}, f32[10,128,64]{2,1,0:T(8,128)S(1)}, s32[]{:T(128)}, f32[32,10]{1,0:T(8,128)S(1)}, f32[32,10,128,64]{3,2,1,0:T(8,128)}, /*index=5*/s32[]{:T(128)}, s32[]{:T(128)}) while((s32[]{:T(128)}, f32[10,128,64]{2,1,0:T(8,128)S(1)}, s32[]{:T(128)}, f32[32,10]{1,0:T(8,128)S(1)}, f32[32,10,128,64]{3,2,1,0:T(8,128)}, ...), condition=%wide.region_8.9_spmd.clone, body=%wide.region_7.8_spmd.clone.sunk | while | flops 327684 | bytes 983273 | solution.py:26
  842.8 1.3 fusion.63
  844.1 1.2 fusion.63
  845.4 1.2 fusion.63
  846.7 1.2 fusion.63
  848.0 1.2 fusion.63
  849.3 1.2 fusion.63
  850.5 1.2 fusion.63
  851.8 1.2 fusion.63
  853.1 1.2 fusion.63
  854.4 1.2 fusion.63
  855.7 1.2 fusion.63
  857.0 1.2 fusion.63
  858.2 1.2 fusion.63
  859.5 1.2 fusion.63
  860.8 1.2 fusion.63
  862.1 1.3 fusion.63
  863.4 1.2 fusion.63
  864.6 1.3 fusion.63
  865.9 1.2 fusion.63
  867.2 1.2 fusion.63
  868.5 1.2 fusion.63
  869.8 1.2 fusion.63
  871.1 1.2 fusion.63
  872.4 1.2 fusion.63
  873.6 1.2 fusion.63
  874.9 1.2 fusion.63
  876.2 1.2 fusion.63
  877.5 1.2 fusion.63
  878.8 1.2 fusion.63
  880.0 1.2 fusion.63
  881.3 1.2 fusion.63
  882.6 1.3 fusion.13
  883.9 1.0 copy.61
  (217 shorter events, 39.3 us)
Async XLA Ops:
  7.2 71.4 %copy-start = (f32[1,224,128]{2,1,0:T(8,128)S(1)}, f32[1,224,128]{2,1,0:T(8,128)}, u32[]{:S(2)}) copy-start(f32[1,224,128]{2,1,0:T(8,128)} %param.17) | copy-start | bytes 344068
  7.2 6.6 copy-start.13
  7.2 71.4 %copy-start.6 = (f32[1,224,128]{2,1,0:T(8,128)S(1)}, f32[1,224,128]{2,1,0:T(8,128)}, u32[]{:S(2)}) copy-start(f32[1,224,128]{2,1,0:T(8,128)} %param.16) | copy-start | bytes 344068
  7.2 71.8 %copy-start.5 = (f32[1,224,640]{2,1,0:T(8,128)S(1)}, f32[1,224,640]{2,1,0:T(8,128)}, u32[]{:S(2)}) copy-start(f32[1,224,640]{2,1,0:T(8,128)} %param.14) | copy-start | bytes 1720324
  7.2 76.6 %all-gather.8.cloned.1.call-start = ((), (), s32[]{:S(2)}) async-start(), calls=%async_computation.2 | async-start | bytes 10813440 | tf_op jit(solution)/shard_map/all_gather | solution.py:14
  12.9 122.3 %all-gather.10.cloned.1.call-start = ((), (), s32[]{:S(2)}) async-start(), calls=%async_computation.3 | async-start | bytes 2867200 | tf_op jit(solution)/shard_map/all_gather | solution.py:80
  13.7 728.2 %all-reduce.5.cloned.1.call-start = ((), (), s32[]{:S(2)}) async-start(), calls=%async_computation.5 | async-start | bytes 13107200
  13.7 70.1 %copy-start.10 = (pred[224,224]{1,0:T(8,128)(4,1)}, pred[224,224]{1,0:T(8,128)(4,1)S(1)}, u32[]{:S(2)}) copy-start(pred[224,224]{1,0:T(8,128)(4,1)S(1)} %iota_compare_fusion) | copy-start | bytes 150532
  83.8 44.5 %copy-start.11 = (f32[10]{0:T(128)S(1)}, f32[10]{0:T(128)}, u32[]{:S(2)}) copy-start(f32[10]{0:T(128)} %param.18) | copy-start | bytes 124
  128.4 6.9 copy-start.9
  135.2 10.4 %copy-start.4 = (f32[1,224,2560]{2,1,0:T(8,128)S(1)}, f32[1,224,2560]{2,1,0:T(8,128)}, u32[]{:S(2)}) copy-start(f32[1,224,2560]{2,1,0:T(8,128)} %all-gather.10.cloned.1.call-done) | copy-start | bytes 6881284
  145.6 7.8 copy-start.2
  153.4 1.3 copy-start.7
  153.4 658.2 %all-gather.12.cloned.1.call-start = ((), (), s32[]{:S(2)}) async-start(), calls=%async_computation.4 | async-start | bytes 10813440 | tf_op jit(solution)/shard_map/all_gather | solution.py:14
  153.6 4.0 copy-start.12
  154.7 9.0 %slice-start = ((s8[6553600]{0:T(1024)(128)(4,1)}), s8[2359296]{0:T(1024)(128)(4,1)S(1)}, s32[]{:S(2)}) async-start(s8[6553600]{0:T(1024)(128)(4,1)} %bitcast.119), calls=%async_computation.6 | async-start | bytes 4718592
  157.5 727.4 %reduce-scatter.3.cloned.1.call-start = ((), (), s32[]{:S(2)}) async-start(), calls=%async_computation.1 | async-start | bytes 2867200 | tf_op jit(solution)/shard_map/reduce_scatter | solution.py:77
  158.8 4.9 slice-start.1
  158.8 4.9 copy-start.3
  842.8 39.8 %copy-start.8 = (f32[224,10,64]{0,2,1:T(8,128)S(1)}, f32[224,10,64]{0,2,1:T(8,128)}, u32[]{:S(2)}) copy-start(f32[224,10,64]{0,2,1:T(8,128)} %fusion.17) | copy-start | bytes 1720324
  882.6 2.3 copy-start.1
Sparse Core Ops, SparseCore 0:
  13.0 65.8 all-gather.7
  80.7 54.4 all-gather.9
  153.5 588.3 all-reduce.4
  745.1 66.3 all-gather.11
  814.7 53.4 reduce-scatter.2
where the time goes:
time: 896 us; the launch traced here: 891 us
  waiting for transfers between devices  641 us (72%)
  local copies, waits for them, and re-layouts  80.8 us (9%)
  blocking collectives  63.2 us (7%)
  matrix products  44.4 us (5%)
  other arithmetic  44 us (5%)
  between operations  15.4 us (2%)
    unnamed x6, waiting for transfers between devices  571 us
    all_gather x2, waiting for transfers between devices, prefix(): pieces = jax.tree.map(lambda part: lax.all_gather(part, axis), value)  67.7 us
    unnamed x1, blocking collectives  63.2 us
    select_n x62, other arithmetic, step(): jnp.where(position < mine, new, old)  43 us
    dynamic_slice x62, local copies, waits for them, and re-layouts, step(): longer = join(so_far, jax.tree.map(lambda part: part[position], pieces))  38.4 us
  transfers between devices with their start and end apart: 5, of which 3 were waited for; matrix products, arithmetic and copies ran while one was open for 16% of the time, Pallas kernels for 0%

commit v1 on v0

v1 whole, which is shorter than its diff:
```python
import functools
import jax
import jax.numpy as jnp
from jax import lax
from jax.experimental import pallas as pl
from jax.experimental.pallas import tpu as pltpu
from jax.sharding import PartitionSpec as P

F32 = jnp.float32
BF16 = jnp.bfloat16
HEAD = 64
LANES = 128
EPS = 1e-05
NN = ((1,), (0,))
NT = ((1,), (1,))
TN = ((0,), (0,))
HIGHEST = lax.Precision.HIGHEST


def split(a):
    high = a.astype(BF16)
    return high, (a - high.astype(F32)).astype(BF16)


def dot(a, b, dims):
    return lax.dot_general(a, b, (dims, ((), ())), preferred_element_type=F32)


def dot3(a, b, dims):
    a_high, a_low = split(a)
    b_high, b_low = split(b)
    return dot(a_high, b_high, dims) + (dot(a_high, b_low, dims) + dot(a_low, b_high, dims))


def call(body, outs, ins, flops, nbytes, scratch=(), smem=(), grid=None, in_specs=None, out_specs=None, name=None):
    if in_specs is None:
        in_specs = [
            pl.BlockSpec(memory_space=pltpu.SMEM if i in smem else pltpu.VMEM) for i in range(len(ins))
        ]
        out_specs = [pl.BlockSpec(memory_space=pltpu.VMEM)] * len(outs)
    return pl.pallas_call(
        body,
        out_shape=[jax.ShapeDtypeStruct(s, F32) for s in outs],
        grid=grid if grid is not None else (),
        in_specs=in_specs,
        out_specs=out_specs,
        scratch_shapes=list(scratch),
        compiler_params=pltpu.CompilerParams(vmem_limit_bytes=48 * 1024 * 1024),
        cost_estimate=pl.CostEstimate(flops=flops, bytes_accessed=nbytes, transcendentals=0),
        name=name,
    )(*ins)


def pair(table, tile, rows, turned=False):
    lane = lax.broadcasted_iota(jnp.int32, (rows, LANES), 1)
    return jnp.where(lane < HEAD, table[:, 2 * tile : 2 * tile + 1], table[:, 2 * tile + 1 : 2 * tile + 2])


def pack(send_ref, state, ranks, pitch):
    rows = state.shape[0] // ranks
    for tile in range(state.shape[1] // LANES):
        for r in range(rows):
            send_ref[pl.ds(tile * rows + r, ranks, stride=pitch), :] = state[
                ranks * r : ranks * (r + 1), LANES * tile : LANES * (tile + 1)
            ]


def unpack(recv_ref, state_ref, ranks, pitch):
    rows = state_ref.shape[0] // ranks
    for tile in range(state_ref.shape[1] // LANES):
        for r in range(rows):
            state_ref[ranks * r : ranks * (r + 1), LANES * tile : LANES * (tile + 1)] = recv_ref[
                pl.ds(tile * rows + r, ranks, stride=pitch), :
            ]


def block_state(ranks, pitch, ld_ref, x_ref, b_ref, send_ref, cum_ref, cum_t_ref):
    length = x_ref.shape[0]
    row = lax.broadcasted_iota(jnp.int32, (length, length), 0)
    col = lax.broadcasted_iota(jnp.int32, (length, length), 1)
    upto = jnp.where(row >= col, 1.0, 0.0).astype(F32)
    ld = ld_ref[...]
    cum = lax.dot_general(ld, upto, (NT, ((), ())), precision=HIGHEST, preferred_element_type=F32)
    cum_t = lax.dot_general(upto, ld, (NT, ((), ())), precision=HIGHEST, preferred_element_type=F32)
    cum_ref[...] = cum
    cum_t_ref[...] = cum_t
    last = cum_t[length - 1 :, :]
    to_end = jnp.exp(last - cum_t)
    scaled = jnp.concatenate(
        [
            x_ref[:, LANES * tile : LANES * (tile + 1)] * pair(to_end, tile, length)
            for tile in range(x_ref.shape[1] // LANES)
        ],
        axis=1,
    )
    state = dot3(b_ref[...], scaled, TN)
    pack(send_ref, state, ranks, pitch)
    heads = ld.shape[0]
    totals = jnp.concatenate([last, jnp.zeros((1, LANES - heads), F32)], axis=1)
    totals = jnp.broadcast_to(totals, (ranks, LANES))
    used = state.size // ranks // LANES
    for spare in range(used, pitch):
        send_ref[pl.ds(spare, ranks, stride=pitch), :] = totals


def local_output(ld_heads, x_ref, b_ref, c_ref, cum_ref, cum_t_ref, skip_ref, y_ref):
    length = x_ref.shape[0]
    row = lax.broadcasted_iota(jnp.int32, (length, length), 0)
    col = lax.broadcasted_iota(jnp.int32, (length, length), 1)
    causal = row >= col
    scores = dot3(c_ref[...], b_ref[...], NT)
    cum = cum_ref[...]
    cum_t = cum_t_ref[...]
    for tile in range(ld_heads // 2):
        parts = []
        for head in (2 * tile, 2 * tile + 1):
            gap = jnp.where(causal, cum_t[:, head : head + 1] - cum[head : head + 1, :], -1e30)
            weights = jnp.exp(gap) * scores
            x = x_ref[:, HEAD * head : HEAD * (head + 1)]
            parts.append(dot3(weights, x, NN) + skip_ref[head] * x)
        y_ref[:, LANES * tile : LANES * (tile + 1)] = jnp.concatenate(parts, axis=1)


def local_grad(ld_heads, dy_ref, b_ref, c_ref, cum_ref, cum_t_ref, skip_ref, dx_ref):
    length = dy_ref.shape[0]
    row = lax.broadcasted_iota(jnp.int32, (length, length), 0)
    col = lax.broadcasted_iota(jnp.int32, (length, length), 1)
    causal = col >= row
    scores = dot3(b_ref[...], c_ref[...], NT)
    cum = cum_ref[...]
    cum_t = cum_t_ref[...]
    for tile in range(ld_heads // 2):
        parts = []
        for head in (2 * tile, 2 * tile + 1):
            gap = jnp.where(causal, cum[head : head + 1, :] - cum_t[:, head : head + 1], -1e30)
            weights = jnp.exp(gap) * scores
            dy = dy_ref[:, HEAD * head : HEAD * (head + 1)]
            parts.append(dot3(weights, dy, NN) + skip_ref[head] * dy)
        dx_ref[:, LANES * tile : LANES * (tile + 1)] = jnp.concatenate(parts, axis=1)


def scan_forward(ranks, pitch, used, width, recv_ref, send_ref, decay_ref):
    tiles = width // LANES
    rows = used // tiles
    totals = recv_ref[pl.ds(used, ranks, stride=pitch), :]
    decays = jnp.exp(totals)
    for tile in range(tiles):
        spread = pair(decays, tile, ranks)
        for r in range(rows):
            decay_ref[pl.ds(tile * rows + r, ranks, stride=pitch), :] = spread
    for spare in range(used, pitch):
        decay_ref[pl.ds(spare, ranks, stride=pitch), :] = decays
    state = jnp.zeros((pitch, LANES), F32)
    for rank in range(ranks):
        here = pl.ds(rank * pitch, pitch)
        send_ref[here, :] = state
        state = state * decay_ref[here, :] + recv_ref[here, :]


def scan_backward(ranks, pitch, recv_ref, decay_ref, send_ref):
    state = jnp.zeros((pitch, LANES), F32)
    for rank in reversed(range(ranks)):
        here = pl.ds(rank * pitch, pitch)
        send_ref[here, :] = state
        state = state * decay_ref[here, :] + recv_ref[here, :]


def gate_and_norm(ranks, pitch, recv_ref, c_ref, cum_t_ref, y_ref, gate_ref, gain_ref, gated_ref, normed_ref, scale_ref, state_ref):
    length, width = y_ref.shape
    unpack(recv_ref, state_ref, ranks, pitch)
    carried = dot3(c_ref[...], state_ref[...], NN)
    from_start = jnp.exp(cum_t_ref[...])
    total = jnp.zeros((length, LANES), F32)
    for tile in range(width // LANES):
        here = slice(LANES * tile, LANES * (tile + 1))
        y = y_ref[:, here] + carried[:, here] * pair(from_start, tile, length)
        gate = gate_ref[:, here]
        gated = y * (gate / (1.0 + jnp.exp(-gate)))
        gated_ref[:, here] = gated
        total = total + gated * gated
    scale = lax.rsqrt(jnp.sum(total, axis=1, keepdims=True) * (1.0 / width) + EPS)
    scale_ref[...] = jnp.broadcast_to(scale, scale_ref.shape)
    normed_ref[...] = gated_ref[...] * scale * gain_ref[...]


def out_blocks(ring, block, steps, pos_ref, normed_ref, w_ref, share_ref):
    half = pl.program_id(0) // (pl.num_programs(0) // 2)
    me = pos_ref[0]
    w = w_ref[...]
    rows = []
    for s in steps:
        index = lax.rem(jnp.where(half == 0, me + 2 * ring - 1 - s, me + 1 + s), ring)
        rows.append(normed_ref[pl.ds(pl.multiple_of(index * block, 8), block), :])
    product = dot3(jnp.concatenate(rows, axis=0) if len(rows) > 1 else rows[0], w, NN)
    for i in range(len(rows)):
        share_ref[i] = product[i * block : (i + 1) * block]


def d_normed_part(count, *refs):
    d_refs, w_ref, out_ref = refs[:count], refs[count], refs[count + 1]
    d = jnp.concatenate([r[...] for r in d_refs], axis=0) if count > 1 else d_refs[0][...]
    product = dot3(d, w_ref[...], NT)

    @pl.when(pl.program_id(0) == 0)
    def _():
        out_ref[...] = product

    @pl.when(pl.program_id(0) > 0)
    def _():
        out_ref[...] += product


def norm_grad(ranks, pitch, block, ring, pos_ref, near_ref, far_ref, gated_ref, scale_ref, gate_ref, gain_ref, c_ref, cum_t_ref, send_ref, dy_ref, dn_ref):
    length, width = gated_ref.shape
    me = pos_ref[0]
    order = ring_order(ring)
    for i, step in enumerate(order):
        index = lax.rem(me + step + ring, ring)
        src = near_ref[i * block : (i + 1) * block, :] if i < ring - 1 else far_ref[...]
        dn_ref[pl.ds(pl.multiple_of(index * block, 8), block), :] = src
    scale = scale_ref[:, :1]
    total = jnp.zeros((length, LANES), F32)
    for tile in range(width // LANES):
        here = slice(LANES * tile, LANES * (tile + 1))
        total = total + dn_ref[:, here] * gain_ref[:, here] * gated_ref[:, here]
    mean = jnp.sum(total, axis=1, keepdims=True) * (1.0 / width)
    shift = scale * scale * scale * mean
    from_start = jnp.exp(cum_t_ref[...])
    scaled = []
    for tile in range(width // LANES):
        here = slice(LANES * tile, LANES * (tile + 1))
        gate = gate_ref[:, here]
        d_gated = dn_ref[:, here] * gain_ref[:, here] * scale - gated_ref[:, here] * shift
        dy = d_gated * (gate / (1.0 + jnp.exp(-gate)))
        dy_ref[:, here] = dy
        scaled.append(dy * pair(from_start, tile, length))
    grad_state = dot3(c_ref[...], jnp.concatenate(scaled, axis=1), TN)
    pack(send_ref, grad_state, ranks, pitch)
    used = grad_state.size // ranks // LANES
    for spare in range(used, pitch):
        send_ref[pl.ds(spare, ranks, stride=pitch), :] = jnp.zeros((ranks, LANES), F32)


def ring_order(ring):
    return [0, -1, 1, 2]


def weight_grad(block, ring, pos_ref, d0_ref, d1_ref, d2_ref, d3_ref, normed_ref, out_ref):
    me = pos_ref[0]
    d = jnp.concatenate([d0_ref[...], d1_ref[...], d2_ref[...], d3_ref[...]], axis=0)
    rows = []
    for step in ring_order(ring):
        index = lax.rem(me + step + ring, ring)
        rows.append(normed_ref[pl.ds(pl.multiple_of(index * block, 8), block), :])
    out_ref[...] = dot3(d, jnp.concatenate(rows, axis=0), TN)


def finish(ranks, pitch, recv_ref, b_ref, cum_t_ref, part_ref, dx_ref, state_ref):
    length, width = part_ref.shape
    unpack(recv_ref, state_ref, ranks, pitch)
    carried = dot3(b_ref[...], state_ref[...], NN)
    cum_t = cum_t_ref[...]
    to_end = jnp.exp(cum_t[length - 1 :, :] - cum_t)
    for tile in range(width // LANES):
        here = slice(LANES * tile, LANES * (tile + 1))
        dx_ref[:, here] = part_ref[:, here] + carried[:, here] * pair(to_end, tile, length)


def shifted(value, axis, step):
    count = lax.axis_size(axis)
    return lax.ppermute(value, axis, [(i, (i + step) % count) for i in range(count)])


def exchange(value, axis):
    return lax.all_to_all(value, axis, 0, 0, tiled=True)


def per_device(head_input, gate_input, log_decay, in_b, in_c, skip, norm_gain, w_out, d_out):
    x, gate, ld, b_mat, c_mat, d_own = head_input[0], gate_input[0], log_decay[0], in_b[0], in_c[0], d_out[0]
    length, width = x.shape
    heads, state = ld.shape[0], b_mat.shape[1]
    model = w_out.shape[1]
    ranks, ring = lax.axis_size("ctx"), lax.axis_size("tp")
    block = d_own.shape[0]
    used = state * width // ranks // LANES
    pitch = -(-(used + 1) // 8) * 8
    gain = norm_gain[None, :]
    pos = lax.axis_index("tp").astype(jnp.int32)[None]
    half = model // 2

    d_prev = shifted(d_own, "tp", 1)
    d_next = shifted(d_own, "tp", -1)
    d_far = jnp.concatenate([shifted(d_prev[:, :half], "tp", 1), shifted(d_next[:, half:], "tp", -1)], axis=1)

    pieces = (ranks * pitch, LANES)
    send, cum, cum_t = call(
        functools.partial(block_state, ranks, pitch),
        [pieces, (heads, length), (length, heads)],
        [ld, x, b_mat],
        flops=6 * length * state * width, nbytes=4 * (length * width * 2), name="block_state",
    )
    recv = exchange(send, "ctx")
    (y_local,) = call(
        functools.partial(local_output, heads),
        [(length, width)],
        [x, b_mat, c_mat, cum, cum_t, skip],
        flops=6 * length * length * width * 4, nbytes=8 * length * width, smem=(5,), name="local_output",
    )
    send, decays = call(
        functools.partial(scan_forward, ranks, pitch, used, width),
        [pieces, pieces],
        [recv],
        flops=10 * ranks * pitch * LANES, nbytes=12 * ranks * pitch * LANES, name="scan_forward",
    )
    recv = exchange(send, "ctx")
    gated, normed, scale = call(
        functools.partial(gate_and_norm, ranks, pitch),
        [(length, width), (length, width), (length, LANES)],
        [recv, c_mat, cum_t, y_local, gate, gain],
        flops=6 * length * state * width, nbytes=16 * length * width,
        scratch=[pltpu.VMEM((state, width), F32)], name="gate_and_norm",
    )

    def out_part(steps):
        tile = 256
        return call(
            functools.partial(out_blocks, ring, block, steps),
            [(len(steps), block, model)],
            [pos, normed, w_out],
            flops=6 * len(steps) * block * width * model, nbytes=4 * width * model,
            grid=(model // tile,),
            in_specs=[
                pl.BlockSpec(memory_space=pltpu.SMEM),
                pl.BlockSpec((length, width), lambda n: (0, 0)),
                pl.BlockSpec((width, tile), lambda n: (0, n)),
            ],
            out_specs=[pl.BlockSpec((len(steps), block, tile), lambda n: (0, 0, n))],
            name="out_blocks",
        )[0]

    first = out_part((0,))[0]
    to_next, to_prev = first[:, :half], first[:, half:]
    rest = out_part(tuple(range(1, ring)))
    for s in range(ring - 1):
        to_next = shifted(to_next, "tp", 1) + rest[s][:, :half]
        to_prev = shifted(to_prev, "tp", -1) + rest[s][:, half:]
    out = jnp.concatenate([to_next, to_prev], axis=1)

    def d_part(parts):
        tile = 256
        rows = sum(p.shape[0] for p in parts)
        return call(
            functools.partial(d_normed_part, len(parts)),
            [(rows, width)],
            [*parts, w_out],
            flops=6 * rows * width * model, nbytes=4 * width * model,
            grid=(model // tile,),
            in_specs=[
                *[pl.BlockSpec((p.shape[0], tile), lambda k: (0, k)) for p in parts],
                pl.BlockSpec((width, tile), lambda k: (0, k)),
            ],
            out_specs=[pl.BlockSpec((rows, width), lambda k: (0, 0))],
            name="d_normed",
        )[0]

    near = d_part([d_own, d_prev, d_next])
    far = d_part([d_far])
    send, dy = call(
        functools.partial(norm_grad, ranks, pitch, block, ring),
        [pieces, (length, width)],
        [pos, near, far, gated, scale, gate, gain, c_mat, cum_t],
        flops=6 * length * state * width, nbytes=20 * length * width, smem=(0,),
        scratch=[pltpu.VMEM((length, width), F32)], name="norm_grad",
    )
    recv = exchange(send, "ctx")
    tile = 256
    (grad_w,) = call(
        functools.partial(weight_grad, block, ring),
        [(model, width)],
        [pos, d_own, d_prev, d_next, d_far, normed],
        flops=6 * length * width * model, nbytes=4 * width * model,
        grid=(model // tile,),
        in_specs=[
            pl.BlockSpec(memory_space=pltpu.SMEM),
            *[pl.BlockSpec((block, tile), lambda k: (0, k))] * 4,
            pl.BlockSpec((length, width), lambda k: (0, 0)),
        ],
        out_specs=[pl.BlockSpec((tile, width), lambda k: (k, 0))],
        name="weight_grad",
    )
    grad_share = lax.psum_scatter(
        lax.psum_scatter(grad_w, "ctx", scatter_dimension=0, tiled=True), "dp", scatter_dimension=0, tiled=True
    )
    (dx_local,) = call(
        functools.partial(local_grad, heads),
        [(length, width)],
        [dy, b_mat, c_mat, cum, cum_t, skip],
        flops=6 * length * length * width * 4, nbytes=8 * length * width, smem=(5,), name="local_grad",
    )
    (send,) = call(
        functools.partial(scan_backward, ranks, pitch),
        [pieces],
        [recv, decays],
        flops=10 * ranks * pitch * LANES, nbytes=12 * ranks * pitch * LANES, name="scan_backward",
    )
    recv = exchange(send, "ctx")
    (dx,) = call(
        functools.partial(finish, ranks, pitch),
        [(length, width)],
        [recv, b_mat, cum_t, dx_local],
        flops=6 * length * state * width, nbytes=12 * length * width,
        scratch=[pltpu.VMEM((state, width), F32)], name="finish",
    )
    return (out[None], dx[None], grad_share)


def solution(mesh):
    placed = (
        P("dp", "ctx", "tp"),
        P("dp", "ctx", "tp"),
        P("dp", "tp", "ctx"),
        P("dp", "ctx", None),
        P("dp", "ctx", None),
        P("tp"),
        P("tp"),
        P("tp", None),
        P("dp", ("ctx", "tp"), None),
    )
    return jax.shard_map(
        per_device,
        mesh=mesh,
        in_specs=placed,
        out_specs=(P("dp", ("ctx", "tp"), None), P("dp", "ctx", "tp"), P(("ctx", "dp"), "tp")),
        check_vma=False,
    )
```

time: 896 us -> 203 us (0.23)
  waiting for transfers between devices: 641 us -> 64 us
  local copies, waits for them, and re-layouts: 80.8 us -> 14.1 us
  blocking collectives: 63.2 us -> 0 us
  Pallas kernels: 0 us -> 52 us
  starting transfers between devices: 0.2 us -> 51.3 us
  matrix products: 44.4 us -> 0 us
  other arithmetic: 44 us -> 4.89 us
    unnamed x6 -> x3, waiting for transfers between devices: 571 us -> 15.7 us
    all_gather x3 -> x0, waiting for transfers between devices: 69.6 us -> none  [the longest x2 67.7 us: prefix(): pieces = jax.tree.map(lambda part: lax.all_gather(part, axis), value)]
    unnamed x1 -> x0, blocking collectives: 63.2 us -> none
    pallas_call x0 -> x13, Pallas kernels: none -> 52 us  [call(): pl.pallas_call(body, out_shape=[jax.ShapeDtypeStruct(s, F32) for s in out...]
    dot_general x10 -> x0, matrix products: 44.4 us -> none  [the longest x1 10.3 us: per_device(): lax.dot_general(d_full, w_out, (((1,), (1,)), ((), ())), precision=highest)]
    select_n x62 -> x0, other arithmetic: 43 us -> none  [step(): jnp.where(position < mine, new, old)]
    dynamic_slice x62 -> x0, local copies, waits for them, and re-layouts: 38.4 us -> none  [step(): longer = join(so_far, jax.tree.map(lambda part: part[position], pieces))]
    ppermute x0 -> x10, starting transfers between devices: none -> 26.3 us  [shifted(): lax.ppermute(value, axis, [(i, (i + step) % count) for i in range(count)])]
  transfers between devices with their start and end apart: 5 -> 16, of which waited for: 3 -> 7; matrix products, arithmetic and copies ran while one was open for 16% -> 5% of each run, Pallas kernels for 0% -> 22%
where the time goes in v1:
time: 203 us; the launch traced here: 201 us
  waiting for transfers between devices  64 us (32%)
  Pallas kernels  52 us (26%)
  starting transfers between devices  51.3 us (25%)
  between operations  14.4 us (7%)
  local copies, waits for them, and re-layouts  14.1 us (7%)
  other arithmetic  4.89 us (2%)
    pallas_call x13, Pallas kernels, call(): pl.pallas_call(body, out_shape=[jax.ShapeDtypeStruct(s, F32) for s in out...  52 us
    ppermute x10, starting transfers between devices, shifted(): lax.ppermute(value, axis, [(i, (i + step) % count) for i in range(count)])  26.3 us
    all_to_all x4, starting transfers between devices, exchange(): return lax.all_to_all(value, axis, 0, 0, tiled=True)  25 us
    reduce_scatter x1, waiting for transfers between devices, per_device(): lax.psum_scatter(grad_w, 'ctx', scatter_dimension=0, tiled=True)  22.4 us
    unnamed x3, waiting for transfers between devices  15.7 us
    ppermute x10, waiting for transfers between devices, shifted(): lax.ppermute(value, axis, [(i, (i + step) % count) for i in range(count)])  14.8 us
    all_to_all x4, waiting for transfers between devices, exchange(): return lax.all_to_all(value, axis, 0, 0, tiled=True)  11.1 us
    unnamed x50, local copies, waits for them, and re-layouts  10 us
  transfers between devices with their start and end apart: 16, of which 7 were waited for; matrix products, arithmetic and copies ran while one was open for 5% of the time, Pallas kernels for 22%

profile of v1, /device:TPU:2, one launch (start us, length us, event | category | flops | bytes accessed | tf_op | source)
XLA Modules:
  0.0 200.8 jit_solution(16137649960976031101)
XLA Ops:
  7.2 0.0 copy-start.1
  7.2 3.3 %collective-permute-start.6 = (f32[56,2560]{1,0:T(8,128)}, f32[56,2560]{1,0:T(8,128)S(1)}, u32[]{:S(2)}, u32[]{:S(2)}) collective-permute-start(f32[56,2560]{1,0:T(8,128)} %bitcast.30), channel_id=1, source_target_pairs={{0,2},{2,4},{4,6},{6,0},{1,3},{3,5},{5,7},{7,1},{8,10},{10,12},{12... | collective-permute-start | bytes 1720328 | tf_op jit(solution)/shard_map/ppermute | solution.py:271
  10.5 0.7 copy.14
  11.2 1.1 copy-done.4
  12.3 0.9 copy-done.11
  13.2 1.9 block_state.1
  15.1 7.6 %all-to-all-start = ((f32[32,24,128]{2,1,0:T(8,128)}), f32[32,24,128]{2,1,0:T(8,128)S(1)}, u32[]{:S(2)}, u32[]{:S(2)}) async-start(f32[32,24,128]{2,1,0:T(8,128)} %bitcast.3), calls=%async_computation | async-start | bytes 786432 | tf_op jit(solution)/shard_map/all_to_all | solution.py:275
  22.7 3.2 %collective-permute-start.7 = (f32[56,2560]{1,0:T(8,128)}, f32[56,2560]{1,0:T(8,128)S(1)}, u32[]{:S(2)}, u32[]{:S(2)}) collective-permute-start(f32[56,2560]{1,0:T(8,128)} %bitcast.31), channel_id=1, source_target_pairs={{0,6},{2,0},{4,2},{6,4},{1,7},{3,1},{5,3},{7,5},{8,14},{10,8},{12,... | collective-permute-start | bytes 1720328 | tf_op jit(solution)/shard_map/ppermute | solution.py:271
  26.0 5.9 %all-to-all-done = f32[32,24,128]{2,1,0:T(8,128)S(1)} async-done(((f32[32,24,128]{2,1,0:T(8,128)}), f32[32,24,128]{2,1,0:T(8,128)S(1)}, u32[]{:S(2)}, u32[]{:S(2)}) %all-to-all-start) | async-done | bytes 393248 | tf_op jit(solution)/shard_map/all_to_all | solution.py:275
  31.8 0.9 scan_forward.1
  32.8 0.7 copy-done.14
  33.5 5.0 %all-to-all-start.1 = ((f32[32,24,128]{2,1,0:T(8,128)}), f32[32,24,128]{2,1,0:T(8,128)S(1)}, u32[]{:S(2)}, u32[]{:S(2)}) async-start(f32[32,24,128]{2,1,0:T(8,128)} %bitcast.5), calls=%async_computation.1 | async-start | bytes 786432 | tf_op jit(solution)/shard_map/all_to_all | solution.py:275
  38.5 0.0 reduce-scatter.6.cloned.1.call-start
  38.5 0.0 collective-permute-done.6.refs_1_.d1_ref
  38.5 0.7 slice.66
  39.3 4.5 %collective-permute-start.8 = (f32[56,1280]{1,0:T(8,128)}, f32[56,1280]{1,0:T(8,128)}, u32[]{:S(2)}, u32[]{:S(2)}) collective-permute-start(f32[56,1280]{1,0:T(8,128)} %slice.66), channel_id=1, source_target_pairs={{0,2},{2,4},{4,6},{6,0},{1,3},{3,5},{5,7},{7,1},{8,10},{10,12},{12... | collective-permute-start | bytes 860168 | tf_op jit(solution)/shard_map/ppermute | solution.py:271
  43.8 0.7 broadcast_in_dim.13.gain_ref
  44.5 8.8 %collective-permute-done.7.refs_2_.d2_ref = f32[56,2560]{1,0:T(8,128)S(1)} collective-permute-done((f32[56,2560]{1,0:T(8,128)}, f32[56,2560]{1,0:T(8,128)S(1)}, u32[]{:S(2)}, u32[]{:S(2)}) %collective-permute-start.7) | collective-permute-done | bytes 573472 | tf_op jit(solution)/shard_map/ppermute | solution.py:271
  53.2 0.7 slice.67
  53.9 2.5 %collective-permute-start.9 = (f32[56,1280]{1,0:T(8,128)}, f32[56,1280]{1,0:T(8,128)}, u32[]{:S(2)}, u32[]{:S(2)}) collective-permute-start(f32[56,1280]{1,0:T(8,128)} %slice.67), channel_id=1, source_target_pairs={{0,6},{2,0},{4,2},{6,4},{1,7},{3,1},{5,3},{7,5},{8,14},{10,8},{12,... | collective-permute-start | bytes 860168 | tf_op jit(solution)/shard_map/ppermute | solution.py:271
  56.4 1.1 copy-done.5
  57.5 0.9 copy-done.8
  58.4 0.9 copy-done.12
  59.3 0.7 copy-done.22
  60.0 2.1 %local_output.1.y_ref = f32[224,640]{1,0:T(8,128)S(1)} custom-call(f32[224,640]{1,0:T(8,128)S(1)} %bitcast.40, f32[224,128]{1,0:T(8,128)S(1)} %bitcast.46, f32[224,128]{1,0:T(8,128)S(1)} %bitcast.41, f32[10,224]{1,0:T(8,128)S(1)} %get-tuple-element.16.cum_ref, f32[224,10]{1,0:T(8,128)S(1)} %get-tuple-element.15.cum_t_ref, f32[10]{0:T(128)S(1)} %copy-done.22), custom_call_target="tpu_custom_call" | custom-call | flops 770703360 | bytes 1146880 | tf_op jit(solution)/shard_map/local_output/pallas_call | solution.py:41
  62.1 0.0 copy-start.2
  62.1 0.8 copy-done.2
  62.9 1.1 copy-done.3
  64.0 0.6 gate_and_norm.1
  64.6 0.0 copy-start.6
  64.6 1.2 constant_dynamic-update-slice_fusion.1
  65.8 2.1 %collective-permute-done.9 = f32[56,1280]{1,0:T(8,128)} collective-permute-done((f32[56,1280]{1,0:T(8,128)}, f32[56,1280]{1,0:T(8,128)}, u32[]{:S(2)}, u32[]{:S(2)}) %collective-permute-start.9) | collective-permute-done | bytes 286752 | tf_op jit(solution)/shard_map/ppermute | solution.py:271
  68.0 1.0 constant_dynamic-update-slice_fusion.refs_0_.d3_ref
  69.0 7.6 %weight_grad.1 = f32[2560,640]{1,0:T(8,128)} custom-call(s32[1]{0:T(128)} %bitcast.pos_ref, f32[56,2560]{1,0:T(8,128)S(1)} %bitcast.32, f32[56,2560]{1,0:T(8,128)S(1)} %collective-permute-done.6.refs_1_.d1_ref, f32[56,2560]{1,0:T(8,128)S(1)} %collective-permute-done.7.refs_2_.d2_ref, f32[56,2560]{1,0:T(8,128)S(1)} %constant_dynamic-update-slice_fusion.refs_0_.d3_ref, ...), custom_call_target="tpu_custom_call" | custom-call | flops 2202009600 | bytes 6553600 | tf_op jit(solution)/shard_map/weight_grad/pallas_call | solution.py:41
  76.6 0.0 reduce-scatter.6.cloned.1.call-update
  76.6 7.4 %out_blocks.2 = f32[1,56,2560]{2,1,0:T(8,128)S(1)} custom-call(s32[1]{0:T(128)} %bitcast.pos_ref, f32[224,640]{1,0:T(8,128)S(1)} %get-tuple-element.17.normed_ref, f32[640,2560]{1,0:T(8,128)} %refs_1_.1), custom_call_target="tpu_custom_call" | custom-call | flops 550502400 | bytes 6553600 | tf_op jit(solution)/shard_map/out_blocks/pallas_call | solution.py:41
  84.0 0.6 collective-permute-start
  84.7 3.6 %collective-permute-start.3 = (f32[56,1280]{1,0:T(8,128)S(1)}, f32[56,1280]{1,0:T(8,128)S(1)}, u32[]{:S(2)}, u32[]{:S(2)}) collective-permute-start(f32[56,1280]{1,0:T(8,128)S(1)} %get-tuple-element.33), channel_id=1, source_target_pairs={{0,6},{2,0},{4,2},{6,4},{1,7},{3,1},{5,3},{7,5},{8,14},{10,8},{12,... | collective-permute-start | bytes 860168 | tf_op jit(solution)/shard_map/ppermute | solution.py:271
  88.3 8.1 %out_blocks.3 = f32[3,56,2560]{2,1,0:T(8,128)S(1)} custom-call(s32[1]{0:T(128)} %bitcast.pos_ref, f32[224,640]{1,0:T(8,128)S(1)} %get-tuple-element.17.normed_ref, f32[640,2560]{1,0:T(8,128)} %refs_1_.1), custom_call_target="tpu_custom_call" | custom-call | flops 1651507200 | bytes 6553600 | tf_op jit(solution)/shard_map/out_blocks/pallas_call | solution.py:41
  96.4 0.9 slice_bitcast_fusion
  97.3 3.9 %collective-permute-done = f32[56,1280]{1,0:T(8,128)S(1)} collective-permute-done((f32[56,1280]{1,0:T(8,128)S(1)}, f32[56,1280]{1,0:T(8,128)S(1)}, u32[]{:S(2)}, u32[]{:S(2)}) %collective-permute-start) | collective-permute-done | bytes 286752 | tf_op jit(solution)/shard_map/ppermute | solution.py:271
  101.2 0.9 slice_add_fusion.5
  102.1 4.4 %collective-permute-start.4 = (f32[56,1280]{1,0:T(8,128)}, f32[56,1280]{1,0:T(8,128)}, u32[]{:S(2)}, u32[]{:S(2)}) collective-permute-start(f32[56,1280]{1,0:T(8,128)} %get-tuple-element.31), channel_id=1, source_target_pairs={{0,6},{2,0},{4,2},{6,4},{1,7},{3,1},{5,3},{7,5},{8,14},{10,8},{12,... | collective-permute-start | bytes 860168 | tf_op jit(solution)/shard_map/ppermute | solution.py:271
  106.5 8.9 %d_normed.2.near_ref = f32[168,640]{1,0:T(8,128)S(1)} custom-call(f32[56,2560]{1,0:T(8,128)S(1)} %bitcast.33, f32[56,2560]{1,0:T(8,128)S(1)} %collective-permute-done.6.refs_1_.d1_ref, f32[56,2560]{1,0:T(8,128)S(1)} %collective-permute-done.7.refs_2_.d2_ref, f32[640,2560]{1,0:T(8,128)} %refs_1_.1), custom_call_target="tpu_custom_call" | custom-call | flops 1651507200 | bytes 6553600 | tf_op jit(solution)/shard_map/d_normed/pallas_call | solution.py:41
  115.4 0.0 copy-start.10
  115.5 0.0 copy-start.13
  115.5 0.0 copy-start.21
  115.5 0.0 copy-start.23
  115.5 8.5 %d_normed.3.far_ref = f32[56,640]{1,0:T(8,128)S(1)} custom-call(f32[56,2560]{1,0:T(8,128)S(1)} %constant_dynamic-update-slice_fusion.refs_0_.d3_ref, f32[640,2560]{1,0:T(8,128)} %refs_1_.1), custom_call_target="tpu_custom_call" | custom-call | flops 550502400 | bytes 6553600 | tf_op jit(solution)/shard_map/d_normed/pallas_call | solution.py:41
  124.1 1.7 norm_grad.1
  125.8 7.4 %all-to-all-start.2 = ((f32[32,24,128]{2,1,0:T(8,128)}), f32[32,24,128]{2,1,0:T(8,128)S(1)}, u32[]{:S(2)}, u32[]{:S(2)}) async-start(f32[32,24,128]{2,1,0:T(8,128)} %bitcast.15), calls=%async_computation.2 | async-start | bytes 786432 | tf_op jit(solution)/shard_map/all_to_all | solution.py:275
  133.2 2.0 %slice_add_fusion.4 = (f32[56,1280]{1,0:T(8,128)}, f32[56,1280]{1,0:T(8,128)S(1)}) fusion(f32[56,1280]{1,0:T(8,128)} %collective-permute-done.1, f32[56,2560]{1,0:T(8,128)} %get-tuple-element.24, f32[56,1280]{1,0:T(8,128)} %collective-permute-done.4), kind=kLoop, calls=%fused_computation.8 | loop fusion | flops 143360 | bytes 1720320 | tf_op jit(solution)/shard_map/add | solution.py:345
  135.2 4.1 %collective-permute-start.5 = (f32[56,1280]{1,0:T(8,128)S(1)}, f32[56,1280]{1,0:T(8,128)}, u32[]{:S(2)}, u32[]{:S(2)}) collective-permute-start(f32[56,1280]{1,0:T(8,128)S(1)} %get-tuple-element.29), channel_id=1, source_target_pairs={{0,6},{2,0},{4,2},{6,4},{1,7},{3,1},{5,3},{7,5},{8,14},{10,8},{12,... | collective-permute-start | bytes 860168 | tf_op jit(solution)/shard_map/ppermute | solution.py:271
  139.3 2.1 %local_grad.1.part_ref = f32[224,640]{1,0:T(8,128)S(1)} custom-call(f32[224,640]{1,0:T(8,128)S(1)} %get-tuple-element.22.dy_ref, f32[224,128]{1,0:T(8,128)S(1)} %bitcast.47, f32[224,128]{1,0:T(8,128)S(1)} %bitcast.44, f32[10,224]{1,0:T(8,128)S(1)} %copy-done.21, f32[224,10]{1,0:T(8,128)S(1)} %get-tuple-element.15.cum_t_ref, f32[10]{0:T(128)S(1)} %copy-done.23), custom_call_target="tpu_custom_call" | custom-call | flops 770703360 | bytes 1146880 | tf_op jit(solution)/shard_map/local_grad/pallas_call | solution.py:41
  141.5 5.2 %all-to-all-done.2 = f32[32,24,128]{2,1,0:T(8,128)S(1)} async-done(((f32[32,24,128]{2,1,0:T(8,128)}), f32[32,24,128]{2,1,0:T(8,128)S(1)}, u32[]{:S(2)}, u32[]{:S(2)}) %all-to-all-start.2) | async-done | bytes 393248 | tf_op jit(solution)/shard_map/all_to_all | solution.py:275
  146.7 0.8 scan_backward.1
  147.6 5.0 %all-to-all-start.3 = ((f32[32,24,128]{2,1,0:T(8,128)}), f32[32,24,128]{2,1,0:T(8,128)S(1)}, u32[]{:S(2)}, u32[]{:S(2)}) async-start(f32[32,24,128]{2,1,0:T(8,128)} %bitcast.17), calls=%async_computation.3 | async-start | bytes 786432 | tf_op jit(solution)/shard_map/all_to_all | solution.py:275
  152.5 0.0 reduce-scatter.8.cloned.1.call-start
  152.6 22.4 %reduce-scatter.6.cloned.1.call-done = f32[80,640]{1,0:T(8,128)} async-done(((f32[2560,640]{1,0:T(8,128)}), f32[80,640]{1,0:T(8,128)}) %reduce-scatter.6.cloned.1.call-update) | async-done | bytes 204816 | tf_op jit(solution)/shard_map/reduce_scatter | solution.py:392
  175.0 0.0 reduce-scatter.8.cloned.1.call-update
  175.0 1.1 slice_add_fusion.3
  176.1 1.3 finish.1
  177.4 0.8 maximum_bitcast_fusion
  178.3 15.7 %reduce-scatter.8.cloned.1.call-done = f32[40,640]{1,0:T(8,128)} async-done(((f32[80,640]{1,0:T(8,128)}), f32[40,640]{1,0:T(8,128)}) %reduce-scatter.8.cloned.1.call-update) | async-done | bytes 102416
  (43 shorter events, 0.1 us)
Async XLA Ops:
  7.2 61.8 %copy-start.1 = (f32[1,56,2560]{2,1,0:T(8,128)S(1)}, f32[1,56,2560]{2,1,0:T(8,128)}, u32[]{:S(2)}) copy-start(f32[1,56,2560]{2,1,0:T(8,128)} %param.17) | copy-start | bytes 1720324
  7.2 55.7 %copy-start = (f32[1,224,640]{2,1,0:T(8,128)S(1)}, f32[1,224,640]{2,1,0:T(8,128)}, u32[]{:S(2)}) copy-start(f32[1,224,640]{2,1,0:T(8,128)} %param.10) | copy-start | bytes 1720324
  7.2 31.4 %collective-permute-start.6 = (f32[56,2560]{1,0:T(8,128)}, f32[56,2560]{1,0:T(8,128)S(1)}, u32[]{:S(2)}, u32[]{:S(2)}) collective-permute-start(f32[56,2560]{1,0:T(8,128)} %bitcast.30), channel_id=1, source_target_pairs={{0,2},{2,4},{4,6},{6,0},{1,3},{3,5},{5,7},{7,1},{8,10},{10,12},{12... | collective-permute-start | bytes 1720328 | tf_op jit(solution)/shard_map/ppermute | solution.py:271
  11.2 1.1 copy-start.4
  12.3 0.9 copy-start.11
  15.1 49.5 %copy-start.20 = (f32[10,224]{1,0:T(8,128)}, f32[10,224]{1,0:T(8,128)S(1)}, u32[]{:S(2)}) copy-start(f32[10,224]{1,0:T(8,128)S(1)} %get-tuple-element.16.cum_ref) | copy-start | bytes 26884
  15.1 16.7 %all-to-all-start = ((f32[32,24,128]{2,1,0:T(8,128)}), f32[32,24,128]{2,1,0:T(8,128)S(1)}, u32[]{:S(2)}, u32[]{:S(2)}) async-start(f32[32,24,128]{2,1,0:T(8,128)} %bitcast.3), calls=%async_computation | async-start | bytes 786432 | tf_op jit(solution)/shard_map/all_to_all | solution.py:275
  22.7 30.5 %collective-permute-start.7 = (f32[56,2560]{1,0:T(8,128)}, f32[56,2560]{1,0:T(8,128)S(1)}, u32[]{:S(2)}, u32[]{:S(2)}) collective-permute-start(f32[56,2560]{1,0:T(8,128)} %bitcast.31), channel_id=1, source_target_pairs={{0,6},{2,0},{4,2},{6,4},{1,7},{3,1},{5,3},{7,5},{8,14},{10,8},{12,... | collective-permute-start | bytes 1720328 | tf_op jit(solution)/shard_map/ppermute | solution.py:271
  32.8 0.7 copy-start.14
  33.5 29.4 %all-to-all-start.1 = ((f32[32,24,128]{2,1,0:T(8,128)}), f32[32,24,128]{2,1,0:T(8,128)S(1)}, u32[]{:S(2)}, u32[]{:S(2)}) async-start(f32[32,24,128]{2,1,0:T(8,128)} %bitcast.5), calls=%async_computation.1 | async-start | bytes 786432 | tf_op jit(solution)/shard_map/all_to_all | solution.py:275
  38.5 136.5 %reduce-scatter.6.cloned.1.call-start = ((), (), s32[]{:S(2)}) async-start(), calls=%async_computation.6 | async-start | bytes 6758400 | tf_op jit(solution)/shard_map/reduce_scatter | solution.py:392
  39.3 25.3 %collective-permute-start.8 = (f32[56,1280]{1,0:T(8,128)}, f32[56,1280]{1,0:T(8,128)}, u32[]{:S(2)}, u32[]{:S(2)}) collective-permute-start(f32[56,1280]{1,0:T(8,128)} %slice.66), channel_id=1, source_target_pairs={{0,2},{2,4},{4,6},{6,0},{1,3},{3,5},{5,7},{7,1},{8,10},{10,12},{12... | collective-permute-start | bytes 860168 | tf_op jit(solution)/shard_map/ppermute | solution.py:271
  44.5 20.1 %copy-start.18 = (f32[1,640]{1,0:T(1,128)}, f32[1,640]{1,0:T(1,128)S(1)}, u32[]{:S(2)}) copy-start(f32[1,640]{1,0:T(1,128)S(1)} %broadcast_in_dim.13.gain_ref) | copy-start | bytes 7684
  53.9 14.0 %collective-permute-start.9 = (f32[56,1280]{1,0:T(8,128)}, f32[56,1280]{1,0:T(8,128)}, u32[]{:S(2)}, u32[]{:S(2)}) collective-permute-start(f32[56,1280]{1,0:T(8,128)} %slice.67), channel_id=1, source_target_pairs={{0,6},{2,0},{4,2},{6,4},{1,7},{3,1},{5,3},{7,5},{8,14},{10,8},{12,... | collective-permute-start | bytes 860168 | tf_op jit(solution)/shard_map/ppermute | solution.py:271
  56.4 1.1 copy-start.5
  57.5 0.9 copy-start.8
  58.4 0.9 copy-start.12
  59.3 0.7 copy-start.22
  62.1 0.8 copy-start.2
  62.9 1.1 copy-start.3
  64.6 4.4 %copy-start.6 = (f32[224,640]{1,0:T(8,128)}, f32[224,640]{1,0:T(8,128)S(1)}, u32[]{:S(2)}) copy-start(f32[224,640]{1,0:T(8,128)S(1)} %get-tuple-element.18.gated_ref) | copy-start | bytes 1720324
  64.6 4.4 %copy-start.16 = (f32[224,128]{1,0:T(8,128)}, f32[224,128]{1,0:T(8,128)S(1)}, u32[]{:S(2)}) copy-start(f32[224,128]{1,0:T(8,128)S(1)} %get-tuple-element.19.scale_ref) | copy-start | bytes 344068
  84.0 17.1 %collective-permute-start = (f32[56,1280]{1,0:T(8,128)S(1)}, f32[56,1280]{1,0:T(8,128)S(1)}, u32[]{:S(2)}, u32[]{:S(2)}) collective-permute-start(f32[56,1280]{1,0:T(8,128)S(1)} %get-tuple-element.32), channel_id=1, source_target_pairs={{0,2},{2,4},{4,6},{6,0},{1,3},{3,5},{5,7},{7,1},{8,10},{10,12},{12... | collective-permute-start | bytes 860168 | tf_op jit(solution)/shard_map/ppermute | solution.py:271
  84.7 16.5 %collective-permute-start.3 = (f32[56,1280]{1,0:T(8,128)S(1)}, f32[56,1280]{1,0:T(8,128)S(1)}, u32[]{:S(2)}, u32[]{:S(2)}) collective-permute-start(f32[56,1280]{1,0:T(8,128)S(1)} %get-tuple-element.33), channel_id=1, source_target_pairs={{0,6},{2,0},{4,2},{6,4},{1,7},{3,1},{5,3},{7,5},{8,14},{10,8},{12,... | collective-permute-start | bytes 860168 | tf_op jit(solution)/shard_map/ppermute | solution.py:271
  102.1 31.0 %collective-permute-start.1 = (f32[56,1280]{1,0:T(8,128)}, f32[56,1280]{1,0:T(8,128)}, u32[]{:S(2)}, u32[]{:S(2)}) collective-permute-start(f32[56,1280]{1,0:T(8,128)} %get-tuple-element.30), channel_id=1, source_target_pairs={{0,2},{2,4},{4,6},{6,0},{1,3},{3,5},{5,7},{7,1},{8,10},{10,12},{12... | collective-permute-start | bytes 860168 | tf_op jit(solution)/shard_map/ppermute | solution.py:271
  102.1 21.9 %copy-start.7 = (f32[224,640]{1,0:T(8,128)S(1)}, f32[224,640]{1,0:T(8,128)}, u32[]{:S(2)}) copy-start(f32[224,640]{1,0:T(8,128)} %copy-done.6) | copy-start | bytes 1720324
  102.1 21.9 %copy-start.9 = (f32[1,224,128]{2,1,0:T(8,128)S(1)}, f32[1,224,128]{2,1,0:T(8,128)}, u32[]{:S(2)}) copy-start(f32[1,224,128]{2,1,0:T(8,128)} %param.13) | copy-start | bytes 344068
  102.1 21.9 %copy-start.17 = (f32[224,128]{1,0:T(8,128)S(1)}, f32[224,128]{1,0:T(8,128)}, u32[]{:S(2)}) copy-start(f32[224,128]{1,0:T(8,128)} %copy-done.16) | copy-start | bytes 344068
  102.1 21.9 %copy-start.19 = (f32[1,640]{1,0:T(1,128)S(1)}, f32[1,640]{1,0:T(1,128)}, u32[]{:S(2)}) copy-start(f32[1,640]{1,0:T(1,128)} %copy-done.18) | copy-start | bytes 7684
  102.1 31.0 %collective-permute-start.4 = (f32[56,1280]{1,0:T(8,128)}, f32[56,1280]{1,0:T(8,128)}, u32[]{:S(2)}, u32[]{:S(2)}) collective-permute-start(f32[56,1280]{1,0:T(8,128)} %get-tuple-element.31), channel_id=1, source_target_pairs={{0,6},{2,0},{4,2},{6,4},{1,7},{3,1},{5,3},{7,5},{8,14},{10,8},{12,... | collective-permute-start | bytes 860168 | tf_op jit(solution)/shard_map/ppermute | solution.py:271
  115.4 23.9 %copy-start.10 = (f32[1,224,128]{2,1,0:T(8,128)S(1)}, f32[1,224,128]{2,1,0:T(8,128)}, u32[]{:S(2)}) copy-start(f32[1,224,128]{2,1,0:T(8,128)} %param.13) | copy-start | bytes 344068
  115.5 23.9 %copy-start.13 = (f32[1,224,128]{2,1,0:T(8,128)S(1)}, f32[1,224,128]{2,1,0:T(8,128)}, u32[]{:S(2)}) copy-start(f32[1,224,128]{2,1,0:T(8,128)} %param.12) | copy-start | bytes 344068
  115.5 23.9 %copy-start.21 = (f32[10,224]{1,0:T(8,128)S(1)}, f32[10,224]{1,0:T(8,128)}, u32[]{:S(2)}) copy-start(f32[10,224]{1,0:T(8,128)} %copy-done.20) | copy-start | bytes 26884
  115.5 23.9 %copy-start.23 = (f32[10]{0:T(128)S(1)}, f32[10]{0:T(128)}, u32[]{:S(2)}) copy-start(f32[10]{0:T(128)} %skip_ref.3) | copy-start | bytes 124
  115.5 31.2 %copy-start.15 = (f32[768,128]{1,0:T(8,128)S(1)}, f32[768,128]{1,0:T(8,128)}, u32[]{:S(2)}) copy-start(f32[768,128]{1,0:T(8,128)} %copy-done.14) | copy-start | bytes 1179652
  125.8 21.0 %all-to-all-start.2 = ((f32[32,24,128]{2,1,0:T(8,128)}), f32[32,24,128]{2,1,0:T(8,128)S(1)}, u32[]{:S(2)}, u32[]{:S(2)}) async-start(f32[32,24,128]{2,1,0:T(8,128)} %bitcast.15), calls=%async_computation.2 | async-start | bytes 786432 | tf_op jit(solution)/shard_map/all_to_all | solution.py:275
  135.2 39.8 %collective-permute-start.2 = (f32[56,1280]{1,0:T(8,128)}, f32[56,1280]{1,0:T(8,128)}, u32[]{:S(2)}, u32[]{:S(2)}) collective-permute-start(f32[56,1280]{1,0:T(8,128)} %get-tuple-element.28), channel_id=1, source_target_pairs={{0,2},{2,4},{4,6},{6,0},{1,3},{3,5},{5,7},{7,1},{8,10},{10,12},{12... | collective-permute-start | bytes 860168 | tf_op jit(solution)/shard_map/ppermute | solution.py:271
  135.2 39.8 %collective-permute-start.5 = (f32[56,1280]{1,0:T(8,128)S(1)}, f32[56,1280]{1,0:T(8,128)}, u32[]{:S(2)}, u32[]{:S(2)}) collective-permute-start(f32[56,1280]{1,0:T(8,128)S(1)} %get-tuple-element.29), channel_id=1, source_target_pairs={{0,6},{2,0},{4,2},{6,4},{1,7},{3,1},{5,3},{7,5},{8,14},{10,8},{12,... | collective-permute-start | bytes 860168 | tf_op jit(solution)/shard_map/ppermute | solution.py:271
  147.6 28.6 %all-to-all-start.3 = ((f32[32,24,128]{2,1,0:T(8,128)}), f32[32,24,128]{2,1,0:T(8,128)S(1)}, u32[]{:S(2)}, u32[]{:S(2)}) async-start(f32[32,24,128]{2,1,0:T(8,128)} %bitcast.17), calls=%async_computation.3 | async-start | bytes 786432 | tf_op jit(solution)/shard_map/all_to_all | solution.py:275
  152.5 41.4 %reduce-scatter.8.cloned.1.call-start = ((), (), s32[]{:S(2)}) async-start(), calls=%async_computation.7 | async-start | bytes 307200
Sparse Core Ops, SparseCore 0:
  76.7 98.2 reduce-scatter.5
  178.0 15.8 reduce-scatter.7

commit v2 on v1

--- a/solution.py
+++ b/solution.py
@@ -32,23 +32,77 @@
     return dot(a_high, b_high, dims) + (dot(a_high, b_low, dims) + dot(a_low, b_high, dims))
 
 
-def call(body, outs, ins, flops, nbytes, scratch=(), smem=(), grid=None, in_specs=None, out_specs=None, name=None):
-    if in_specs is None:
-        in_specs = [
-            pl.BlockSpec(memory_space=pltpu.SMEM if i in smem else pltpu.VMEM) for i in range(len(ins))
-        ]
-        out_specs = [pl.BlockSpec(memory_space=pltpu.VMEM)] * len(outs)
+TILE = 256
+
+
+class Copies:
+    def __init__(self, sources, held, in_sems, tile_sems, made, targets, out_sems):
+        self.sources, self.held, self.in_sems, self.tile_sems = sources, held, in_sems, tile_sems
+        self.out = [pltpu.make_async_copy(a, b, out_sems.at[j]) for j, (a, b) in enumerate(zip(made, targets))]
+        self.started = set()
+
+    def whole(self, i):
+        return pltpu.make_async_copy(self.sources[i], self.held[i], self.in_sems.at[i])
+
+    def tile(self, i, k):
+        here = pl.ds(pl.multiple_of(k * TILE, TILE), TILE)
+        return pltpu.make_async_copy(self.sources[i].at[:, here], self.held[i].at[:, here], self.tile_sems.at[k])
+
+    def flush(self, *which):
+        for j in which:
+            self.out[j].start()
+            self.started.add(j)
+
+
+def call(body, outs, ins, name, us, scratch=(), smem=(), tiled=None, after=(), io=False, fixed=(), vmem=40):
+    outs = [o if isinstance(o, jax.ShapeDtypeStruct) else jax.ShapeDtypeStruct(o, F32) for o in outs]
+    n, m = len(ins), len(outs)
+    big = [i for i in range(n) if i not in smem]
+    tiles = ins[tiled].shape[1] // TILE if tiled is not None else 1
+
+    def run(*refs):
+        refs = list(refs)
+        sources, refs = refs[:n], refs[n + len(after) :]
+        targets, refs = refs[:m], refs[m:]
+        held, refs = dict(zip(big, refs[: len(big)])), refs[len(big) :]
+        made, refs = refs[:m], refs[m:]
+        in_sems, tile_sems, out_sems = refs[:3]
+        copies = Copies(sources, held, in_sems, tile_sems, made, targets, out_sems)
+        for i in big:
+            if i != tiled:
+                copies.whole(i).start()
+        if tiled is not None:
+            for k in range(tiles):
+                copies.tile(tiled, k).start()
+        for i in big:
+            if i != tiled:
+                copies.whole(i).wait()
+        operands = [held.get(i, sources[i]) for i in range(n)]
+        body(*([copies] if io else []), *operands, *made, *refs[3:])
+        copies.flush(*[j for j in range(m) if j not in copies.started])
+        for c in copies.out:
+            c.wait()
+
     return pl.pallas_call(
-        body,
-        out_shape=[jax.ShapeDtypeStruct(s, F32) for s in outs],
-        grid=grid if grid is not None else (),
-        in_specs=in_specs,
-        out_specs=out_specs,
-        scratch_shapes=list(scratch),
-        compiler_params=pltpu.CompilerParams(vmem_limit_bytes=48 * 1024 * 1024),
-        cost_estimate=pl.CostEstimate(flops=flops, bytes_accessed=nbytes, transcendentals=0),
+        run,
+        out_shape=outs,
+        in_specs=[
+            *[pl.BlockSpec(memory_space=pltpu.SMEM if i in smem else pltpu.HBM) for i in range(n)],
+            *[pl.BlockSpec(memory_space=pltpu.HBM)] * len(after),
+        ],
+        out_specs=[pl.BlockSpec(memory_space=pltpu.HBM)] * m,
+        scratch_shapes=[
+            *[pltpu.VMEM(ins[i].shape, ins[i].dtype) for i in big],
+            *[pltpu.VMEM(o.shape, o.dtype) for o in outs],
+            pltpu.SemaphoreType.DMA((n,)),
+            pltpu.SemaphoreType.DMA((tiles,)),
+            pltpu.SemaphoreType.DMA((m,)),
+            *scratch,
+        ],
+        compiler_params=pltpu.CompilerParams(vmem_limit_bytes=vmem * 1024 * 1024),
+        cost_estimate=pl.CostEstimate(flops=0, bytes_accessed=int(us * 3e6), transcendentals=0),
         name=name,
-    )(*ins)
+    )(*[pltpu.with_memory_space_constraint(v, pltpu.HBM) if i in fixed else v for i, v in enumerate(ins)], *after)
 
 
 def pair(table, tile, rows, turned=False):
@@ -165,7 +219,11 @@
         state = state * decay_ref[here, :] + recv_ref[here, :]
 
 
-def gate_and_norm(ranks, pitch, recv_ref, c_ref, cum_t_ref, y_ref, gate_ref, gain_ref, gated_ref, normed_ref, scale_ref, state_ref):
+def gate_out(
+    ring, ranks, pitch, io, pos_ref, recv_ref, c_ref, cum_t_ref, y_ref, gate_ref, gain_ref, w_ref,
+    gated_ref, normed_ref, scale_ref, far_left_ref, far_right_ref, next_ref, prev_ref, own_ref,
+    state_ref, high_ref, low_ref,
+):
     length, width = y_ref.shape
     unpack(recv_ref, state_ref, ranks, pitch)
     carried = dot3(c_ref[...], state_ref[...], NN)
@@ -181,43 +239,80 @@
     scale = lax.rsqrt(jnp.sum(total, axis=1, keepdims=True) * (1.0 / width) + EPS)
     scale_ref[...] = jnp.broadcast_to(scale, scale_ref.shape)
     normed_ref[...] = gated_ref[...] * scale * gain_ref[...]
-
-
-def out_blocks(ring, block, steps, pos_ref, normed_ref, w_ref, share_ref):
-    half = pl.program_id(0) // (pl.num_programs(0) // 2)
+    io.flush(0, 1, 2)
     me = pos_ref[0]
-    w = w_ref[...]
+    block = own_ref.shape[0]
     rows = []
-    for s in steps:
-        index = lax.rem(jnp.where(half == 0, me + 2 * ring - 1 - s, me + 1 + s), ring)
+    for step in (2, 1, -1, 0):
+        index = lax.rem(me + step + ring, ring)
         rows.append(normed_ref[pl.ds(pl.multiple_of(index * block, 8), block), :])
-    product = dot3(jnp.concatenate(rows, axis=0) if len(rows) > 1 else rows[0], w, NN)
-    for i in range(len(rows)):
-        share_ref[i] = product[i * block : (i + 1) * block]
-
-
-def d_normed_part(count, *refs):
-    d_refs, w_ref, out_ref = refs[:count], refs[count], refs[count + 1]
-    d = jnp.concatenate([r[...] for r in d_refs], axis=0) if count > 1 else d_refs[0][...]
-    product = dot3(d, w_ref[...], NT)
-
-    @pl.when(pl.program_id(0) == 0)
-    def _():
-        out_ref[...] = product
-
-    @pl.when(pl.program_id(0) > 0)
-    def _():
-        out_ref[...] += product
-
-
-def norm_grad(ranks, pitch, block, ring, pos_ref, near_ref, far_ref, gated_ref, scale_ref, gate_ref, gain_ref, c_ref, cum_t_ref, send_ref, dy_ref, dn_ref):
+    high_ref[...], low_ref[...] = split(jnp.concatenate(rows, axis=0))
+    half = far_left_ref.shape[1]
+    for side, far_ref in enumerate((far_left_ref, far_right_ref)):
+
+        @pl.loop(0, half // TILE)
+        def _(n):
+            k = side * (half // TILE) + n
+            io.tile(7, k).wait()
+            here = pl.ds(pl.multiple_of(k * TILE, TILE), TILE)
+            high, low = split(w_ref[:, here])
+            product = dot(high_ref[...], high, NN) + (dot(high_ref[...], low, NN) + dot(low_ref[...], high, NN))
+            far_ref[:, pl.ds(pl.multiple_of(n * TILE, TILE), TILE)] = product[:block]
+            next_ref[:, here] = product[block : 2 * block]
+            prev_ref[:, here] = product[2 * block : 3 * block]
+            own_ref[:, here] = product[3 * block :]
+
+        io.flush(3 + side)
+
+
+def turn(
+    ring, rows, pos_ref, own_ref, prev_ref, next_ref, far_left_ref, far_right_ref, normed_ref,
+    keep_ref, give_ref, high_ref, low_ref, held_ref, turned_ref,
+):
+    me, core = pos_ref[0], pos_ref[1]
+    block, model = own_ref.shape
+    length = normed_ref.shape[0]
+    wide, padded = turned_ref.shape
+    held_ref[length:, :] = jnp.zeros((padded - length, wide), F32)
+    for part in range(model // wide):
+        here = slice(part * wide, (part + 1) * wide)
+        if part * wide < model // 2:
+            far = far_left_ref[:, here]
+        else:
+            far = far_right_ref[:, part * wide - model // 2 : (part + 1) * wide - model // 2]
+        for step, piece in ((0, own_ref[:, here]), (-1, prev_ref[:, here]), (1, next_ref[:, here]), (2, far)):
+            index = lax.rem(me + step + ring, ring)
+            held_ref[pl.ds(pl.multiple_of(index * block, 8), block), :] = piece
+        turned = held_ref[...].T
+        turned_ref[...] = turned
+        high_ref[here, :], low_ref[here, :] = split(turned)
+        for chip in range(wide // (2 * rows)):
+            at = (part * wide // (2 * rows) + chip) * rows
+            keep_ref[at : at + rows, :] = turned_ref[pl.ds(pl.multiple_of((2 * chip + core) * rows, 8), rows), :]
+            give_ref[at : at + rows, :] = turned_ref[pl.ds(pl.multiple_of((2 * chip + 1 - core) * rows, 8), rows), :]
+    width = normed_ref.shape[1]
+    held_ref[:length, :width] = normed_ref[...]
+    give_ref[model // 2 :, :] = held_ref[:, :width].T
+
+
+def normed_grad(io, high_ref, low_ref, w_ref, dn_ref, sum_ref):
+    sum_ref[...] = jnp.zeros_like(sum_ref)
+
+    @pl.loop(0, w_ref.shape[1] // TILE)
+    def _(k):
+        io.tile(2, k).wait()
+        here = pl.ds(pl.multiple_of(k * TILE, TILE), TILE)
+        w_high, w_low = split(w_ref[:, here])
+        high, low = high_ref[here, :], low_ref[here, :]
+        sum_ref[...] += dot(w_high, high, NN) + (dot(w_high, low, NN) + dot(w_low, high, NN))
+
+    dn_ref[...] = sum_ref[...].T[: dn_ref.shape[0]]
+
+
+def norm_grad(
+    ranks, pitch, dn_ref, gated_ref, scale_ref, gate_ref, gain_ref, c_ref, cum_t_ref, send_ref, dy_ref
+):
     length, width = gated_ref.shape
-    me = pos_ref[0]
-    order = ring_order(ring)
-    for i, step in enumerate(order):
-        index = lax.rem(me + step + ring, ring)
-        src = near_ref[i * block : (i + 1) * block, :] if i < ring - 1 else far_ref[...]
-        dn_ref[pl.ds(pl.multiple_of(index * block, 8), block), :] = src
     scale = scale_ref[:, :1]
     total = jnp.zeros((length, LANES), F32)
     for tile in range(width // LANES):
@@ -241,18 +336,40 @@
         send_ref[pl.ds(spare, ranks, stride=pitch), :] = jnp.zeros((ranks, LANES), F32)
 
 
-def ring_order(ring):
-    return [0, -1, 1, 2]
-
-
-def weight_grad(block, ring, pos_ref, d0_ref, d1_ref, d2_ref, d3_ref, normed_ref, out_ref):
-    me = pos_ref[0]
-    d = jnp.concatenate([d0_ref[...], d1_ref[...], d2_ref[...], d3_ref[...]], axis=0)
-    rows = []
-    for step in ring_order(ring):
-        index = lax.rem(me + step + ring, ring)
-        rows.append(normed_ref[pl.ds(pl.multiple_of(index * block, 8), block), :])
-    out_ref[...] = dot3(d, jnp.concatenate(rows, axis=0), TN)
+def weight_grad(across, down, io, keep_ref, other_ref, normed_ref, out_ref, n_high_ref, n_low_ref, o_high_ref, o_low_ref):
+    length, width = normed_ref.shape
+    padded = keep_ref.shape[1]
+    rows = keep_ref.shape[0] // (across * down)
+    n_high_ref[:length, :], n_low_ref[:length, :] = split(normed_ref[...])
+    n_high_ref[length:, :] = jnp.zeros((padded - length, width), BF16)
+    n_low_ref[length:, :] = jnp.zeros((padded - length, width), BF16)
+    o_high_ref[...], o_low_ref[...] = split(other_ref[keep_ref.shape[0] :, :].T)
+    n_high, n_low, o_high, o_low = n_high_ref[...], n_low_ref[...], o_high_ref[...], o_low_ref[...]
+    for y in range(down):
+        here = slice(y * across * rows, (y + 1) * across * rows)
+        k_high, k_low = split(keep_ref[here, :])
+        t_high, t_low = split(other_ref[here, :])
+        small = dot(k_high, n_low, NN) + dot(k_low, n_high, NN) + dot(t_high, o_low, NN) + dot(t_low, o_high, NN)
+        product = dot(k_high, n_high, NN) + dot(t_high, o_high, NN) + small
+        for x in range(across):
+            at = (x * down + y) * rows
+            out_ref[at : at + rows, :] = product[x * rows : (x + 1) * rows]
+
+
+def sum_column(count, recv_ref, share_ref):
+    rows = share_ref.shape[0]
+    total = recv_ref[:rows, :]
+    for i in range(1, count):
+        total = total + recv_ref[i * rows : (i + 1) * rows, :]
+    share_ref[...] = total
+
+
+def pass_on(next_ref, prev_ref, up_ref, down_ref, next_out_ref, prev_out_ref):
+    half = up_ref.shape[1]
+    next_out_ref[:, :half] = next_ref[:, :half] + up_ref[...]
+    next_out_ref[:, half:] = next_ref[:, half:]
+    prev_out_ref[:, :half] = prev_ref[:, :half]
+    prev_out_ref[:, half:] = prev_ref[:, half:] + down_ref[...]
 
 
 def finish(ranks, pitch, recv_ref, b_ref, cum_t_ref, part_ref, dx_ref, state_ref):
@@ -271,6 +388,10 @@
     return lax.ppermute(value, axis, [(i, (i + step) % count) for i in range(count)])
 
 
+def swapped(value, axis):
+    return lax.ppermute(value, axis, [(i, i ^ 1) for i in range(lax.axis_size(axis))])
+
+
 def exchange(value, axis):
     return lax.all_to_all(value, axis, 0, 0, tiled=True)
 
@@ -280,138 +401,117 @@
     length, width = x.shape
     heads, state = ld.shape[0], b_mat.shape[1]
     model = w_out.shape[1]
-    ranks, ring = lax.axis_size("ctx"), lax.axis_size("tp")
+    ranks, ring, seqs = lax.axis_size("ctx"), lax.axis_size("tp"), lax.axis_size("dp")
     block = d_own.shape[0]
     used = state * width // ranks // LANES
     pitch = -(-(used + 1) // 8) * 8
+    pieces = (ranks * pitch, LANES)
     gain = norm_gain[None, :]
-    pos = lax.axis_index("tp").astype(jnp.int32)[None]
+    dp = lax.axis_index("dp")
+    pos = jnp.stack([lax.axis_index("tp"), lax.rem(lax.axis_index("ctx"), 2), dp]).astype(jnp.int32)
     half = model // 2
-
-    d_prev = shifted(d_own, "tp", 1)
-    d_next = shifted(d_own, "tp", -1)
-    d_far = jnp.concatenate([shifted(d_prev[:, :half], "tp", 1), shifted(d_next[:, half:], "tp", -1)], axis=1)
-
-    pieces = (ranks * pitch, LANES)
+    chips = ranks // 2
+    rows = model // ranks
+    wide = max(width, 2 * rows)
+    padded = -(-length // LANES) * LANES
+    across = 4 if chips % 16 == 0 else 2
+    down = chips // across
+    lines = [[y * across + x for x in range(across)] for y in range(down)]
+    lines = [
+        [[2 * chip + c for chip in line] for line in way for c in range(2)] for way in (lines, list(zip(*lines)))
+    ]
+
+    d_prev, d_next = shifted(d_own, "tp", 1), shifted(d_own, "tp", -1)
+    far_left, far_right = shifted(d_prev[:, :half], "tp", 1), shifted(d_next[:, half:], "tp", -1)
+
     send, cum, cum_t = call(
         functools.partial(block_state, ranks, pitch),
         [pieces, (heads, length), (length, heads)],
         [ld, x, b_mat],
-        flops=6 * length * state * width, nbytes=4 * (length * width * 2), name="block_state",
+        fixed=(0, 1, 2), name="block_state", us=0.3,
     )
     recv = exchange(send, "ctx")
     (y_local,) = call(
         functools.partial(local_output, heads),
         [(length, width)],
         [x, b_mat, c_mat, cum, cum_t, skip],
-        flops=6 * length * length * width * 4, nbytes=8 * length * width, smem=(5,), name="local_output",
+        smem=(5,), fixed=(0, 1, 2), name="local_output", us=0.3,
     )
     send, decays = call(
         functools.partial(scan_forward, ranks, pitch, used, width),
         [pieces, pieces],
         [recv],
-        flops=10 * ranks * pitch * LANES, nbytes=12 * ranks * pitch * LANES, name="scan_forward",
+        after=[y_local], name="scan_forward", us=0.3,
     )
     recv = exchange(send, "ctx")
-    gated, normed, scale = call(
-        functools.partial(gate_and_norm, ranks, pitch),
-        [(length, width), (length, width), (length, LANES)],
-        [recv, c_mat, cum_t, y_local, gate, gain],
-        flops=6 * length * state * width, nbytes=16 * length * width,
-        scratch=[pltpu.VMEM((state, width), F32)], name="gate_and_norm",
-    )
-
-    def out_part(steps):
-        tile = 256
-        return call(
-            functools.partial(out_blocks, ring, block, steps),
-            [(len(steps), block, model)],
-            [pos, normed, w_out],
-            flops=6 * len(steps) * block * width * model, nbytes=4 * width * model,
-            grid=(model // tile,),
-            in_specs=[
-                pl.BlockSpec(memory_space=pltpu.SMEM),
-                pl.BlockSpec((length, width), lambda n: (0, 0)),
-                pl.BlockSpec((width, tile), lambda n: (0, n)),
-            ],
-            out_specs=[pl.BlockSpec((len(steps), block, tile), lambda n: (0, 0, n))],
-            name="out_blocks",
-        )[0]
-
-    first = out_part((0,))[0]
-    to_next, to_prev = first[:, :half], first[:, half:]
-    rest = out_part(tuple(range(1, ring)))
-    for s in range(ring - 1):
-        to_next = shifted(to_next, "tp", 1) + rest[s][:, :half]
-        to_prev = shifted(to_prev, "tp", -1) + rest[s][:, half:]
-    out = jnp.concatenate([to_next, to_prev], axis=1)
-
-    def d_part(parts):
-        tile = 256
-        rows = sum(p.shape[0] for p in parts)
-        return call(
-            functools.partial(d_normed_part, len(parts)),
-            [(rows, width)],
-            [*parts, w_out],
-            flops=6 * rows * width * model, nbytes=4 * width * model,
-            grid=(model // tile,),
-            in_specs=[
-                *[pl.BlockSpec((p.shape[0], tile), lambda k: (0, k)) for p in parts],
-                pl.BlockSpec((width, tile), lambda k: (0, k)),
-            ],
-            out_specs=[pl.BlockSpec((rows, width), lambda k: (0, 0))],
-            name="d_normed",
-        )[0]
-
-    near = d_part([d_own, d_prev, d_next])
-    far = d_part([d_far])
+    gated, normed, scale, part_left, part_right, part_next, part_prev, part_own = call(
+        functools.partial(gate_out, ring, ranks, pitch),
+        [(length, width)] * 2 + [(length, LANES)] + [(block, half)] * 2 + [(block, model)] * 3,
+        [pos, recv, c_mat, cum_t, y_local, gate, gain, w_out],
+        smem=(0,), tiled=7, fixed=(2, 5, 7), io=True,
+        scratch=[pltpu.VMEM((state, width), F32)] + [pltpu.VMEM((length, width), BF16)] * 2,
+        name="gate_out", us=7,
+    )
+    up_far, down_far = shifted(part_left, "tp", 1), shifted(part_right, "tp", -1)
+    keep, give, d_high, d_low = call(
+        functools.partial(turn, ring, rows),
+        [(half, padded), (half + width, padded)] + [jax.ShapeDtypeStruct((model, padded), BF16)] * 2,
+        [pos, d_own, d_prev, d_next, far_left, far_right, normed],
+        scratch=[pltpu.VMEM((padded, wide), F32), pltpu.VMEM((wide, padded), F32)],
+        smem=(0,), name="turn", us=0.3,
+    )
+    other = swapped(give, "ctx")
+    (d_normed,) = call(
+        normed_grad, [(length, width)], [d_high, d_low, w_out],
+        tiled=2, fixed=(2,), io=True, scratch=[pltpu.VMEM((width, padded), F32)], name="normed_grad", us=0.3,
+    )
+    (grad_w,) = call(
+        functools.partial(weight_grad, across, down), [(half, width)], [keep, other, normed],
+        scratch=[pltpu.VMEM((padded, width), BF16)] * 4,
+        io=True, after=[d_normed], name="weight_grad", us=0.3,
+    )
+    grad_w = lax.psum_scatter(grad_w, "ctx", scatter_dimension=0, tiled=True, axis_index_groups=lines[0])
     send, dy = call(
-        functools.partial(norm_grad, ranks, pitch, block, ring),
+        functools.partial(norm_grad, ranks, pitch),
         [pieces, (length, width)],
-        [pos, near, far, gated, scale, gate, gain, c_mat, cum_t],
-        flops=6 * length * state * width, nbytes=20 * length * width, smem=(0,),
-        scratch=[pltpu.VMEM((length, width), F32)], name="norm_grad",
+        [d_normed, gated, scale, gate, gain, c_mat, cum_t],
+        fixed=(3,), name="norm_grad", us=0.3,
     )
     recv = exchange(send, "ctx")
-    tile = 256
-    (grad_w,) = call(
-        functools.partial(weight_grad, block, ring),
-        [(model, width)],
-        [pos, d_own, d_prev, d_next, d_far, normed],
-        flops=6 * length * width * model, nbytes=4 * width * model,
-        grid=(model // tile,),
-        in_specs=[
-            pl.BlockSpec(memory_space=pltpu.SMEM),
-            *[pl.BlockSpec((block, tile), lambda k: (0, k))] * 4,
-            pl.BlockSpec((length, width), lambda k: (0, 0)),
-        ],
-        out_specs=[pl.BlockSpec((tile, width), lambda k: (k, 0))],
-        name="weight_grad",
-    )
-    grad_share = lax.psum_scatter(
-        lax.psum_scatter(grad_w, "ctx", scatter_dimension=0, tiled=True), "dp", scatter_dimension=0, tiled=True
-    )
     (dx_local,) = call(
         functools.partial(local_grad, heads),
         [(length, width)],
         [dy, b_mat, c_mat, cum, cum_t, skip],
-        flops=6 * length * length * width * 4, nbytes=8 * length * width, smem=(5,), name="local_grad",
-    )
+        smem=(5,), fixed=(1, 2), name="local_grad", us=0.3,
+    )
+    part_next, part_prev = call(
+        pass_on, [(block, model)] * 2, [part_next, part_prev, up_far, down_far],
+        after=[dx_local], name="pass_on", us=0.3,
+    )
+    up, low = shifted(part_next, "tp", 1), shifted(part_prev, "tp", -1)
     (send,) = call(
         functools.partial(scan_backward, ranks, pitch),
         [pieces],
         [recv, decays],
-        flops=10 * ranks * pitch * LANES, nbytes=12 * ranks * pitch * LANES, name="scan_backward",
+        after=[part_next], name="scan_backward", us=0.3,
     )
     recv = exchange(send, "ctx")
     (dx,) = call(
         functools.partial(finish, ranks, pitch),
         [(length, width)],
         [recv, b_mat, cum_t, dx_local],
-        flops=6 * length * state * width, nbytes=12 * length * width,
-        scratch=[pltpu.VMEM((state, width), F32)], name="finish",
-    )
-    return (out[None], dx[None], grad_share)
+        fixed=(1,),
+        scratch=[pltpu.VMEM((state, width), F32)], name="finish", us=0.3,
+    )
+    out = part_own + up + low
+    grad_w, _, out = lax.optimization_barrier((grad_w, dx, out))
+    columns = [[seqs * i + p for i in line for p in range(seqs)] for line in lines[1]]
+    grad_w = lax.all_to_all(grad_w, ("ctx", "dp"), 0, 0, tiled=True, axis_index_groups=columns)
+    (share,) = call(
+        functools.partial(sum_column, down * seqs), [(rows // seqs, width)], [grad_w],
+        name="sum_column", us=1,
+    )
+    return (out[None], dx[None], share)
 
 
 def solution(mesh):

time: 203 us -> 161 us (0.79)
  waiting for transfers between devices: 64 us -> 18.7 us
  blocking collectives: 0 us -> 33.2 us
  starting transfers between devices: 51.3 us -> 38.1 us
  Pallas kernels: 52 us -> 44.1 us
  local copies, waits for them, and re-layouts: 14.1 us -> 10.1 us
  other arithmetic: 4.89 us -> 2.03 us
    all_to_all x0 -> x2, blocking collectives: none -> 33.2 us  [the longest x1 17.3 us: per_device(): lax.all_to_all(grad_w, ('ctx', 'dp'), 0, 0, tiled=True, axis_index_groups...]
    reduce_scatter x1, waiting for transfers between devices: 22.4 us -> 0.01 us  [per_device(): lax.psum_scatter(grad_w, 'ctx', scatter_dimension=0, tiled=True, axis_ind...]
    unnamed x3 -> x1, waiting for transfers between devices: 15.7 us -> 0.02 us
    ppermute x10 -> x8, starting transfers between devices: 26.3 us -> 17.7 us  [shifted(): lax.ppermute(value, axis, [(i, (i + step) % count) for i in range(count)])]
    pallas_call x13, Pallas kernels: 52 us -> 44.1 us  [call(): pl.pallas_call(run, out_shape=outs, in_specs=[*[pl.BlockSpec(memory_space...]
    ppermute x10 -> x8, waiting for transfers between devices: 14.8 us -> 7.81 us  [shifted(): lax.ppermute(value, axis, [(i, (i + step) % count) for i in range(count)])]
    all_to_all x4 -> x3, starting transfers between devices: 25 us -> 20.1 us  [exchange(): return lax.all_to_all(value, axis, 0, 0, tiled=True)]
    add x3 -> x1, other arithmetic: 4.05 us -> 1.95 us  [per_device(): out = part_own + up + low]
  transfers between devices with their start and end apart: 16 -> 13, of which waited for: 7 -> 6; matrix products, arithmetic and copies ran while one was open for 5% -> 3% of each run, Pallas kernels for 22% -> 21%
where the time goes in v2:
time: 161 us
  Pallas kernels  44.1 us (27%)
  starting transfers between devices  38.1 us (24%)
  blocking collectives  33.2 us (21%)
  waiting for transfers between devices  18.7 us (12%)
  between operations  14.3 us (9%)
  local copies, waits for them, and re-layouts  10.1 us (6%)
  other arithmetic  2.03 us (1%)
    pallas_call x13, Pallas kernels, call(): pl.pallas_call(run, out_shape=outs, in_specs=[*[pl.BlockSpec(memory_space...  44.1 us
    all_to_all x3, starting transfers between devices, exchange(): return lax.all_to_all(value, axis, 0, 0, tiled=True)  20.1 us
    ppermute x8, starting transfers between devices, shifted(): lax.ppermute(value, axis, [(i, (i + step) % count) for i in range(count)])  17.7 us
    all_to_all x1, blocking collectives, per_device(): lax.all_to_all(grad_w, ('ctx', 'dp'), 0, 0, tiled=True, axis_index_groups...  17.3 us
    all_to_all x1, blocking collectives, exchange(): return lax.all_to_all(value, axis, 0, 0, tiled=True)  16 us
    all_to_all x3, waiting for transfers between devices, exchange(): return lax.all_to_all(value, axis, 0, 0, tiled=True)  10.8 us
    unnamed x39, local copies, waits for them, and re-layouts  8.59 us
    ppermute x8, waiting for transfers between devices, shifted(): lax.ppermute(value, axis, [(i, (i + step) % count) for i in range(count)])  7.81 us
  transfers between devices with their start and end apart: 13, of which 6 were waited for; matrix products, arithmetic and copies ran while one was open for 3% of the time, Pallas kernels for 21%

profile of v2, /device:TPU:2, one launch (start us, length us, event | category | flops | bytes accessed | tf_op | source)
XLA Modules:
  0.0 160.5 jit_solution(8102489432407884952)
XLA Ops:
  7.2 6.4 %collective-permute-start.1 = (f32[56,2560]{1,0:T(8,128)}, f32[56,2560]{1,0:T(8,128)S(1)}, u32[]{:S(2)}, u32[]{:S(2)}) collective-permute-start(f32[56,2560]{1,0:T(8,128)} %bitcast.33), channel_id=1, source_target_pairs={{0,6},{2,0},{4,2},{6,4},{1,7},{3,1},{5,3},{7,5},{8,14},{10,8},{12,... | collective-permute-start | bytes 1720328 | tf_op jit(solution)/shard_map/ppermute | solution.py:388
  13.5 0.0 collective-permute-start
  13.5 1.3 copy.14
  14.9 3.1 %block_state.1 = (f32[768,128]{1,0:T(8,128)}, f32[10,224]{1,0:T(8,128)S(1)}, f32[224,10]{1,0:T(8,128)S(1)}) custom-call(f32[10,224]{1,0:T(8,128)} %bitcast.47, f32[224,640]{1,0:T(8,128)} %bitcast.38, f32[224,128]{1,0:T(8,128)} %bitcast.40), custom_call_target="tpu_custom_call" | custom-call | bytes 900000 | tf_op jit(solution)/shard_map/block_state/pallas_call | solution.py:86
  17.9 0.0 copy-start.12
  17.9 7.6 %all-to-all-start = ((f32[32,24,128]{2,1,0:T(8,128)}), f32[32,24,128]{2,1,0:T(8,128)S(1)}, u32[]{:S(2)}, u32[]{:S(2)}) async-start(f32[32,24,128]{2,1,0:T(8,128)} %bitcast.6), calls=%async_computation | async-start | bytes 786432 | tf_op jit(solution)/shard_map/all_to_all | solution.py:396
  25.6 0.0 copy-start.16
  25.6 0.6 copy-done.16
  26.2 3.4 %local_output.1.refs_1_.refs_4_ = f32[224,640]{1,0:T(8,128)S(1)} custom-call(f32[224,640]{1,0:T(8,128)} %bitcast.39, f32[224,128]{1,0:T(8,128)} %bitcast.41, f32[224,128]{1,0:T(8,128)} %bitcast.24, f32[10,224]{1,0:T(8,128)S(1)} %get-tuple-element.27.refs_3_, f32[224,10]{1,0:T(8,128)S(1)} %get-tuple-element.28.refs_4_.refs_3_.refs_6_.refs_2_, f32[10]{0:T(128)S(1)} %copy-done.16), custom_call_target="tpu_custom_call" | custom-call | bytes 900000 | tf_op jit(solution)/shard_map/local_output/pallas_call | solution.py:86
  29.7 5.0 %all-to-all-done = f32[32,24,128]{2,1,0:T(8,128)S(1)} async-done(((f32[32,24,128]{2,1,0:T(8,128)}), f32[32,24,128]{2,1,0:T(8,128)S(1)}, u32[]{:S(2)}, u32[]{:S(2)}) %all-to-all-start) | async-done | bytes 393248 | tf_op jit(solution)/shard_map/all_to_all | solution.py:396
  34.7 0.0 copy-done.12
  34.7 1.1 scan_forward.1
  35.8 5.0 %all-to-all-start.1 = ((f32[32,24,128]{2,1,0:T(8,128)}), f32[32,24,128]{2,1,0:T(8,128)S(1)}, u32[]{:S(2)}, u32[]{:S(2)}) async-start(f32[32,24,128]{2,1,0:T(8,128)} %bitcast.9), calls=%async_computation.1 | async-start | bytes 786432 | tf_op jit(solution)/shard_map/all_to_all | solution.py:396
  40.8 0.0 reduce-scatter.2.cloned.1.call-start
  40.9 0.0 collective-permute-done.1.refs_3_
  40.9 0.7 slice.9
  41.6 4.1 %collective-permute-start.3 = (f32[56,1280]{1,0:T(8,128)}, f32[56,1280]{1,0:T(8,128)}, u32[]{:S(2)}, u32[]{:S(2)}) collective-permute-start(f32[56,1280]{1,0:T(8,128)} %slice.9), channel_id=1, source_target_pairs={{0,6},{2,0},{4,2},{6,4},{1,7},{3,1},{5,3},{7,5},{8,14},{10,8},{12,... | collective-permute-start | bytes 860168 | tf_op jit(solution)/shard_map/ppermute | solution.py:388
  45.8 0.0 collective-permute-done.refs_2_
  45.8 0.7 slice.8
  46.5 0.0 collective-permute-start.2
  46.5 0.0 copy-start.14
  46.5 0.1 pad_add_fusion.refs_0_
  46.6 3.4 %all-to-all-done.1 = f32[32,24,128]{2,1,0:T(8,128)S(1)} async-done(((f32[32,24,128]{2,1,0:T(8,128)}), f32[32,24,128]{2,1,0:T(8,128)S(1)}, u32[]{:S(2)}, u32[]{:S(2)}) %all-to-all-start.1) | async-done | bytes 393248 | tf_op jit(solution)/shard_map/all_to_all | solution.py:396
  50.0 8.3 %gate_out.1 = (f32[224,640]{1,0:T(8,128)S(1)}, f32[224,640]{1,0:T(8,128)S(1)}, f32[224,128]{1,0:T(8,128)S(1)}, f32[56,1280]{1,0:T(8,128)}, f32[56,1280]{1,0:T(8,...) custom-call(s32[3]{0:T(128)S(1)} %pad_add_fusion.refs_0_, f32[768,128]{1,0:T(8,128)S(1)} %bitcast.28, ...), custom_call_target="tpu_custom_call" | custom-call | bytes 21000000 | tf_op jit(solution)/shard_map/gate_out/pallas_call | solution.py:86
  58.4 0.0 copy-start.3
  58.4 0.8 copy-done.3
  59.2 0.7 copy-done.10
  59.8 0.0 collective-permute-done.3.refs_5_
  59.8 3.4 %collective-permute-done.2.refs_4_ = f32[56,1280]{1,0:T(8,128)} collective-permute-done((f32[56,1280]{1,0:T(8,128)}, f32[56,1280]{1,0:T(8,128)}, u32[]{:S(2)}, u32[]{:S(2)}) %collective-permute-start.2) | collective-permute-done | bytes 286752 | tf_op jit(solution)/shard_map/ppermute | solution.py:388
  63.2 3.9 %turn.1 = (f32[1280,256]{1,0:T(8,128)S(1)}, f32[1920,256]{1,0:T(8,128)S(1)}, bf16[2560,256]{1,0:T(8,128)(2,1)S(1)}, bf16[2560,256]{1,0:T(8,128)(2,1)S(1)}) custom-call(s32[3]{0:T(128)S(1)} %pad_add_fusion.refs_0_, f32[56,2560]{1,0:T(8,128)S(1)} %bitcast.35, f32[56,2560]{1,0:T(8,128)S(1)} %collective-permute-done.refs_2_, ...), custom_call_target="tpu_custom_call" | custom-call | bytes 900000 | tf_op jit(solution)/shard_map/turn/pallas_call | solution.py:86
  67.2 0.3 collective-permute-start.4
  67.5 6.0 %normed_grad.1.refs_3_.refs_0_ = f32[224,640]{1,0:T(8,128)S(1)} custom-call(bf16[2560,256]{1,0:T(8,128)(2,1)S(1)} %get-tuple-element.33.refs_0_, bf16[2560,256]{1,0:T(8,128)(2,1)S(1)} %get-tuple-element.34.refs_1_, f32[640,2560]{1,0:T(8,128)} %refs_2_.1), custom_call_target="tpu_custom_call" | custom-call | bytes 900000 | tf_op jit(solution)/shard_map/normed_grad/pallas_call | solution.py:86
  73.5 0.0 collective-permute-done.4.refs_1_
  73.5 5.4 %weight_grad.1 = f32[1280,640]{1,0:T(8,128)} custom-call(f32[1280,256]{1,0:T(8,128)S(1)} %get-tuple-element.31.refs_0_, f32[1920,256]{1,0:T(8,128)S(1)} %collective-permute-done.4.refs_1_, f32[224,640]{1,0:T(8,128)S(1)} %get-tuple-element.30.refs_6_.refs_2_, f32[224,640]{1,0:T(8,128)S(1)} %normed_grad.1.refs_3_.refs_0_), custom_call_target="tpu_custom_call" | custom-call | bytes 900000 | tf_op jit(solution)/shard_map/weight_grad/pallas_call | solution.py:86
  79.0 0.0 copy-start
  79.0 0.0 copy-start.4
  79.0 0.0 reduce-scatter.2.cloned.1.call-update
  79.0 0.1 collective-permute-start.5
  79.1 4.1 %collective-permute-start.6 = (f32[56,1280]{1,0:T(8,128)}, f32[56,1280]{1,0:T(8,128)}, u32[]{:S(2)}, u32[]{:S(2)}) collective-permute-start(f32[56,1280]{1,0:T(8,128)} %get-tuple-element.42), channel_id=1, source_target_pairs={{0,6},{2,0},{4,2},{6,4},{1,7},{3,1},{5,3},{7,5},{8,14},{10,8},{12,... | collective-permute-start | bytes 860168 | tf_op jit(solution)/shard_map/ppermute | solution.py:388
  83.2 0.9 copy-done.11
  84.1 3.2 %norm_grad.1 = (f32[768,128]{1,0:T(8,128)}, f32[224,640]{1,0:T(8,128)S(1)}) custom-call(f32[224,640]{1,0:T(8,128)S(1)} %normed_grad.1.refs_3_.refs_0_, f32[224,640]{1,0:T(8,128)S(1)} %copy-done.4, f32[224,128]{1,0:T(8,128)S(1)} %copy-done.11, f32[224,640]{1,0:T(8,128)} %bitcast.37, f32[1,640]{1,0:T(1,128)S(1)} %copy-done.15, f32[224,128]{1,0:T(8,128)S(1)} %bitcast.27, ...), custom_call_target="tpu_custom_call" | custom-call | bytes 900000 | tf_op jit(solution)/shard_map/norm_grad/pallas_call | solution.py:86
  87.3 0.0 copy-start.5
  87.3 0.8 copy-done.5
  88.1 7.5 %all-to-all-start.2 = ((f32[32,24,128]{2,1,0:T(8,128)}), f32[32,24,128]{2,1,0:T(8,128)S(1)}, u32[]{:S(2)}, u32[]{:S(2)}) async-start(f32[32,24,128]{2,1,0:T(8,128)} %bitcast.12), calls=%async_computation.3 | async-start | bytes 786432 | tf_op jit(solution)/shard_map/all_to_all | solution.py:396
  95.6 0.0 copy-start.6
  95.6 1.1 copy-done.6
  96.7 0.7 copy-done.13
  97.4 0.7 copy-done.17
  98.1 3.4 %local_grad.1.refs_4_.refs_3_ = f32[224,640]{1,0:T(8,128)S(1)} custom-call(f32[224,640]{1,0:T(8,128)S(1)} %copy-done.6, f32[224,128]{1,0:T(8,128)} %bitcast.42, f32[224,128]{1,0:T(8,128)} %bitcast.26, f32[10,224]{1,0:T(8,128)S(1)} %copy-done.13, f32[224,10]{1,0:T(8,128)S(1)} %get-tuple-element.28.refs_4_.refs_3_.refs_6_.refs_2_, f32[10]{0:T(128)S(1)} %copy-done.17), custom_call_target="tpu_custom_call" | custom-call | bytes 900000 | tf_op jit(solution)/shard_map/local_grad/pallas_call | solution.py:86
  101.5 0.0 collective-permute-done.5.refs_2_
  101.5 0.0 collective-permute-done.6.refs_3_
  101.5 2.3 %pass_on.1 = (f32[56,2560]{1,0:T(8,128)S(1)}, f32[56,2560]{1,0:T(8,128)}) custom-call(f32[56,2560]{1,0:T(8,128)S(1)} %get-tuple-element.39.refs_0_, f32[56,2560]{1,0:T(8,128)S(1)} %copy-done.2, f32[56,1280]{1,0:T(8,128)} %collective-permute-done.5.refs_2_, f32[56,1280]{1,0:T(8,128)} %collective-permute-done.6.refs_3_, f32[224,640]{1,0:T(8,128)S(1)} %local_grad.1.refs_4_.refs_3_), custom_call_target="tpu_custom_call" | custom-call | bytes 900000 | tf_op jit(solution)/shard_map/pass_on/pallas_call | solution.py:86
  103.8 0.1 collective-permute-start.8
  103.9 2.9 %collective-permute-start.7 = (f32[56,2560]{1,0:T(8,128)S(1)}, f32[56,2560]{1,0:T(8,128)}, u32[]{:S(2)}, u32[]{:S(2)}) collective-permute-start(f32[56,2560]{1,0:T(8,128)S(1)} %get-tuple-element.44.refs_2_), channel_id=1, source_target_pairs={{0,2},{2,4},{4,6},{6,0},{1,3},{3,5},{5,7},{7,1},{8,10},{10,12},{12... | collective-permute-start | bytes 1720328 | tf_op jit(solution)/shard_map/ppermute | solution.py:388
  106.8 2.4 %all-to-all-done.2 = f32[32,24,128]{2,1,0:T(8,128)S(1)} async-done(((f32[32,24,128]{2,1,0:T(8,128)}), f32[32,24,128]{2,1,0:T(8,128)S(1)}, u32[]{:S(2)}, u32[]{:S(2)}) %all-to-all-start.2) | async-done | bytes 393248 | tf_op jit(solution)/shard_map/all_to_all | solution.py:396
  109.2 1.0 copy-done.9
  110.2 0.7 scan_backward.1
  110.9 16.0 %all_to_all.55 = f32[32,24,128]{2,1,0:T(8,128)S(1)} all-to-all(f32[32,24,128]{2,1,0:T(8,128)S(1)} %bitcast.32), channel_id=1, replica_groups=mesh['ctx'=32,'tp'=4,'dp'=2] {'ctx'}, dimensions={0} | all-to-all | bytes 786432 | tf_op jit(solution)/shard_map/all_to_all | solution.py:396
  126.8 2.4 %finish.1 = f32[224,640]{1,0:T(8,128)} custom-call(f32[768,128]{1,0:T(8,128)S(1)} %bitcast.29, f32[224,128]{1,0:T(8,128)} %bitcast.43, f32[224,10]{1,0:T(8,128)S(1)} %get-tuple-element.28.refs_4_.refs_3_.refs_6_.refs_2_, f32[224,640]{1,0:T(8,128)S(1)} %local_grad.1.refs_4_.refs_3_), custom_call_target="tpu_custom_call" | custom-call | bytes 900000 | tf_op jit(solution)/shard_map/finish/pallas_call | solution.py:86
  129.2 3.1 %collective-permute-done.8 = f32[56,2560]{1,0:T(8,128)S(1)} collective-permute-done((f32[56,2560]{1,0:T(8,128)}, f32[56,2560]{1,0:T(8,128)S(1)}, u32[]{:S(2)}, u32[]{:S(2)}) %collective-permute-start.8) | collective-permute-done | bytes 573472 | tf_op jit(solution)/shard_map/ppermute | solution.py:388
  132.3 1.3 collective-permute-done.7
  133.6 1.9 %add_add_fusion = f32[56,2560]{1,0:T(8,128)} fusion(f32[56,2560]{1,0:T(8,128)S(1)} %collective-permute-done.8, f32[56,2560]{1,0:T(8,128)S(1)} %get-tuple-element.45, f32[56,2560]{1,0:T(8,128)} %collective-permute-done.7), kind=kLoop, calls=%fused_computation | loop fusion | flops 286720 | bytes 2293760 | tf_op jit(solution)/shard_map/add | solution.py:506
  135.6 17.3 %all_to_all.56 = f32[8,40,640]{2,1,0:T(8,128)S(1)} all-to-all(f32[8,40,640]{2,1,0:T(8,128)} %bitcast.44), channel_id=1, replica_groups={{0,1,64,65,128,129,192,193},{8,9,72,73,136,137,200,201},{16,17,80,81,14..., dimensions={0} | all-to-all | bytes 1638400 | tf_op jit(solution)/shard_map/all_to_all | solution.py:509
  152.9 0.8 sum_column.1
  (22 shorter events, 0.0 us)
Async XLA Ops:
  7.2 33.7 %collective-permute-start.1 = (f32[56,2560]{1,0:T(8,128)}, f32[56,2560]{1,0:T(8,128)S(1)}, u32[]{:S(2)}, u32[]{:S(2)}) collective-permute-start(f32[56,2560]{1,0:T(8,128)} %bitcast.33), channel_id=1, source_target_pairs={{0,6},{2,0},{4,2},{6,4},{1,7},{3,1},{5,3},{7,5},{8,14},{10,8},{12,... | collective-permute-start | bytes 1720328 | tf_op jit(solution)/shard_map/ppermute | solution.py:388
  13.5 32.2 %collective-permute-start = (f32[56,2560]{1,0:T(8,128)}, f32[56,2560]{1,0:T(8,128)S(1)}, u32[]{:S(2)}, u32[]{:S(2)}) collective-permute-start(f32[56,2560]{1,0:T(8,128)} %bitcast.34), channel_id=1, source_target_pairs={{0,2},{2,4},{4,6},{6,0},{1,3},{3,5},{5,7},{7,1},{8,10},{10,12},{12... | collective-permute-start | bytes 1720328 | tf_op jit(solution)/shard_map/ppermute | solution.py:388
  17.9 16.7 %copy-start.12 = (f32[10,224]{1,0:T(8,128)}, f32[10,224]{1,0:T(8,128)S(1)}, u32[]{:S(2)}) copy-start(f32[10,224]{1,0:T(8,128)S(1)} %get-tuple-element.27.refs_3_) | copy-start | bytes 26884
  17.9 16.7 %all-to-all-start = ((f32[32,24,128]{2,1,0:T(8,128)}), f32[32,24,128]{2,1,0:T(8,128)S(1)}, u32[]{:S(2)}, u32[]{:S(2)}) async-start(f32[32,24,128]{2,1,0:T(8,128)} %bitcast.6), calls=%async_computation | async-start | bytes 786432 | tf_op jit(solution)/shard_map/all_to_all | solution.py:396
  25.6 0.7 copy-start.16
  26.2 20.3 %copy-start.18 = (f32[640]{0:T(1024)S(1)}, f32[640]{0:T(1024)}, u32[]{:S(2)}) copy-start(f32[640]{0:T(1024)} %param.15) | copy-start | bytes 7684
  35.8 14.2 %copy-start.8 = (f32[768,128]{1,0:T(8,128)}, f32[768,128]{1,0:T(8,128)S(1)}, u32[]{:S(2)}) copy-start(f32[768,128]{1,0:T(8,128)S(1)} %get-tuple-element.38.refs_1_) | copy-start | bytes 1179652
  35.8 14.2 %all-to-all-start.1 = ((f32[32,24,128]{2,1,0:T(8,128)}), f32[32,24,128]{2,1,0:T(8,128)S(1)}, u32[]{:S(2)}, u32[]{:S(2)}) async-start(f32[32,24,128]{2,1,0:T(8,128)} %bitcast.9), calls=%async_computation.1 | async-start | bytes 786432 | tf_op jit(solution)/shard_map/all_to_all | solution.py:396
  40.8 94.8 %reduce-scatter.2.cloned.1.call-start = ((), (), s32[]{:S(2)}) async-start(), calls=%async_computation.6 | async-start | bytes 4096000 | tf_op jit(solution)/shard_map/reduce_scatter | solution.py:473
  41.6 18.2 %collective-permute-start.3 = (f32[56,1280]{1,0:T(8,128)}, f32[56,1280]{1,0:T(8,128)}, u32[]{:S(2)}, u32[]{:S(2)}) collective-permute-start(f32[56,1280]{1,0:T(8,128)} %slice.9), channel_id=1, source_target_pairs={{0,6},{2,0},{4,2},{6,4},{1,7},{3,1},{5,3},{7,5},{8,14},{10,8},{12,... | collective-permute-start | bytes 860168 | tf_op jit(solution)/shard_map/ppermute | solution.py:388
  46.5 16.7 %collective-permute-start.2 = (f32[56,1280]{1,0:T(8,128)}, f32[56,1280]{1,0:T(8,128)}, u32[]{:S(2)}, u32[]{:S(2)}) collective-permute-start(f32[56,1280]{1,0:T(8,128)} %slice.8), channel_id=1, source_target_pairs={{0,2},{2,4},{4,6},{6,0},{1,3},{3,5},{5,7},{7,1},{8,10},{10,12},{12... | collective-permute-start | bytes 860168 | tf_op jit(solution)/shard_map/ppermute | solution.py:388
  46.5 11.8 %copy-start.14 = (f32[1,640]{1,0:T(1,128)}, f32[1,640]{1,0:T(1,128)S(1)}, u32[]{:S(2)}) copy-start(f32[1,640]{1,0:T(1,128)S(1)} %broadcast_in_dim.9.refs_6_.refs_4_) | copy-start | bytes 7684
  50.0 13.2 %copy-start.7 = (f32[1,56,2560]{2,1,0:T(8,128)S(1)}, f32[1,56,2560]{2,1,0:T(8,128)}, u32[]{:S(2)}) copy-start(f32[1,56,2560]{2,1,0:T(8,128)} %param.17) | copy-start | bytes 1720324
  58.4 0.8 copy-start.3
  59.2 0.7 copy-start.10
  59.8 13.7 %copy-start.1 = (f32[56,2560]{1,0:T(8,128)}, f32[56,2560]{1,0:T(8,128)S(1)}, u32[]{:S(2)}) copy-start(f32[56,2560]{1,0:T(8,128)S(1)} %get-tuple-element.40.refs_1_) | copy-start | bytes 1720324
  67.2 6.4 %collective-permute-start.4 = (f32[1920,256]{1,0:T(8,128)S(1)}, f32[1920,256]{1,0:T(8,128)S(1)}, u32[]{:S(2)}, u32[]{:S(2)}) collective-permute-start(f32[1920,256]{1,0:T(8,128)S(1)} %get-tuple-element.32), channel_id=1, source_target_pairs={{0,8},{8,0},{16,24},{24,16},{32,40},{40,32},{48,56},{56,48},{64,72... | collective-permute-start | bytes 5898248 | tf_op jit(solution)/shard_map/ppermute | solution.py:392
  79.0 4.3 %copy-start = (f32[1,224,128]{2,1,0:T(8,128)S(1)}, f32[1,224,128]{2,1,0:T(8,128)}, u32[]{:S(2)}) copy-start(f32[1,224,128]{2,1,0:T(8,128)} %param.13) | copy-start | bytes 344068
  79.0 4.3 %copy-start.4 = (f32[224,640]{1,0:T(8,128)S(1)}, f32[224,640]{1,0:T(8,128)}, u32[]{:S(2)}) copy-start(f32[224,640]{1,0:T(8,128)} %copy-done.3) | copy-start | bytes 1720324
  79.0 4.3 %copy-start.15 = (f32[1,640]{1,0:T(1,128)S(1)}, f32[1,640]{1,0:T(1,128)}, u32[]{:S(2)}) copy-start(f32[1,640]{1,0:T(1,128)} %copy-done.14) | copy-start | bytes 7684
  79.0 22.4 %collective-permute-start.5 = (f32[56,1280]{1,0:T(8,128)}, f32[56,1280]{1,0:T(8,128)}, u32[]{:S(2)}, u32[]{:S(2)}) collective-permute-start(f32[56,1280]{1,0:T(8,128)} %get-tuple-element.41), channel_id=1, source_target_pairs={{0,2},{2,4},{4,6},{6,0},{1,3},{3,5},{5,7},{7,1},{8,10},{10,12},{12... | collective-permute-start | bytes 860168 | tf_op jit(solution)/shard_map/ppermute | solution.py:388
  79.1 22.4 %collective-permute-start.6 = (f32[56,1280]{1,0:T(8,128)}, f32[56,1280]{1,0:T(8,128)}, u32[]{:S(2)}, u32[]{:S(2)}) collective-permute-start(f32[56,1280]{1,0:T(8,128)} %get-tuple-element.42), channel_id=1, source_target_pairs={{0,6},{2,0},{4,2},{6,4},{1,7},{3,1},{5,3},{7,5},{8,14},{10,8},{12,... | collective-permute-start | bytes 860168 | tf_op jit(solution)/shard_map/ppermute | solution.py:388
  83.2 0.9 copy-start.11
  84.1 17.3 %copy-start.2 = (f32[56,2560]{1,0:T(8,128)S(1)}, f32[56,2560]{1,0:T(8,128)}, u32[]{:S(2)}) copy-start(f32[56,2560]{1,0:T(8,128)} %copy-done.1) | copy-start | bytes 1720324
  87.3 0.8 copy-start.5
  88.1 21.1 %all-to-all-start.2 = ((f32[32,24,128]{2,1,0:T(8,128)}), f32[32,24,128]{2,1,0:T(8,128)S(1)}, u32[]{:S(2)}, u32[]{:S(2)}) async-start(f32[32,24,128]{2,1,0:T(8,128)} %bitcast.12), calls=%async_computation.3 | async-start | bytes 786432 | tf_op jit(solution)/shard_map/all_to_all | solution.py:396
  95.6 1.1 copy-start.6
  96.7 0.7 copy-start.13
  97.4 0.7 copy-start.17
  103.8 28.5 %collective-permute-start.8 = (f32[56,2560]{1,0:T(8,128)}, f32[56,2560]{1,0:T(8,128)S(1)}, u32[]{:S(2)}, u32[]{:S(2)}) collective-permute-start(f32[56,2560]{1,0:T(8,128)} %get-tuple-element.46), channel_id=1, source_target_pairs={{0,6},{2,0},{4,2},{6,4},{1,7},{3,1},{5,3},{7,5},{8,14},{10,8},{12,... | collective-permute-start | bytes 1720328 | tf_op jit(solution)/shard_map/ppermute | solution.py:388
  103.9 29.7 %collective-permute-start.7 = (f32[56,2560]{1,0:T(8,128)S(1)}, f32[56,2560]{1,0:T(8,128)}, u32[]{:S(2)}, u32[]{:S(2)}) collective-permute-start(f32[56,2560]{1,0:T(8,128)S(1)} %get-tuple-element.44.refs_2_), channel_id=1, source_target_pairs={{0,2},{2,4},{4,6},{6,0},{1,3},{3,5},{5,7},{7,1},{8,10},{10,12},{12... | collective-permute-start | bytes 1720328 | tf_op jit(solution)/shard_map/ppermute | solution.py:388
  109.2 1.0 copy-start.9
Sparse Core Ops, SparseCore 0:
  79.1 44.3 reduce-scatter.1

commit v3 on v2

--- a/solution.py
+++ b/solution.py
@@ -295,7 +295,11 @@
     give_ref[model // 2 :, :] = held_ref[:, :width].T
 
 
-def normed_grad(io, high_ref, low_ref, w_ref, dn_ref, sum_ref):
+def norm_grad(
+    ranks, pitch, io, high_ref, low_ref, w_ref, gated_ref, scale_ref, gate_ref, gain_ref, c_ref, cum_t_ref,
+    send_ref, dy_ref, sum_ref, dn_ref,
+):
+    length, width = gated_ref.shape
     sum_ref[...] = jnp.zeros_like(sum_ref)
 
     @pl.loop(0, w_ref.shape[1] // TILE)
@@ -306,18 +310,12 @@
         high, low = high_ref[here, :], low_ref[here, :]
         sum_ref[...] += dot(w_high, high, NN) + (dot(w_high, low, NN) + dot(w_low, high, NN))
 
-    dn_ref[...] = sum_ref[...].T[: dn_ref.shape[0]]
-
-
-def norm_grad(
-    ranks, pitch, dn_ref, gated_ref, scale_ref, gate_ref, gain_ref, c_ref, cum_t_ref, send_ref, dy_ref
-):
-    length, width = gated_ref.shape
+    dn_ref[...] = sum_ref[...].T
     scale = scale_ref[:, :1]
     total = jnp.zeros((length, LANES), F32)
     for tile in range(width // LANES):
         here = slice(LANES * tile, LANES * (tile + 1))
-        total = total + dn_ref[:, here] * gain_ref[:, here] * gated_ref[:, here]
+        total = total + dn_ref[:length, here] * gain_ref[:, here] * gated_ref[:, here]
     mean = jnp.sum(total, axis=1, keepdims=True) * (1.0 / width)
     shift = scale * scale * scale * mean
     from_start = jnp.exp(cum_t_ref[...])
@@ -325,7 +323,7 @@
     for tile in range(width // LANES):
         here = slice(LANES * tile, LANES * (tile + 1))
         gate = gate_ref[:, here]
-        d_gated = dn_ref[:, here] * gain_ref[:, here] * scale - gated_ref[:, here] * shift
+        d_gated = dn_ref[:length, here] * gain_ref[:, here] * scale - gated_ref[:, here] * shift
         dy = d_gated * (gate / (1.0 + jnp.exp(-gate)))
         dy_ref[:, here] = dy
         scaled.append(dy * pair(from_start, tile, length))
@@ -461,22 +459,20 @@
         smem=(0,), name="turn", us=0.3,
     )
     other = swapped(give, "ctx")
-    (d_normed,) = call(
-        normed_grad, [(length, width)], [d_high, d_low, w_out],
-        tiled=2, fixed=(2,), io=True, scratch=[pltpu.VMEM((width, padded), F32)], name="normed_grad", us=0.3,
+    send, dy = call(
+        functools.partial(norm_grad, ranks, pitch),
+        [pieces, (length, width)],
+        [d_high, d_low, w_out, gated, scale, gate, gain, c_mat, cum_t],
+        tiled=2, fixed=(2, 5, 7), io=True,
+        scratch=[pltpu.VMEM((width, padded), F32), pltpu.VMEM((padded, width), F32)],
+        name="norm_grad", us=0.3,
     )
     (grad_w,) = call(
         functools.partial(weight_grad, across, down), [(half, width)], [keep, other, normed],
         scratch=[pltpu.VMEM((padded, width), BF16)] * 4,
-        io=True, after=[d_normed], name="weight_grad", us=0.3,
+        io=True, after=[dy], name="weight_grad", us=0.3,
     )
     grad_w = lax.psum_scatter(grad_w, "ctx", scatter_dimension=0, tiled=True, axis_index_groups=lines[0])
-    send, dy = call(
-        functools.partial(norm_grad, ranks, pitch),
-        [pieces, (length, width)],
-        [d_normed, gated, scale, gate, gain, c_mat, cum_t],
-        fixed=(3,), name="norm_grad", us=0.3,
-    )
     recv = exchange(send, "ctx")
     (dx_local,) = call(
         functools.partial(local_grad, heads),

time: 161 us -> 159 us (0.988)
  local copies, waits for them, and re-layouts: 10.1 us -> 6.01 us
  blocking collectives: 33.2 us -> 37.2 us
    unnamed x39 -> x17, local copies, waits for them, and re-layouts: 8.59 us -> 4.53 us
    all_to_all x1, blocking collectives: 16 us -> 20 us  [exchange(): return lax.all_to_all(value, axis, 0, 0, tiled=True)]
    pallas_call x13 -> x12, Pallas kernels: 44.1 us -> 43.1 us  [call(): pl.pallas_call(run, out_shape=outs, in_specs=[*[pl.BlockSpec(memory_space...]
  transfers between devices with their start and end apart: 13 -> 13, of which waited for: 6 -> 6; matrix products, arithmetic and copies ran while one was open for 3% -> 2% of each run, Pallas kernels for 21% -> 21%
where the time goes in v3:
time: 159 us
  Pallas kernels  43.1 us (27%)
  starting transfers between devices  39.5 us (25%)
  blocking collectives  37.2 us (23%)
  waiting for transfers between devices  17.7 us (11%)
  between operations  14.3 us (9%)
  local copies, waits for them, and re-layouts  6.01 us (4%)
    pallas_call x12, Pallas kernels, call(): pl.pallas_call(run, out_shape=outs, in_specs=[*[pl.BlockSpec(memory_space...  43.1 us
    all_to_all x3, starting transfers between devices, exchange(): return lax.all_to_all(value, axis, 0, 0, tiled=True)  20.1 us
    all_to_all x1, blocking collectives, exchange(): return lax.all_to_all(value, axis, 0, 0, tiled=True)  20 us
    ppermute x8, starting transfers between devices, shifted(): lax.ppermute(value, axis, [(i, (i + step) % count) for i in range(count)])  19.1 us
    all_to_all x1, blocking collectives, per_device(): lax.all_to_all(grad_w, ('ctx', 'dp'), 0, 0, tiled=True, axis_index_groups...  17.2 us
    all_to_all x3, waiting for transfers between devices, exchange(): return lax.all_to_all(value, axis, 0, 0, tiled=True)  9.6 us
    ppermute x8, waiting for transfers between devices, shifted(): lax.ppermute(value, axis, [(i, (i + step) % count) for i in range(count)])  8.1 us
    unnamed x17, local copies, waits for them, and re-layouts  4.53 us
  transfers between devices with their start and end apart: 13, of which 6 were waited for; matrix products, arithmetic and copies ran while one was open for 2% of the time, Pallas kernels for 21%

profile of v3, /device:TPU:2, one launch (start us, length us, event | category | flops | bytes accessed | tf_op | source)
XLA Modules:
  0.0 158.8 jit_solution(7199494398464881145)
XLA Ops:
  7.2 6.4 %collective-permute-start.1 = (f32[56,2560]{1,0:T(8,128)}, f32[56,2560]{1,0:T(8,128)S(1)}, u32[]{:S(2)}, u32[]{:S(2)}) collective-permute-start(f32[56,2560]{1,0:T(8,128)} %bitcast.29), channel_id=1, source_target_pairs={{0,6},{2,0},{4,2},{6,4},{1,7},{3,1},{5,3},{7,5},{8,14},{10,8},{12,... | collective-permute-start | bytes 1720328 | tf_op jit(solution)/shard_map/ppermute | solution.py:386
  13.5 0.0 collective-permute-start
  13.5 1.3 copy.14
  14.9 3.1 %block_state.1 = (f32[768,128]{1,0:T(8,128)}, f32[10,224]{1,0:T(8,128)S(1)}, f32[224,10]{1,0:T(8,128)S(1)}) custom-call(f32[10,224]{1,0:T(8,128)} %bitcast.47, f32[224,640]{1,0:T(8,128)} %bitcast.34, f32[224,128]{1,0:T(8,128)} %bitcast.40), custom_call_target="tpu_custom_call" | custom-call | bytes 900000 | tf_op jit(solution)/shard_map/block_state/pallas_call | solution.py:86
  17.9 7.6 %all-to-all-start = ((f32[32,24,128]{2,1,0:T(8,128)}), f32[32,24,128]{2,1,0:T(8,128)S(1)}, u32[]{:S(2)}, u32[]{:S(2)}) async-start(f32[32,24,128]{2,1,0:T(8,128)} %bitcast.6), calls=%async_computation | async-start | bytes 786432 | tf_op jit(solution)/shard_map/all_to_all | solution.py:394
  25.6 0.0 copy-start.5
  25.6 0.6 copy-done.5
  26.2 0.0 copy-start.7
  26.2 3.4 %local_output.1.refs_1_.refs_4_ = f32[224,640]{1,0:T(8,128)S(1)} custom-call(f32[224,640]{1,0:T(8,128)} %bitcast.35, f32[224,128]{1,0:T(8,128)} %bitcast.41, f32[224,128]{1,0:T(8,128)} %bitcast.36, f32[10,224]{1,0:T(8,128)S(1)} %get-tuple-element.27.refs_3_, f32[224,10]{1,0:T(8,128)S(1)} %get-tuple-element.28.refs_4_.refs_3_.refs_8_.refs_2_, f32[10]{0:T(128)S(1)} %copy-done.5), custom_call_target="tpu_custom_call" | custom-call | bytes 900000 | tf_op jit(solution)/shard_map/local_output/pallas_call | solution.py:86
  29.7 5.0 %all-to-all-done = f32[32,24,128]{2,1,0:T(8,128)S(1)} async-done(((f32[32,24,128]{2,1,0:T(8,128)}), f32[32,24,128]{2,1,0:T(8,128)S(1)}, u32[]{:S(2)}, u32[]{:S(2)}) %all-to-all-start) | async-done | bytes 393248 | tf_op jit(solution)/shard_map/all_to_all | solution.py:394
  34.7 1.1 scan_forward.1
  35.8 0.0 copy-start.3
  35.8 0.7 copy-done.3
  36.6 5.0 %all-to-all-start.1 = ((f32[32,24,128]{2,1,0:T(8,128)}), f32[32,24,128]{2,1,0:T(8,128)S(1)}, u32[]{:S(2)}, u32[]{:S(2)}) async-start(f32[32,24,128]{2,1,0:T(8,128)} %bitcast.9), calls=%async_computation.1 | async-start | bytes 786432 | tf_op jit(solution)/shard_map/all_to_all | solution.py:394
  41.6 0.0 reduce-scatter.2.cloned.1.call-start
  41.6 0.0 collective-permute-done.1.refs_3_
  41.6 0.7 slice.9
  42.4 4.1 %collective-permute-start.3 = (f32[56,1280]{1,0:T(8,128)}, f32[56,1280]{1,0:T(8,128)}, u32[]{:S(2)}, u32[]{:S(2)}) collective-permute-start(f32[56,1280]{1,0:T(8,128)} %slice.9), channel_id=1, source_target_pairs={{0,6},{2,0},{4,2},{6,4},{1,7},{3,1},{5,3},{7,5},{8,14},{10,8},{12,... | collective-permute-start | bytes 860168 | tf_op jit(solution)/shard_map/ppermute | solution.py:386
  46.5 0.0 collective-permute-done.refs_2_
  46.5 0.7 slice.8
  47.2 0.0 collective-permute-start.2
  47.2 0.0 copy-done.7
  47.3 0.1 pad_add_fusion.refs_0_
  47.3 3.4 %all-to-all-done.1 = f32[32,24,128]{2,1,0:T(8,128)S(1)} async-done(((f32[32,24,128]{2,1,0:T(8,128)}), f32[32,24,128]{2,1,0:T(8,128)S(1)}, u32[]{:S(2)}, u32[]{:S(2)}) %all-to-all-start.1) | async-done | bytes 393248 | tf_op jit(solution)/shard_map/all_to_all | solution.py:394
  50.8 0.0 copy-start.2
  50.8 8.3 %gate_out.1 = (f32[224,640]{1,0:T(8,128)S(1)}, f32[224,640]{1,0:T(8,128)S(1)}, f32[224,128]{1,0:T(8,128)S(1)}, f32[56,1280]{1,0:T(8,128)}, f32[56,1280]{1,0:T(8,...) custom-call(s32[3]{0:T(128)S(1)} %pad_add_fusion.refs_0_, f32[768,128]{1,0:T(8,128)S(1)} %bitcast.24, ...), custom_call_target="tpu_custom_call" | custom-call | bytes 21000000 | tf_op jit(solution)/shard_map/gate_out/pallas_call | solution.py:86
  59.1 0.0 copy-start
  59.1 0.8 copy-done
  59.9 0.0 collective-permute-done.3.refs_5_
  59.9 4.1 %collective-permute-done.2.refs_4_ = f32[56,1280]{1,0:T(8,128)} collective-permute-done((f32[56,1280]{1,0:T(8,128)}, f32[56,1280]{1,0:T(8,128)}, u32[]{:S(2)}, u32[]{:S(2)}) %collective-permute-start.2) | collective-permute-done | bytes 286752 | tf_op jit(solution)/shard_map/ppermute | solution.py:386
  64.0 0.0 copy-done.2
  64.0 3.9 %turn.1 = (f32[1280,256]{1,0:T(8,128)S(1)}, f32[1920,256]{1,0:T(8,128)S(1)}, bf16[2560,256]{1,0:T(8,128)(2,1)S(1)}, bf16[2560,256]{1,0:T(8,128)(2,1)S(1)}) custom-call(s32[3]{0:T(128)S(1)} %pad_add_fusion.refs_0_, f32[56,2560]{1,0:T(8,128)S(1)} %bitcast.31, f32[56,2560]{1,0:T(8,128)S(1)} %collective-permute-done.refs_2_, ...), custom_call_target="tpu_custom_call" | custom-call | bytes 900000 | tf_op jit(solution)/shard_map/turn/pallas_call | solution.py:86
  67.9 0.3 collective-permute-start.4
  68.2 8.2 %norm_grad.1 = (f32[768,128]{1,0:T(8,128)}, f32[224,640]{1,0:T(8,128)S(1)}) custom-call(bf16[2560,256]{1,0:T(8,128)(2,1)S(1)} %get-tuple-element.33.refs_0_, bf16[2560,256]{1,0:T(8,128)(2,1)S(1)} %get-tuple-element.34.refs_1_, f32[640,2560]{1,0:T(8,128)} %refs_2_.1, f32[224,640]{1,0:T(8,128)S(1)} %get-tuple-element.35.refs_3_, ...), custom_call_target="tpu_custom_call" | custom-call | bytes 900000 | tf_op jit(solution)/shard_map/norm_grad/pallas_call | solution.py:86
  76.4 0.0 collective-permute-done.4.refs_1_
  76.4 5.4 %weight_grad.1 = f32[1280,640]{1,0:T(8,128)} custom-call(f32[1280,256]{1,0:T(8,128)S(1)} %get-tuple-element.31.refs_0_, f32[1920,256]{1,0:T(8,128)S(1)} %collective-permute-done.4.refs_1_, f32[224,640]{1,0:T(8,128)S(1)} %get-tuple-element.30.refs_6_.refs_2_, f32[224,640]{1,0:T(8,128)S(1)} %get-tuple-element.37.refs_3_.refs_0_), custom_call_target="tpu_custom_call" | custom-call | bytes 900000 | tf_op jit(solution)/shard_map/weight_grad/pallas_call | solution.py:86
  81.8 0.0 copy-start.6
  81.8 0.0 reduce-scatter.2.cloned.1.call-update
  81.9 0.0 copy-start.1
  81.9 0.1 collective-permute-start.5
  82.0 4.1 %collective-permute-start.6 = (f32[56,1280]{1,0:T(8,128)}, f32[56,1280]{1,0:T(8,128)}, u32[]{:S(2)}, u32[]{:S(2)}) collective-permute-start(f32[56,1280]{1,0:T(8,128)} %get-tuple-element.43), channel_id=1, source_target_pairs={{0,6},{2,0},{4,2},{6,4},{1,7},{3,1},{5,3},{7,5},{8,14},{10,8},{12,... | collective-permute-start | bytes 860168 | tf_op jit(solution)/shard_map/ppermute | solution.py:386
  86.1 7.5 %all-to-all-start.2 = ((f32[32,24,128]{2,1,0:T(8,128)}), f32[32,24,128]{2,1,0:T(8,128)S(1)}, u32[]{:S(2)}, u32[]{:S(2)}) async-start(f32[32,24,128]{2,1,0:T(8,128)} %bitcast.12), calls=%async_computation.3 | async-start | bytes 786432 | tf_op jit(solution)/shard_map/all_to_all | solution.py:394
  93.6 0.0 copy-done.6
  93.6 3.4 %local_grad.1.refs_4_.refs_3_ = f32[224,640]{1,0:T(8,128)S(1)} custom-call(f32[224,640]{1,0:T(8,128)S(1)} %get-tuple-element.37.refs_3_.refs_0_, f32[224,128]{1,0:T(8,128)} %bitcast.42, f32[224,128]{1,0:T(8,128)} %bitcast.39, f32[10,224]{1,0:T(8,128)S(1)} %get-tuple-element.27.refs_3_, f32[224,10]{1,0:T(8,128)S(1)} %get-tuple-element.28.refs_4_.refs_3_.refs_8_.refs_2_, ...), custom_call_target="tpu_custom_call" | custom-call | bytes 900000 | tf_op jit(solution)/shard_map/local_grad/pallas_call | solution.py:86
  97.0 2.3 %collective-permute-done.5.refs_2_ = f32[56,1280]{1,0:T(8,128)} collective-permute-done((f32[56,1280]{1,0:T(8,128)}, f32[56,1280]{1,0:T(8,128)}, u32[]{:S(2)}, u32[]{:S(2)}) %collective-permute-start.5) | collective-permute-done | bytes 286752 | tf_op jit(solution)/shard_map/ppermute | solution.py:386
  99.3 0.0 collective-permute-done.6.refs_3_
  99.3 0.0 copy-done.1
  99.3 2.4 %pass_on.1 = (f32[56,2560]{1,0:T(8,128)}, f32[56,2560]{1,0:T(8,128)}) custom-call(f32[56,2560]{1,0:T(8,128)S(1)} %get-tuple-element.40.refs_0_, f32[56,2560]{1,0:T(8,128)S(1)} %copy-done.1, f32[56,1280]{1,0:T(8,128)} %collective-permute-done.5.refs_2_, f32[56,1280]{1,0:T(8,128)} %collective-permute-done.6.refs_3_, f32[224,640]{1,0:T(8,128)S(1)} %local_grad.1.refs_4_.refs_3_), custom_call_target="tpu_custom_call" | custom-call | bytes 900000 | tf_op jit(solution)/shard_map/pass_on/pallas_call | solution.py:86
  101.7 4.3 %collective-permute-start.8 = (f32[56,2560]{1,0:T(8,128)}, f32[56,2560]{1,0:T(8,128)S(1)}, u32[]{:S(2)}, u32[]{:S(2)}) collective-permute-start(f32[56,2560]{1,0:T(8,128)} %get-tuple-element.46), channel_id=1, source_target_pairs={{0,6},{2,0},{4,2},{6,4},{1,7},{3,1},{5,3},{7,5},{8,14},{10,8},{12,... | collective-permute-start | bytes 1720328 | tf_op jit(solution)/shard_map/ppermute | solution.py:386
  106.0 0.0 collective-permute-start.7
  106.0 1.2 all-to-all-done.2
  107.2 0.0 copy-start.4
  107.2 1.0 copy-done.4
  108.2 0.7 scan_backward.1
  108.8 20.0 %all_to_all.55 = f32[32,24,128]{2,1,0:T(8,128)S(1)} all-to-all(f32[32,24,128]{2,1,0:T(8,128)S(1)} %bitcast.28), channel_id=1, replica_groups=mesh['ctx'=32,'tp'=4,'dp'=2] {'ctx'}, dimensions={0} | all-to-all | bytes 786432 | tf_op jit(solution)/shard_map/all_to_all | solution.py:394
  128.8 2.4 %finish.1 = f32[224,640]{1,0:T(8,128)} custom-call(f32[768,128]{1,0:T(8,128)S(1)} %bitcast.25, f32[224,128]{1,0:T(8,128)} %bitcast.43, f32[224,10]{1,0:T(8,128)S(1)} %get-tuple-element.28.refs_4_.refs_3_.refs_8_.refs_2_, f32[224,640]{1,0:T(8,128)S(1)} %local_grad.1.refs_4_.refs_3_), custom_call_target="tpu_custom_call" | custom-call | bytes 900000 | tf_op jit(solution)/shard_map/finish/pallas_call | solution.py:86
  131.2 0.0 collective-permute-done.8
  131.2 1.7 %collective-permute-done.7 = f32[56,2560]{1,0:T(8,128)S(1)} collective-permute-done((f32[56,2560]{1,0:T(8,128)}, f32[56,2560]{1,0:T(8,128)S(1)}, u32[]{:S(2)}, u32[]{:S(2)}) %collective-permute-start.7) | collective-permute-done | bytes 573472 | tf_op jit(solution)/shard_map/ppermute | solution.py:386
  133.0 0.9 add_add_fusion
  133.8 0.0 reduce-scatter.2.cloned.1.call-done
  133.9 17.2 %all_to_all.56 = f32[8,40,640]{2,1,0:T(8,128)S(1)} all-to-all(f32[8,40,640]{2,1,0:T(8,128)} %bitcast.44), channel_id=1, replica_groups={{0,1,64,65,128,129,192,193},{8,9,72,73,136,137,200,201},{16,17,80,81,14..., dimensions={0} | all-to-all | bytes 1638400 | tf_op jit(solution)/shard_map/all_to_all | solution.py:505
  151.1 0.8 sum_column.1
  (1 shorter events, 0.0 us)
Async XLA Ops:
  7.2 34.5 %collective-permute-start.1 = (f32[56,2560]{1,0:T(8,128)}, f32[56,2560]{1,0:T(8,128)S(1)}, u32[]{:S(2)}, u32[]{:S(2)}) collective-permute-start(f32[56,2560]{1,0:T(8,128)} %bitcast.29), channel_id=1, source_target_pairs={{0,6},{2,0},{4,2},{6,4},{1,7},{3,1},{5,3},{7,5},{8,14},{10,8},{12,... | collective-permute-start | bytes 1720328 | tf_op jit(solution)/shard_map/ppermute | solution.py:386
  13.5 33.0 %collective-permute-start = (f32[56,2560]{1,0:T(8,128)}, f32[56,2560]{1,0:T(8,128)S(1)}, u32[]{:S(2)}, u32[]{:S(2)}) collective-permute-start(f32[56,2560]{1,0:T(8,128)} %bitcast.30), channel_id=1, source_target_pairs={{0,2},{2,4},{4,6},{6,0},{1,3},{3,5},{5,7},{7,1},{8,10},{10,12},{12... | collective-permute-start | bytes 1720328 | tf_op jit(solution)/shard_map/ppermute | solution.py:386
  17.9 16.7 %all-to-all-start = ((f32[32,24,128]{2,1,0:T(8,128)}), f32[32,24,128]{2,1,0:T(8,128)S(1)}, u32[]{:S(2)}, u32[]{:S(2)}) async-start(f32[32,24,128]{2,1,0:T(8,128)} %bitcast.6), calls=%async_computation | async-start | bytes 786432 | tf_op jit(solution)/shard_map/all_to_all | solution.py:394
  25.6 0.7 copy-start.5
  26.2 21.0 %copy-start.7 = (f32[640]{0:T(1024)S(1)}, f32[640]{0:T(1024)}, u32[]{:S(2)}) copy-start(f32[640]{0:T(1024)} %param.15) | copy-start | bytes 7684
  35.8 0.8 copy-start.3
  36.6 14.2 %all-to-all-start.1 = ((f32[32,24,128]{2,1,0:T(8,128)}), f32[32,24,128]{2,1,0:T(8,128)S(1)}, u32[]{:S(2)}, u32[]{:S(2)}) async-start(f32[32,24,128]{2,1,0:T(8,128)} %bitcast.9), calls=%async_computation.1 | async-start | bytes 786432 | tf_op jit(solution)/shard_map/all_to_all | solution.py:394
  41.6 92.3 %reduce-scatter.2.cloned.1.call-start = ((), (), s32[]{:S(2)}) async-start(), calls=%async_computation.6 | async-start | bytes 4096000 | tf_op jit(solution)/shard_map/reduce_scatter | solution.py:475
  42.4 17.5 %collective-permute-start.3 = (f32[56,1280]{1,0:T(8,128)}, f32[56,1280]{1,0:T(8,128)}, u32[]{:S(2)}, u32[]{:S(2)}) collective-permute-start(f32[56,1280]{1,0:T(8,128)} %slice.9), channel_id=1, source_target_pairs={{0,6},{2,0},{4,2},{6,4},{1,7},{3,1},{5,3},{7,5},{8,14},{10,8},{12,... | collective-permute-start | bytes 860168 | tf_op jit(solution)/shard_map/ppermute | solution.py:386
  47.2 16.7 %collective-permute-start.2 = (f32[56,1280]{1,0:T(8,128)}, f32[56,1280]{1,0:T(8,128)}, u32[]{:S(2)}, u32[]{:S(2)}) collective-permute-start(f32[56,1280]{1,0:T(8,128)} %slice.8), channel_id=1, source_target_pairs={{0,2},{2,4},{4,6},{6,0},{1,3},{3,5},{5,7},{7,1},{8,10},{10,12},{12... | collective-permute-start | bytes 860168 | tf_op jit(solution)/shard_map/ppermute | solution.py:386
  50.8 13.2 %copy-start.2 = (f32[1,56,2560]{2,1,0:T(8,128)S(1)}, f32[1,56,2560]{2,1,0:T(8,128)}, u32[]{:S(2)}) copy-start(f32[1,56,2560]{2,1,0:T(8,128)} %param.17) | copy-start | bytes 1720324
  59.1 0.8 copy-start
  67.9 8.5 %collective-permute-start.4 = (f32[1920,256]{1,0:T(8,128)S(1)}, f32[1920,256]{1,0:T(8,128)S(1)}, u32[]{:S(2)}, u32[]{:S(2)}) collective-permute-start(f32[1920,256]{1,0:T(8,128)S(1)} %get-tuple-element.32), channel_id=1, source_target_pairs={{0,8},{8,0},{16,24},{24,16},{32,40},{40,32},{48,56},{56,48},{64,72... | collective-permute-start | bytes 5898248 | tf_op jit(solution)/shard_map/ppermute | solution.py:390
  81.8 11.8 %copy-start.6 = (f32[10]{0:T(128)S(1)}, f32[10]{0:T(128)}, u32[]{:S(2)}) copy-start(f32[10]{0:T(128)} %refs_5_.3) | copy-start | bytes 124
  81.9 17.4 %copy-start.1 = (f32[56,2560]{1,0:T(8,128)S(1)}, f32[56,2560]{1,0:T(8,128)}, u32[]{:S(2)}) copy-start(f32[56,2560]{1,0:T(8,128)} %copy-done) | copy-start | bytes 1720324
  81.9 17.4 %collective-permute-start.5 = (f32[56,1280]{1,0:T(8,128)}, f32[56,1280]{1,0:T(8,128)}, u32[]{:S(2)}, u32[]{:S(2)}) collective-permute-start(f32[56,1280]{1,0:T(8,128)} %get-tuple-element.42), channel_id=1, source_target_pairs={{0,2},{2,4},{4,6},{6,0},{1,3},{3,5},{5,7},{7,1},{8,10},{10,12},{12... | collective-permute-start | bytes 860168 | tf_op jit(solution)/shard_map/ppermute | solution.py:386
  82.0 17.3 %collective-permute-start.6 = (f32[56,1280]{1,0:T(8,128)}, f32[56,1280]{1,0:T(8,128)}, u32[]{:S(2)}, u32[]{:S(2)}) collective-permute-start(f32[56,1280]{1,0:T(8,128)} %get-tuple-element.43), channel_id=1, source_target_pairs={{0,6},{2,0},{4,2},{6,4},{1,7},{3,1},{5,3},{7,5},{8,14},{10,8},{12,... | collective-permute-start | bytes 860168 | tf_op jit(solution)/shard_map/ppermute | solution.py:386
  86.1 21.1 %all-to-all-start.2 = ((f32[32,24,128]{2,1,0:T(8,128)}), f32[32,24,128]{2,1,0:T(8,128)S(1)}, u32[]{:S(2)}, u32[]{:S(2)}) async-start(f32[32,24,128]{2,1,0:T(8,128)} %bitcast.12), calls=%async_computation.3 | async-start | bytes 786432 | tf_op jit(solution)/shard_map/all_to_all | solution.py:394
  101.7 29.6 %collective-permute-start.8 = (f32[56,2560]{1,0:T(8,128)}, f32[56,2560]{1,0:T(8,128)S(1)}, u32[]{:S(2)}, u32[]{:S(2)}) collective-permute-start(f32[56,2560]{1,0:T(8,128)} %get-tuple-element.46), channel_id=1, source_target_pairs={{0,6},{2,0},{4,2},{6,4},{1,7},{3,1},{5,3},{7,5},{8,14},{10,8},{12,... | collective-permute-start | bytes 1720328 | tf_op jit(solution)/shard_map/ppermute | solution.py:386
  106.0 27.0 %collective-permute-start.7 = (f32[56,2560]{1,0:T(8,128)}, f32[56,2560]{1,0:T(8,128)S(1)}, u32[]{:S(2)}, u32[]{:S(2)}) collective-permute-start(f32[56,2560]{1,0:T(8,128)} %get-tuple-element.44.refs_2_), channel_id=1, source_target_pairs={{0,2},{2,4},{4,6},{6,0},{1,3},{3,5},{5,7},{7,1},{8,10},{10,12},{12... | collective-permute-start | bytes 1720328 | tf_op jit(solution)/shard_map/ppermute | solution.py:386
  107.2 1.0 copy-start.4
Sparse Core Ops, SparseCore 0:
  82.0 46.2 reduce-scatter.1

commit v4 on v3

--- a/solution.py
+++ b/solution.py
@@ -54,7 +54,7 @@
             self.started.add(j)
 
 
-def call(body, outs, ins, name, us, scratch=(), smem=(), tiled=None, after=(), io=False, fixed=(), vmem=40):
+def call(body, outs, ins, name, us, scratch=(), smem=(), tiled=None, after=(), io=False, fixed=(), far=(), vmem=40):
     outs = [o if isinstance(o, jax.ShapeDtypeStruct) else jax.ShapeDtypeStruct(o, F32) for o in outs]
     n, m = len(ins), len(outs)
     big = [i for i in range(n) if i not in smem]
@@ -85,7 +85,7 @@
 
     return pl.pallas_call(
         run,
-        out_shape=outs,
+        out_shape=[pltpu.HBM(o.shape, o.dtype) if j in far else o for j, o in enumerate(outs)],
         in_specs=[
             *[pl.BlockSpec(memory_space=pltpu.SMEM if i in smem else pltpu.HBM) for i in range(n)],
             *[pl.BlockSpec(memory_space=pltpu.HBM)] * len(after),
@@ -133,7 +133,7 @@
     row = lax.broadcasted_iota(jnp.int32, (length, length), 0)
     col = lax.broadcasted_iota(jnp.int32, (length, length), 1)
     upto = jnp.where(row >= col, 1.0, 0.0).astype(F32)
-    ld = ld_ref[...]
+    ld = ld_ref[:, 0, :]
     cum = lax.dot_general(ld, upto, (NT, ((), ())), precision=HIGHEST, preferred_element_type=F32)
     cum_t = lax.dot_general(upto, ld, (NT, ((), ())), precision=HIGHEST, preferred_element_type=F32)
     cum_ref[...] = cum
@@ -395,7 +395,7 @@
 
 
 def per_device(head_input, gate_input, log_decay, in_b, in_c, skip, norm_gain, w_out, d_out):
-    x, gate, ld, b_mat, c_mat, d_own = head_input[0], gate_input[0], log_decay[0], in_b[0], in_c[0], d_out[0]
+    x, gate, ld, b_mat, c_mat, d_own = head_input[0], gate_input[0], log_decay.transpose(1, 0, 2), in_b[0], in_c[0], d_out[0]
     length, width = x.shape
     heads, state = ld.shape[0], b_mat.shape[1]
     model = w_out.shape[1]
@@ -439,14 +439,14 @@
         functools.partial(scan_forward, ranks, pitch, used, width),
         [pieces, pieces],
         [recv],
-        after=[y_local], name="scan_forward", us=0.3,
+        after=[y_local], far=(0, 1), name="scan_forward", us=0.3,
     )
     recv = exchange(send, "ctx")
     gated, normed, scale, part_left, part_right, part_next, part_prev, part_own = call(
         functools.partial(gate_out, ring, ranks, pitch),
         [(length, width)] * 2 + [(length, LANES)] + [(block, half)] * 2 + [(block, model)] * 3,
         [pos, recv, c_mat, cum_t, y_local, gate, gain, w_out],
-        smem=(0,), tiled=7, fixed=(2, 5, 7), io=True,
+        smem=(0,), tiled=7, fixed=(2, 5, 7), io=True, far=(3, 4, 5, 6, 7),
         scratch=[pltpu.VMEM((state, width), F32)] + [pltpu.VMEM((length, width), BF16)] * 2,
         name="gate_out", us=7,
     )
@@ -481,7 +481,7 @@
         smem=(5,), fixed=(1, 2), name="local_grad", us=0.3,
     )
     part_next, part_prev = call(
-        pass_on, [(block, model)] * 2, [part_next, part_prev, up_far, down_far],
+        pass_on, [(block, model)] * 2, [part_next, part_prev, up_far, down_far], fixed=(0, 1),
         after=[dx_local], name="pass_on", us=0.3,
     )
     up, low = shifted(part_next, "tp", 1), shifted(part_prev, "tp", -1)
@@ -489,6 +489,7 @@
         functools.partial(scan_backward, ranks, pitch),
         [pieces],
         [recv, decays],
+        fixed=(1,),
         after=[part_next], name="scan_backward", us=0.3,
     )
     recv = exchange(send, "ctx")
@@ -500,7 +501,7 @@
         scratch=[pltpu.VMEM((state, width), F32)], name="finish", us=0.3,
     )
     out = part_own + up + low
-    grad_w, _, out = lax.optimization_barrier((grad_w, dx, out))
+    grad_w, *_ = lax.optimization_barrier((grad_w, dx, up, low))
     columns = [[seqs * i + p for i in line for p in range(seqs)] for line in lines[1]]
     grad_w = lax.all_to_all(grad_w, ("ctx", "dp"), 0, 0, tiled=True, axis_index_groups=columns)
     (share,) = call(

time: 159 us -> 156 us (0.981); the launches traced: 159 us -> 154 us
  blocking collectives: 37.2 us -> 19 us
  waiting for transfers between devices: 17.7 us -> 28.7 us
  starting transfers between devices: 39.5 us -> 44.9 us
  local copies, waits for them, and re-layouts: 6.01 us -> 1.7 us
    all_to_all x1 -> x0, blocking collectives: 17.2 us -> none  [per_device(): lax.all_to_all(grad_w, ('ctx', 'dp'), 0, 0, tiled=True, axis_index_groups...]
    all_to_all x0 -> x1, waiting for transfers between devices: none -> 9.79 us  [per_device(): lax.all_to_all(grad_w, ('ctx', 'dp'), 0, 0, tiled=True, axis_index_groups...]
    all_to_all x0 -> x1, starting transfers between devices: none -> 6.65 us  [per_device(): lax.all_to_all(grad_w, ('ctx', 'dp'), 0, 0, tiled=True, axis_index_groups...]
    all_to_all x3, waiting for transfers between devices: 9.6 us -> 13.2 us  [exchange(): return lax.all_to_all(value, axis, 0, 0, tiled=True)]
    unnamed x17 -> x14, local copies, waits for them, and re-layouts: 4.53 us -> 1.66 us
    ppermute x8, waiting for transfers between devices: 8.1 us -> 5.66 us  [shifted(): lax.ppermute(value, axis, [(i, (i + step) % count) for i in range(count)])]
    broadcast_in_dim x0 -> x1, other arithmetic: none -> 2.19 us  [per_device(): return (out[None], dx[None], share)]
  transfers between devices with their start and end apart: 13 -> 14, of which waited for: 6 -> 7; matrix products, arithmetic and copies ran while one was open for 2% -> 2% of each run, Pallas kernels for 21% -> 22%
where the time goes in v4:
time: 156 us; the launch traced here: 154 us
  starting transfers between devices  44.9 us (29%)
  Pallas kernels  43 us (28%)
  waiting for transfers between devices  28.7 us (18%)
  blocking collectives  19 us (12%)
  between operations  14.3 us (9%)
  other arithmetic  2.27 us (1%)
  local copies, waits for them, and re-layouts  1.7 us (1%)
    pallas_call x12, Pallas kernels, call(): pl.pallas_call(run, out_shape=[pltpu.HBM(o.shape, o.dtype) if j in far el...  43 us
    all_to_all x3, starting transfers between devices, exchange(): return lax.all_to_all(value, axis, 0, 0, tiled=True)  20.1 us
    all_to_all x1, blocking collectives, exchange(): return lax.all_to_all(value, axis, 0, 0, tiled=True)  19 us
    ppermute x8, starting transfers between devices, shifted(): lax.ppermute(value, axis, [(i, (i + step) % count) for i in range(count)])  17.8 us
    all_to_all x3, waiting for transfers between devices, exchange(): return lax.all_to_all(value, axis, 0, 0, tiled=True)  13.2 us
    all_to_all x1, waiting for transfers between devices, per_device(): lax.all_to_all(grad_w, ('ctx', 'dp'), 0, 0, tiled=True, axis_index_groups...  9.79 us
    all_to_all x1, starting transfers between devices, per_device(): lax.all_to_all(grad_w, ('ctx', 'dp'), 0, 0, tiled=True, axis_index_groups...  6.65 us
    ppermute x8, waiting for transfers between devices, shifted(): lax.ppermute(value, axis, [(i, (i + step) % count) for i in range(count)])  5.66 us
  transfers between devices with their start and end apart: 14, of which 7 were waited for; matrix products, arithmetic and copies ran while one was open for 2% of the time, Pallas kernels for 22%

profile of v4, /device:TPU:2, one launch (start us, length us, event | category | flops | bytes accessed | tf_op | source)
XLA Modules:
  0.0 153.8 jit_solution(17907332481127408446)
XLA Ops:
  7.2 6.4 %collective-permute-start.3 = (f32[56,2560]{1,0:T(8,128)}, f32[56,2560]{1,0:T(8,128)S(1)}, u32[]{:S(2)}, u32[]{:S(2)}) collective-permute-start(f32[56,2560]{1,0:T(8,128)} %bitcast.28), channel_id=1, source_target_pairs={{0,6},{2,0},{4,2},{6,4},{1,7},{3,1},{5,3},{7,5},{8,14},{10,8},{12,... | collective-permute-start | bytes 1720328 | tf_op jit(solution)/shard_map/ppermute | solution.py:386
  13.5 0.0 collective-permute-start.2
  13.5 3.1 %block_state.1 = (f32[768,128]{1,0:T(8,128)}, f32[10,224]{1,0:T(8,128)S(1)}, f32[224,10]{1,0:T(8,128)S(1)}) custom-call(f32[10,1,224]{2,1,0:T(1,128)} %bitcast.46, f32[224,640]{1,0:T(8,128)} %bitcast.33, f32[224,128]{1,0:T(8,128)} %bitcast.39), custom_call_target="tpu_custom_call" | custom-call | bytes 900000 | tf_op jit(solution)/shard_map/block_state/pallas_call | solution.py:86
  16.6 7.6 %all-to-all-start = ((f32[32,24,128]{2,1,0:T(8,128)}), f32[32,24,128]{2,1,0:T(8,128)S(1)}, u32[]{:S(2)}, u32[]{:S(2)}) async-start(f32[32,24,128]{2,1,0:T(8,128)} %bitcast.6), calls=%async_computation | async-start | bytes 786432 | tf_op jit(solution)/shard_map/all_to_all | solution.py:394
  24.3 0.0 copy-start.1
  24.3 0.6 copy-done.1
  24.9 0.0 copy-start.4
  24.9 3.4 %local_output.1.refs_1_.refs_4_ = f32[224,640]{1,0:T(8,128)S(1)} custom-call(f32[224,640]{1,0:T(8,128)} %bitcast.34, f32[224,128]{1,0:T(8,128)} %bitcast.40, f32[224,128]{1,0:T(8,128)} %bitcast.35, f32[10,224]{1,0:T(8,128)S(1)} %get-tuple-element.26.refs_3_, f32[224,10]{1,0:T(8,128)S(1)} %get-tuple-element.27.refs_4_.refs_3_.refs_8_.refs_2_, f32[10]{0:T(128)S(1)} %copy-done.1), custom_call_target="tpu_custom_call" | custom-call | bytes 900000 | tf_op jit(solution)/shard_map/local_output/pallas_call | solution.py:86
  28.3 5.0 %all-to-all-done = f32[32,24,128]{2,1,0:T(8,128)S(1)} async-done(((f32[32,24,128]{2,1,0:T(8,128)}), f32[32,24,128]{2,1,0:T(8,128)S(1)}, u32[]{:S(2)}, u32[]{:S(2)}) %all-to-all-start) | async-done | bytes 393248 | tf_op jit(solution)/shard_map/all_to_all | solution.py:394
  33.3 1.3 scan_forward.1
  34.6 5.0 %all-to-all-start.1 = ((f32[32,24,128]{2,1,0:T(8,128)}), f32[32,24,128]{2,1,0:T(8,128)S(1)}, u32[]{:S(2)}, u32[]{:S(2)}) async-start(f32[32,24,128]{2,1,0:T(8,128)} %bitcast.45), calls=%async_computation.1 | async-start | bytes 786432 | tf_op jit(solution)/shard_map/all_to_all | solution.py:394
  39.7 0.0 reduce-scatter.2.cloned.1.call-start
  39.7 0.0 collective-permute-done.3.refs_3_
  39.7 4.2 %collective-permute-start.5 = (f32[56,1280]{1,0:T(8,128)S(1)}, f32[56,1280]{1,0:T(8,128)S(1)}, u32[]{:S(2)}, u32[]{:S(2)}) collective-permute-start(f32[56,1280]{1,0:T(8,128)S(1)} %slice.9), channel_id=1, source_target_pairs={{0,6},{2,0},{4,2},{6,4},{1,7},{3,1},{5,3},{7,5},{8,14},{10,8},{12,... | collective-permute-start | bytes 860168 | tf_op jit(solution)/shard_map/ppermute | solution.py:386
  43.9 0.0 collective-permute-done.2.refs_2_
  44.0 0.1 collective-permute-start.4
  44.1 0.0 copy-done.4
  44.1 0.1 pad_add_fusion.refs_0_
  44.2 4.7 %all-to-all-done.1 = f32[32,24,128]{2,1,0:T(8,128)S(1)} async-done(((f32[32,24,128]{2,1,0:T(8,128)}), f32[32,24,128]{2,1,0:T(8,128)S(1)}, u32[]{:S(2)}, u32[]{:S(2)}) %all-to-all-start.1) | async-done | bytes 393248 | tf_op jit(solution)/shard_map/all_to_all | solution.py:394
  48.8 0.0 copy-start
  48.9 8.8 %gate_out.1 = (f32[224,640]{1,0:T(8,128)S(1)}, f32[224,640]{1,0:T(8,128)S(1)}, f32[224,128]{1,0:T(8,128)S(1)}, f32[56,1280]{1,0:T(8,128)}, f32[56,1280]{1,0:T(8,...) custom-call(s32[3]{0:T(128)S(1)} %pad_add_fusion.refs_0_, f32[768,128]{1,0:T(8,128)S(1)} %bitcast.23, ...), custom_call_target="tpu_custom_call" | custom-call | bytes 21000000 | tf_op jit(solution)/shard_map/gate_out/pallas_call | solution.py:86
  57.7 0.0 collective-permute-done.5.refs_5_
  57.7 2.7 %collective-permute-done.4.refs_4_ = f32[56,1280]{1,0:T(8,128)S(1)} collective-permute-done((f32[56,1280]{1,0:T(8,128)S(1)}, f32[56,1280]{1,0:T(8,128)S(1)}, u32[]{:S(2)}, u32[]{:S(2)}) %collective-permute-start.4) | collective-permute-done | bytes 286752 | tf_op jit(solution)/shard_map/ppermute | solution.py:386
  60.5 0.0 copy-done
  60.5 3.1 %turn.1 = (f32[1280,256]{1,0:T(8,128)S(1)}, f32[1920,256]{1,0:T(8,128)S(1)}, bf16[2560,256]{1,0:T(8,128)(2,1)S(1)}, bf16[2560,256]{1,0:T(8,128)(2,1)S(1)}) custom-call(s32[3]{0:T(128)S(1)} %pad_add_fusion.refs_0_, f32[56,2560]{1,0:T(8,128)S(1)} %bitcast.30, f32[56,2560]{1,0:T(8,128)S(1)} %collective-permute-done.2.refs_2_, ...), custom_call_target="tpu_custom_call" | custom-call | bytes 900000 | tf_op jit(solution)/shard_map/turn/pallas_call | solution.py:86
  63.6 0.3 collective-permute-start.8
  63.9 8.2 %norm_grad.1 = (f32[768,128]{1,0:T(8,128)}, f32[224,640]{1,0:T(8,128)S(1)}) custom-call(bf16[2560,256]{1,0:T(8,128)(2,1)S(1)} %get-tuple-element.35.refs_0_, bf16[2560,256]{1,0:T(8,128)(2,1)S(1)} %get-tuple-element.36.refs_1_, f32[640,2560]{1,0:T(8,128)} %refs_2_.1, f32[224,640]{1,0:T(8,128)S(1)} %get-tuple-element.37.refs_3_, ...), custom_call_target="tpu_custom_call" | custom-call | bytes 900000 | tf_op jit(solution)/shard_map/norm_grad/pallas_call | solution.py:86
  72.0 0.0 collective-permute-done.8.refs_1_
  72.0 5.4 %weight_grad.1 = f32[1280,640]{1,0:T(8,128)} custom-call(f32[1280,256]{1,0:T(8,128)S(1)} %get-tuple-element.44.refs_0_, f32[1920,256]{1,0:T(8,128)S(1)} %collective-permute-done.8.refs_1_, f32[224,640]{1,0:T(8,128)S(1)} %get-tuple-element.34.refs_6_.refs_2_, f32[224,640]{1,0:T(8,128)S(1)} %get-tuple-element.39.refs_0_.refs_3_), custom_call_target="tpu_custom_call" | custom-call | bytes 900000 | tf_op jit(solution)/shard_map/weight_grad/pallas_call | solution.py:86
  77.5 0.0 copy-start.6
  77.5 0.0 copy-start.5
  77.5 0.0 copy-start.2
  77.5 0.0 reduce-scatter.2.cloned.1.call-update
  77.5 0.9 copy-done.6
  78.4 0.0 collective-permute-start
  78.4 0.1 copy-done.5
  78.5 4.1 %collective-permute-start.1 = (f32[56,1280]{1,0:T(8,128)S(1)}, f32[56,1280]{1,0:T(8,128)S(1)}, u32[]{:S(2)}, u32[]{:S(2)}) collective-permute-start(f32[56,1280]{1,0:T(8,128)S(1)} %copy-done.5), channel_id=1, source_target_pairs={{0,6},{2,0},{4,2},{6,4},{1,7},{3,1},{5,3},{7,5},{8,14},{10,8},{12,... | collective-permute-start | bytes 860168 | tf_op jit(solution)/shard_map/ppermute | solution.py:386
  82.6 7.5 %all-to-all-start.2 = ((f32[32,24,128]{2,1,0:T(8,128)}), f32[32,24,128]{2,1,0:T(8,128)S(1)}, u32[]{:S(2)}, u32[]{:S(2)}) async-start(f32[32,24,128]{2,1,0:T(8,128)} %bitcast.14), calls=%async_computation.2 | async-start | bytes 786432 | tf_op jit(solution)/shard_map/all_to_all | solution.py:394
  90.0 0.0 copy-done.2
  90.1 3.4 %local_grad.1.refs_4_.refs_3_ = f32[224,640]{1,0:T(8,128)S(1)} custom-call(f32[224,640]{1,0:T(8,128)S(1)} %get-tuple-element.39.refs_0_.refs_3_, f32[224,128]{1,0:T(8,128)} %bitcast.41, f32[224,128]{1,0:T(8,128)} %bitcast.38, f32[10,224]{1,0:T(8,128)S(1)} %get-tuple-element.26.refs_3_, f32[224,10]{1,0:T(8,128)S(1)} %get-tuple-element.27.refs_4_.refs_3_.refs_8_.refs_2_, ...), custom_call_target="tpu_custom_call" | custom-call | bytes 900000 | tf_op jit(solution)/shard_map/local_grad/pallas_call | solution.py:86
  93.5 2.0 %collective-permute-done.refs_2_ = f32[56,1280]{1,0:T(8,128)S(1)} collective-permute-done((f32[56,1280]{1,0:T(8,128)S(1)}, f32[56,1280]{1,0:T(8,128)S(1)}, u32[]{:S(2)}, u32[]{:S(2)}) %collective-permute-start) | collective-permute-done | bytes 286752 | tf_op jit(solution)/shard_map/ppermute | solution.py:386
  95.4 0.0 collective-permute-done.1.refs_3_
  95.4 1.6 %pass_on.1 = (f32[56,2560]{1,0:T(8,128)S(1)}, f32[56,2560]{1,0:T(8,128)S(1)}) custom-call(f32[56,2560]{1,0:T(8,128)} %get-tuple-element.30.refs_0_, f32[56,2560]{1,0:T(8,128)} %get-tuple-element.31.refs_1_, f32[56,1280]{1,0:T(8,128)S(1)} %collective-permute-done.refs_2_, f32[56,1280]{1,0:T(8,128)S(1)} %collective-permute-done.1.refs_3_, ...), custom_call_target="tpu_custom_call" | custom-call | bytes 900000 | tf_op jit(solution)/shard_map/pass_on/pallas_call | solution.py:86
  97.0 3.1 %collective-permute-start.7 = (f32[56,2560]{1,0:T(8,128)S(1)}, f32[56,2560]{1,0:T(8,128)}, u32[]{:S(2)}, u32[]{:S(2)}) collective-permute-start(f32[56,2560]{1,0:T(8,128)S(1)} %get-tuple-element.41), channel_id=1, source_target_pairs={{0,6},{2,0},{4,2},{6,4},{1,7},{3,1},{5,3},{7,5},{8,14},{10,8},{12,... | collective-permute-start | bytes 1720328 | tf_op jit(solution)/shard_map/ppermute | solution.py:386
  100.1 0.0 collective-permute-start.6
  100.1 3.5 %all-to-all-done.2 = f32[32,24,128]{2,1,0:T(8,128)S(1)} async-done(((f32[32,24,128]{2,1,0:T(8,128)}), f32[32,24,128]{2,1,0:T(8,128)S(1)}, u32[]{:S(2)}, u32[]{:S(2)}) %all-to-all-start.2) | async-done | bytes 393248 | tf_op jit(solution)/shard_map/all_to_all | solution.py:394
  103.6 1.5 scan_backward.1
  105.1 0.0 copy-start.3
  105.1 19.0 %all_to_all.55 = f32[32,24,128]{2,1,0:T(8,128)S(1)} all-to-all(f32[32,24,128]{2,1,0:T(8,128)S(1)} %bitcast.27), channel_id=1, replica_groups=mesh['ctx'=32,'tp'=4,'dp'=2] {'ctx'}, dimensions={0} | all-to-all | bytes 786432 | tf_op jit(solution)/shard_map/all_to_all | solution.py:394
  124.1 2.4 %finish.1 = f32[224,640]{1,0:T(8,128)} custom-call(f32[768,128]{1,0:T(8,128)S(1)} %bitcast.24, f32[224,128]{1,0:T(8,128)} %bitcast.42, f32[224,10]{1,0:T(8,128)S(1)} %get-tuple-element.27.refs_4_.refs_3_.refs_8_.refs_2_, f32[224,640]{1,0:T(8,128)S(1)} %local_grad.1.refs_4_.refs_3_), custom_call_target="tpu_custom_call" | custom-call | bytes 900000 | tf_op jit(solution)/shard_map/finish/pallas_call | solution.py:86
  126.5 0.0 collective-permute-done.7
  126.6 0.9 collective-permute-done.6
  127.5 0.0 reduce-scatter.2.cloned.1.call-done
  127.5 6.6 %all-to-all-start.4 = ((f32[8,40,640]{2,1,0:T(8,128)}), f32[8,40,640]{2,1,0:T(8,128)S(1)}, u32[]{:S(2)}, u32[]{:S(2)}) async-start(f32[8,40,640]{2,1,0:T(8,128)} %bitcast.43), calls=%async_computation.5 | async-start | bytes 1638400 | tf_op jit(solution)/shard_map/all_to_all | solution.py:506
  134.1 0.0 copy-done.3
  134.1 2.2 %add_bitcast_fusion = f32[1,56,2560]{2,1,0:T(8,128)} fusion(f32[56,2560]{1,0:T(8,128)} %collective-permute-done.7, f32[56,2560]{1,0:T(8,128)S(1)} %copy-done.3, f32[56,2560]{1,0:T(8,128)} %collective-permute-done.6), kind=kLoop, calls=%fused_computation | loop fusion | flops 286720 | bytes 2293760 | tf_op jit(solution)/shard_map/broadcast_in_dim | solution.py:511
  136.3 9.8 %all-to-all-done.4 = f32[8,40,640]{2,1,0:T(8,128)S(1)} async-done(((f32[8,40,640]{2,1,0:T(8,128)}), f32[8,40,640]{2,1,0:T(8,128)S(1)}, u32[]{:S(2)}, u32[]{:S(2)}) %all-to-all-start.4) | async-done | bytes 819232 | tf_op jit(solution)/shard_map/all_to_all | solution.py:506
  146.1 0.8 sum_column.1
  (3 shorter events, 0.0 us)
Async XLA Ops:
  7.2 32.5 %collective-permute-start.3 = (f32[56,2560]{1,0:T(8,128)}, f32[56,2560]{1,0:T(8,128)S(1)}, u32[]{:S(2)}, u32[]{:S(2)}) collective-permute-start(f32[56,2560]{1,0:T(8,128)} %bitcast.28), channel_id=1, source_target_pairs={{0,6},{2,0},{4,2},{6,4},{1,7},{3,1},{5,3},{7,5},{8,14},{10,8},{12,... | collective-permute-start | bytes 1720328 | tf_op jit(solution)/shard_map/ppermute | solution.py:386
  13.5 30.4 %collective-permute-start.2 = (f32[56,2560]{1,0:T(8,128)}, f32[56,2560]{1,0:T(8,128)S(1)}, u32[]{:S(2)}, u32[]{:S(2)}) collective-permute-start(f32[56,2560]{1,0:T(8,128)} %bitcast.29), channel_id=1, source_target_pairs={{0,2},{2,4},{4,6},{6,0},{1,3},{3,5},{5,7},{7,1},{8,10},{10,12},{12... | collective-permute-start | bytes 1720328 | tf_op jit(solution)/shard_map/ppermute | solution.py:386
  16.6 16.7 %all-to-all-start = ((f32[32,24,128]{2,1,0:T(8,128)}), f32[32,24,128]{2,1,0:T(8,128)S(1)}, u32[]{:S(2)}, u32[]{:S(2)}) async-start(f32[32,24,128]{2,1,0:T(8,128)} %bitcast.6), calls=%async_computation | async-start | bytes 786432 | tf_op jit(solution)/shard_map/all_to_all | solution.py:394
  24.3 0.7 copy-start.1
  24.9 19.2 %copy-start.4 = (f32[640]{0:T(1024)S(1)}, f32[640]{0:T(1024)}, u32[]{:S(2)}) copy-start(f32[640]{0:T(1024)} %param.15) | copy-start | bytes 7684
  34.6 14.2 %all-to-all-start.1 = ((f32[32,24,128]{2,1,0:T(8,128)}), f32[32,24,128]{2,1,0:T(8,128)S(1)}, u32[]{:S(2)}, u32[]{:S(2)}) async-start(f32[32,24,128]{2,1,0:T(8,128)} %bitcast.45), calls=%async_computation.1 | async-start | bytes 786432 | tf_op jit(solution)/shard_map/all_to_all | solution.py:394
  39.7 87.8 %reduce-scatter.2.cloned.1.call-start = ((), (), s32[]{:S(2)}) async-start(), calls=%async_computation.6 | async-start | bytes 4096000 | tf_op jit(solution)/shard_map/reduce_scatter | solution.py:475
  39.7 18.0 %collective-permute-start.5 = (f32[56,1280]{1,0:T(8,128)S(1)}, f32[56,1280]{1,0:T(8,128)S(1)}, u32[]{:S(2)}, u32[]{:S(2)}) collective-permute-start(f32[56,1280]{1,0:T(8,128)S(1)} %slice.9), channel_id=1, source_target_pairs={{0,6},{2,0},{4,2},{6,4},{1,7},{3,1},{5,3},{7,5},{8,14},{10,8},{12,... | collective-permute-start | bytes 860168 | tf_op jit(solution)/shard_map/ppermute | solution.py:386
  44.0 16.5 %collective-permute-start.4 = (f32[56,1280]{1,0:T(8,128)S(1)}, f32[56,1280]{1,0:T(8,128)S(1)}, u32[]{:S(2)}, u32[]{:S(2)}) collective-permute-start(f32[56,1280]{1,0:T(8,128)S(1)} %slice.8), channel_id=1, source_target_pairs={{0,2},{2,4},{4,6},{6,0},{1,3},{3,5},{5,7},{7,1},{8,10},{10,12},{12... | collective-permute-start | bytes 860168 | tf_op jit(solution)/shard_map/ppermute | solution.py:386
  48.8 11.6 %copy-start = (f32[1,56,2560]{2,1,0:T(8,128)S(1)}, f32[1,56,2560]{2,1,0:T(8,128)}, u32[]{:S(2)}) copy-start(f32[1,56,2560]{2,1,0:T(8,128)} %param.17) | copy-start | bytes 1720324
  63.6 8.4 %collective-permute-start.8 = (f32[1920,256]{1,0:T(8,128)S(1)}, f32[1920,256]{1,0:T(8,128)S(1)}, u32[]{:S(2)}, u32[]{:S(2)}) collective-permute-start(f32[1920,256]{1,0:T(8,128)S(1)} %get-tuple-element.45), channel_id=1, source_target_pairs={{0,8},{8,0},{16,24},{24,16},{32,40},{40,32},{48,56},{56,48},{64,72... | collective-permute-start | bytes 5898248 | tf_op jit(solution)/shard_map/ppermute | solution.py:390
  77.5 1.0 copy-start.6
  77.5 1.0 copy-start.5
  77.5 12.6 %copy-start.2 = (f32[10]{0:T(128)S(1)}, f32[10]{0:T(128)}, u32[]{:S(2)}) copy-start(f32[10]{0:T(128)} %refs_5_.3) | copy-start | bytes 124
  78.4 17.0 %collective-permute-start = (f32[56,1280]{1,0:T(8,128)S(1)}, f32[56,1280]{1,0:T(8,128)S(1)}, u32[]{:S(2)}, u32[]{:S(2)}) collective-permute-start(f32[56,1280]{1,0:T(8,128)S(1)} %copy-done.6), channel_id=1, source_target_pairs={{0,2},{2,4},{4,6},{6,0},{1,3},{3,5},{5,7},{7,1},{8,10},{10,12},{12... | collective-permute-start | bytes 860168 | tf_op jit(solution)/shard_map/ppermute | solution.py:386
  78.5 16.9 %collective-permute-start.1 = (f32[56,1280]{1,0:T(8,128)S(1)}, f32[56,1280]{1,0:T(8,128)S(1)}, u32[]{:S(2)}, u32[]{:S(2)}) collective-permute-start(f32[56,1280]{1,0:T(8,128)S(1)} %copy-done.5), channel_id=1, source_target_pairs={{0,6},{2,0},{4,2},{6,4},{1,7},{3,1},{5,3},{7,5},{8,14},{10,8},{12,... | collective-permute-start | bytes 860168 | tf_op jit(solution)/shard_map/ppermute | solution.py:386
  82.6 21.1 %all-to-all-start.2 = ((f32[32,24,128]{2,1,0:T(8,128)}), f32[32,24,128]{2,1,0:T(8,128)S(1)}, u32[]{:S(2)}, u32[]{:S(2)}) async-start(f32[32,24,128]{2,1,0:T(8,128)} %bitcast.14), calls=%async_computation.2 | async-start | bytes 786432 | tf_op jit(solution)/shard_map/all_to_all | solution.py:394
  97.0 29.5 %collective-permute-start.7 = (f32[56,2560]{1,0:T(8,128)S(1)}, f32[56,2560]{1,0:T(8,128)}, u32[]{:S(2)}, u32[]{:S(2)}) collective-permute-start(f32[56,2560]{1,0:T(8,128)S(1)} %get-tuple-element.41), channel_id=1, source_target_pairs={{0,6},{2,0},{4,2},{6,4},{1,7},{3,1},{5,3},{7,5},{8,14},{10,8},{12,... | collective-permute-start | bytes 1720328 | tf_op jit(solution)/shard_map/ppermute | solution.py:386
  100.1 27.4 %collective-permute-start.6 = (f32[56,2560]{1,0:T(8,128)S(1)}, f32[56,2560]{1,0:T(8,128)}, u32[]{:S(2)}, u32[]{:S(2)}) collective-permute-start(f32[56,2560]{1,0:T(8,128)S(1)} %get-tuple-element.40.refs_2_), channel_id=1, source_target_pairs={{0,2},{2,4},{4,6},{6,0},{1,3},{3,5},{5,7},{7,1},{8,10},{10,12},{12... | collective-permute-start | bytes 1720328 | tf_op jit(solution)/shard_map/ppermute | solution.py:386
  105.1 29.0 %copy-start.3 = (f32[56,2560]{1,0:T(8,128)S(1)}, f32[56,2560]{1,0:T(8,128)}, u32[]{:S(2)}) copy-start(f32[56,2560]{1,0:T(8,128)} %get-tuple-element.29) | copy-start | bytes 1720324
  127.5 18.6 %all-to-all-start.4 = ((f32[8,40,640]{2,1,0:T(8,128)}), f32[8,40,640]{2,1,0:T(8,128)S(1)}, u32[]{:S(2)}, u32[]{:S(2)}) async-start(f32[8,40,640]{2,1,0:T(8,128)} %bitcast.43), calls=%async_computation.5 | async-start | bytes 1638400 | tf_op jit(solution)/shard_map/all_to_all | solution.py:506
Sparse Core Ops, SparseCore 0:
  77.6 46.2 reduce-scatter.1

commit v5 on v2

--- a/solution.py
+++ b/solution.py
@@ -54,7 +54,7 @@
             self.started.add(j)
 
 
-def call(body, outs, ins, name, us, scratch=(), smem=(), tiled=None, after=(), io=False, fixed=(), vmem=40):
+def call(body, outs, ins, name, us, scratch=(), smem=(), tiled=None, after=(), io=False, fixed=(), far=(), vmem=40):
     outs = [o if isinstance(o, jax.ShapeDtypeStruct) else jax.ShapeDtypeStruct(o, F32) for o in outs]
     n, m = len(ins), len(outs)
     big = [i for i in range(n) if i not in smem]
@@ -85,7 +85,7 @@
 
     return pl.pallas_call(
         run,
-        out_shape=outs,
+        out_shape=[pltpu.HBM(o.shape, o.dtype) if j in far else o for j, o in enumerate(outs)],
         in_specs=[
             *[pl.BlockSpec(memory_space=pltpu.SMEM if i in smem else pltpu.HBM) for i in range(n)],
             *[pl.BlockSpec(memory_space=pltpu.HBM)] * len(after),
@@ -133,7 +133,7 @@
     row = lax.broadcasted_iota(jnp.int32, (length, length), 0)
     col = lax.broadcasted_iota(jnp.int32, (length, length), 1)
     upto = jnp.where(row >= col, 1.0, 0.0).astype(F32)
-    ld = ld_ref[...]
+    ld = ld_ref[:, 0, :]
     cum = lax.dot_general(ld, upto, (NT, ((), ())), precision=HIGHEST, preferred_element_type=F32)
     cum_t = lax.dot_general(upto, ld, (NT, ((), ())), precision=HIGHEST, preferred_element_type=F32)
     cum_ref[...] = cum
@@ -397,7 +397,7 @@
 
 
 def per_device(head_input, gate_input, log_decay, in_b, in_c, skip, norm_gain, w_out, d_out):
-    x, gate, ld, b_mat, c_mat, d_own = head_input[0], gate_input[0], log_decay[0], in_b[0], in_c[0], d_out[0]
+    x, gate, ld, b_mat, c_mat, d_own = head_input[0], gate_input[0], log_decay.transpose(1, 0, 2), in_b[0], in_c[0], d_out[0]
     length, width = x.shape
     heads, state = ld.shape[0], b_mat.shape[1]
     model = w_out.shape[1]
@@ -441,14 +441,14 @@
         functools.partial(scan_forward, ranks, pitch, used, width),
         [pieces, pieces],
         [recv],
-        after=[y_local], name="scan_forward", us=0.3,
+        after=[y_local], far=(0, 1), name="scan_forward", us=0.3,
     )
     recv = exchange(send, "ctx")
     gated, normed, scale, part_left, part_right, part_next, part_prev, part_own = call(
         functools.partial(gate_out, ring, ranks, pitch),
         [(length, width)] * 2 + [(length, LANES)] + [(block, half)] * 2 + [(block, model)] * 3,
         [pos, recv, c_mat, cum_t, y_local, gate, gain, w_out],
-        smem=(0,), tiled=7, fixed=(2, 5, 7), io=True,
+        smem=(0,), tiled=7, fixed=(2, 5, 7), io=True, far=(3, 4, 5, 6, 7),
         scratch=[pltpu.VMEM((state, width), F32)] + [pltpu.VMEM((length, width), BF16)] * 2,
         name="gate_out", us=7,
     )
@@ -470,12 +470,13 @@
         scratch=[pltpu.VMEM((padded, width), BF16)] * 4,
         io=True, after=[d_normed], name="weight_grad", us=0.3,
     )
+    whole = grad_w
     grad_w = lax.psum_scatter(grad_w, "ctx", scatter_dimension=0, tiled=True, axis_index_groups=lines[0])
     send, dy = call(
         functools.partial(norm_grad, ranks, pitch),
         [pieces, (length, width)],
         [d_normed, gated, scale, gate, gain, c_mat, cum_t],
-        fixed=(3,), name="norm_grad", us=0.3,
+        fixed=(3,), after=[whole], name="norm_grad", us=0.3,
     )
     recv = exchange(send, "ctx")
     (dx_local,) = call(
@@ -485,7 +486,7 @@
         smem=(5,), fixed=(1, 2), name="local_grad", us=0.3,
     )
     part_next, part_prev = call(
-        pass_on, [(block, model)] * 2, [part_next, part_prev, up_far, down_far],
+        pass_on, [(block, model)] * 2, [part_next, part_prev, up_far, down_far], fixed=(0, 1),
         after=[dx_local], name="pass_on", us=0.3,
     )
     up, low = shifted(part_next, "tp", 1), shifted(part_prev, "tp", -1)
@@ -493,6 +494,7 @@
         functools.partial(scan_backward, ranks, pitch),
         [pieces],
         [recv, decays],
+        fixed=(1,),
         after=[part_next], name="scan_backward", us=0.3,
     )
     recv = exchange(send, "ctx")
@@ -504,7 +506,7 @@
         scratch=[pltpu.VMEM((state, width), F32)], name="finish", us=0.3,
     )
     out = part_own + up + low
-    grad_w, _, out = lax.optimization_barrier((grad_w, dx, out))
+    grad_w, *_ = lax.optimization_barrier((grad_w, dx, up, low))
     columns = [[seqs * i + p for i in line for p in range(seqs)] for line in lines[1]]
     grad_w = lax.all_to_all(grad_w, ("ctx", "dp"), 0, 0, tiled=True, axis_index_groups=columns)
     (share,) = call(

time: 161 us -> 153 us (0.950)
  blocking collectives: 33.2 us -> 17.9 us
  waiting for transfers between devices: 18.7 us -> 29.7 us
  local copies, waits for them, and re-layouts: 10.1 us -> 2.95 us
  starting transfers between devices: 38.1 us -> 41.2 us
    all_to_all x1 -> x0, blocking collectives: 17.3 us -> none  [per_device(): lax.all_to_all(grad_w, ('ctx', 'dp'), 0, 0, tiled=True, axis_index_groups...]
    all_to_all x0 -> x1, waiting for transfers between devices: none -> 11.4 us  [per_device(): lax.all_to_all(grad_w, ('ctx', 'dp'), 0, 0, tiled=True, axis_index_groups...]
    unnamed x39 -> x14, local copies, waits for them, and re-layouts: 8.59 us -> 1.5 us
    all_to_all x0 -> x1, starting transfers between devices: none -> 3.78 us  [per_device(): lax.all_to_all(grad_w, ('ctx', 'dp'), 0, 0, tiled=True, axis_index_groups...]
    ppermute x8, waiting for transfers between devices: 7.81 us -> 4.43 us  [shifted(): lax.ppermute(value, axis, [(i, (i + step) % count) for i in range(count)])]
    all_to_all x3, waiting for transfers between devices: 10.8 us -> 13.9 us  [exchange(): return lax.all_to_all(value, axis, 0, 0, tiled=True)]
    broadcast_in_dim x0 -> x1, other arithmetic: none -> 1.95 us  [per_device(): return (out[None], dx[None], share)]
    add x1 -> x0, other arithmetic: 1.95 us -> none  [per_device(): out = part_own + up + low]
  transfers between devices with their start and end apart: 13 -> 14, of which waited for: 6 -> 6; matrix products, arithmetic and copies ran while one was open for 3% -> 2% of each run, Pallas kernels for 21% -> 23%
where the time goes in v5:
time: 153 us; the launch traced here: 152 us
  Pallas kernels  44 us (29%)
  starting transfers between devices  41.2 us (27%)
  waiting for transfers between devices  29.7 us (19%)
  blocking collectives  17.9 us (12%)
  between operations  14.3 us (9%)
  local copies, waits for them, and re-layouts  2.95 us (2%)
  other arithmetic  2.03 us (1%)
    pallas_call x13, Pallas kernels, call(): pl.pallas_call(run, out_shape=[pltpu.HBM(o.shape, o.dtype) if j in far el...  44 us
    all_to_all x3, starting transfers between devices, exchange(): return lax.all_to_all(value, axis, 0, 0, tiled=True)  20.1 us
    all_to_all x1, blocking collectives, exchange(): return lax.all_to_all(value, axis, 0, 0, tiled=True)  17.9 us
    ppermute x8, starting transfers between devices, shifted(): lax.ppermute(value, axis, [(i, (i + step) % count) for i in range(count)])  17 us
    all_to_all x3, waiting for transfers between devices, exchange(): return lax.all_to_all(value, axis, 0, 0, tiled=True)  13.9 us
    all_to_all x1, waiting for transfers between devices, per_device(): lax.all_to_all(grad_w, ('ctx', 'dp'), 0, 0, tiled=True, axis_index_groups...  11.4 us
    ppermute x8, waiting for transfers between devices, shifted(): lax.ppermute(value, axis, [(i, (i + step) % count) for i in range(count)])  4.43 us
    all_to_all x1, starting transfers between devices, per_device(): lax.all_to_all(grad_w, ('ctx', 'dp'), 0, 0, tiled=True, axis_index_groups...  3.78 us
  transfers between devices with their start and end apart: 14, of which 6 were waited for; matrix products, arithmetic and copies ran while one was open for 2% of the time, Pallas kernels for 23%

profile of v5, /device:TPU:2, one launch (start us, length us, event | category | flops | bytes accessed | tf_op | source)
XLA Modules:
  0.0 152.1 jit_solution(694577831629424203)
XLA Ops:
  7.2 6.4 %collective-permute-start.3 = (f32[56,2560]{1,0:T(8,128)}, f32[56,2560]{1,0:T(8,128)S(1)}, u32[]{:S(2)}, u32[]{:S(2)}) collective-permute-start(f32[56,2560]{1,0:T(8,128)} %bitcast.32), channel_id=1, source_target_pairs={{0,6},{2,0},{4,2},{6,4},{1,7},{3,1},{5,3},{7,5},{8,14},{10,8},{12,... | collective-permute-start | bytes 1720328 | tf_op jit(solution)/shard_map/ppermute | solution.py:388
  13.5 0.0 collective-permute-start.2
  13.5 3.1 %block_state.1 = (f32[768,128]{1,0:T(8,128)}, f32[10,224]{1,0:T(8,128)S(1)}, f32[224,10]{1,0:T(8,128)S(1)}) custom-call(f32[10,1,224]{2,1,0:T(1,128)} %bitcast.46, f32[224,640]{1,0:T(8,128)} %bitcast.37, f32[224,128]{1,0:T(8,128)} %bitcast.39), custom_call_target="tpu_custom_call" | custom-call | bytes 900000 | tf_op jit(solution)/shard_map/block_state/pallas_call | solution.py:86
  16.6 7.6 %all-to-all-start = ((f32[32,24,128]{2,1,0:T(8,128)}), f32[32,24,128]{2,1,0:T(8,128)S(1)}, u32[]{:S(2)}, u32[]{:S(2)}) async-start(f32[32,24,128]{2,1,0:T(8,128)} %bitcast.6), calls=%async_computation | async-start | bytes 786432 | tf_op jit(solution)/shard_map/all_to_all | solution.py:396
  24.3 0.0 copy-start.2
  24.3 0.6 copy-done.2
  24.9 0.0 copy-start.5
  24.9 3.4 %local_output.1.refs_1_.refs_4_ = f32[224,640]{1,0:T(8,128)S(1)} custom-call(f32[224,640]{1,0:T(8,128)} %bitcast.38, f32[224,128]{1,0:T(8,128)} %bitcast.40, f32[224,128]{1,0:T(8,128)} %bitcast.23, f32[10,224]{1,0:T(8,128)S(1)} %get-tuple-element.26.refs_3_, f32[224,10]{1,0:T(8,128)S(1)} %get-tuple-element.27.refs_4_.refs_3_.refs_6_.refs_2_, f32[10]{0:T(128)S(1)} %copy-done.2), custom_call_target="tpu_custom_call" | custom-call | bytes 900000 | tf_op jit(solution)/shard_map/local_output/pallas_call | solution.py:86
  28.3 5.0 %all-to-all-done = f32[32,24,128]{2,1,0:T(8,128)S(1)} async-done(((f32[32,24,128]{2,1,0:T(8,128)}), f32[32,24,128]{2,1,0:T(8,128)S(1)}, u32[]{:S(2)}, u32[]{:S(2)}) %all-to-all-start) | async-done | bytes 393248 | tf_op jit(solution)/shard_map/all_to_all | solution.py:396
  33.3 1.3 scan_forward.1
  34.6 5.0 %all-to-all-start.1 = ((f32[32,24,128]{2,1,0:T(8,128)}), f32[32,24,128]{2,1,0:T(8,128)S(1)}, u32[]{:S(2)}, u32[]{:S(2)}) async-start(f32[32,24,128]{2,1,0:T(8,128)} %bitcast.45), calls=%async_computation.1 | async-start | bytes 786432 | tf_op jit(solution)/shard_map/all_to_all | solution.py:396
  39.6 0.0 reduce-scatter.2.cloned.1.call-start
  39.7 0.0 collective-permute-done.3.refs_3_
  39.7 0.7 slice.9
  40.4 4.1 %collective-permute-start.5 = (f32[56,1280]{1,0:T(8,128)}, f32[56,1280]{1,0:T(8,128)S(1)}, u32[]{:S(2)}, u32[]{:S(2)}) collective-permute-start(f32[56,1280]{1,0:T(8,128)} %slice.9), channel_id=1, source_target_pairs={{0,6},{2,0},{4,2},{6,4},{1,7},{3,1},{5,3},{7,5},{8,14},{10,8},{12,... | collective-permute-start | bytes 860168 | tf_op jit(solution)/shard_map/ppermute | solution.py:388
  44.6 0.0 collective-permute-done.2.refs_2_
  44.6 0.7 slice.8
  45.3 0.0 collective-permute-start.4
  45.3 0.0 copy-done.5
  45.3 0.1 pad_add_fusion.refs_0_
  45.4 3.5 %all-to-all-done.1 = f32[32,24,128]{2,1,0:T(8,128)S(1)} async-done(((f32[32,24,128]{2,1,0:T(8,128)}), f32[32,24,128]{2,1,0:T(8,128)S(1)}, u32[]{:S(2)}, u32[]{:S(2)}) %all-to-all-start.1) | async-done | bytes 393248 | tf_op jit(solution)/shard_map/all_to_all | solution.py:396
  48.8 0.0 copy-start.1
  48.8 8.9 %gate_out.1 = (f32[224,640]{1,0:T(8,128)S(1)}, f32[224,640]{1,0:T(8,128)S(1)}, f32[224,128]{1,0:T(8,128)S(1)}, f32[56,1280]{1,0:T(8,128)}, f32[56,1280]{1,0:T(8,...) custom-call(s32[3]{0:T(128)S(1)} %pad_add_fusion.refs_0_, f32[768,128]{1,0:T(8,128)S(1)} %bitcast.27, ...), custom_call_target="tpu_custom_call" | custom-call | bytes 21000000 | tf_op jit(solution)/shard_map/gate_out/pallas_call | solution.py:86
  57.7 0.0 collective-permute-done.5.refs_5_
  57.7 4.2 %collective-permute-done.4.refs_4_ = f32[56,1280]{1,0:T(8,128)S(1)} collective-permute-done((f32[56,1280]{1,0:T(8,128)}, f32[56,1280]{1,0:T(8,128)S(1)}, u32[]{:S(2)}, u32[]{:S(2)}) %collective-permute-start.4) | collective-permute-done | bytes 286752 | tf_op jit(solution)/shard_map/ppermute | solution.py:388
  61.9 0.0 copy-done.1
  61.9 3.1 %turn.1 = (f32[1280,256]{1,0:T(8,128)S(1)}, f32[1920,256]{1,0:T(8,128)S(1)}, bf16[2560,256]{1,0:T(8,128)(2,1)S(1)}, bf16[2560,256]{1,0:T(8,128)(2,1)S(1)}) custom-call(s32[3]{0:T(128)S(1)} %pad_add_fusion.refs_0_, f32[56,2560]{1,0:T(8,128)S(1)} %bitcast.34, f32[56,2560]{1,0:T(8,128)S(1)} %collective-permute-done.2.refs_2_, ...), custom_call_target="tpu_custom_call" | custom-call | bytes 900000 | tf_op jit(solution)/shard_map/turn/pallas_call | solution.py:86
  65.0 0.3 collective-permute-start.6
  65.3 6.0 %normed_grad.1.refs_3_.refs_0_ = f32[224,640]{1,0:T(8,128)S(1)} custom-call(bf16[2560,256]{1,0:T(8,128)(2,1)S(1)} %get-tuple-element.35.refs_0_, bf16[2560,256]{1,0:T(8,128)(2,1)S(1)} %get-tuple-element.36.refs_1_, f32[640,2560]{1,0:T(8,128)} %refs_2_.1), custom_call_target="tpu_custom_call" | custom-call | bytes 900000 | tf_op jit(solution)/shard_map/normed_grad/pallas_call | solution.py:86
  71.3 0.0 collective-permute-done.6.refs_1_
  71.4 5.4 %weight_grad.1.refs_7_ = f32[1280,640]{1,0:T(8,128)} custom-call(f32[1280,256]{1,0:T(8,128)S(1)} %get-tuple-element.39.refs_0_, f32[1920,256]{1,0:T(8,128)S(1)} %collective-permute-done.6.refs_1_, f32[224,640]{1,0:T(8,128)S(1)} %get-tuple-element.34.refs_6_.refs_2_, f32[224,640]{1,0:T(8,128)S(1)} %normed_grad.1.refs_3_.refs_0_), custom_call_target="tpu_custom_call" | custom-call | bytes 900000 | tf_op jit(solution)/shard_map/weight_grad/pallas_call | solution.py:86
  76.8 0.0 copy-start.6
  76.8 0.0 copy-start
  76.8 0.0 reduce-scatter.2.cloned.1.call-update
  76.8 0.1 collective-permute-start
  76.9 0.8 copy-done.6
  77.7 3.3 %collective-permute-start.1 = (f32[56,1280]{1,0:T(8,128)S(1)}, f32[56,1280]{1,0:T(8,128)S(1)}, u32[]{:S(2)}, u32[]{:S(2)}) collective-permute-start(f32[56,1280]{1,0:T(8,128)S(1)} %copy-done.6), channel_id=1, source_target_pairs={{0,6},{2,0},{4,2},{6,4},{1,7},{3,1},{5,3},{7,5},{8,14},{10,8},{12,... | collective-permute-start | bytes 860168 | tf_op jit(solution)/shard_map/ppermute | solution.py:388
  81.0 0.0 copy-done
  81.0 0.0 copy-start.3
  81.0 3.2 %norm_grad.1 = (f32[768,128]{1,0:T(8,128)}, f32[224,640]{1,0:T(8,128)S(1)}) custom-call(f32[224,640]{1,0:T(8,128)S(1)} %normed_grad.1.refs_3_.refs_0_, f32[224,640]{1,0:T(8,128)S(1)} %get-tuple-element.37.refs_1_, f32[224,128]{1,0:T(8,128)S(1)} %get-tuple-element.38.refs_2_, f32[224,640]{1,0:T(8,128)} %bitcast.36, ...), custom_call_target="tpu_custom_call" | custom-call | bytes 900000 | tf_op jit(solution)/shard_map/norm_grad/pallas_call | solution.py:86
  84.2 7.5 %all-to-all-start.2 = ((f32[32,24,128]{2,1,0:T(8,128)}), f32[32,24,128]{2,1,0:T(8,128)S(1)}, u32[]{:S(2)}, u32[]{:S(2)}) async-start(f32[32,24,128]{2,1,0:T(8,128)} %bitcast.14), calls=%async_computation.2 | async-start | bytes 786432 | tf_op jit(solution)/shard_map/all_to_all | solution.py:396
  91.7 0.0 copy-done.3
  91.8 3.4 %local_grad.1.refs_4_.refs_3_ = f32[224,640]{1,0:T(8,128)S(1)} custom-call(f32[224,640]{1,0:T(8,128)S(1)} %get-tuple-element.41.refs_0_, f32[224,128]{1,0:T(8,128)} %bitcast.41, f32[224,128]{1,0:T(8,128)} %bitcast.25, f32[10,224]{1,0:T(8,128)S(1)} %get-tuple-element.26.refs_3_, f32[224,10]{1,0:T(8,128)S(1)} %get-tuple-element.27.refs_4_.refs_3_.refs_6_.refs_2_, ...), custom_call_target="tpu_custom_call" | custom-call | bytes 900000 | tf_op jit(solution)/shard_map/local_grad/pallas_call | solution.py:86
  95.2 0.0 collective-permute-done.refs_2_
  95.2 0.0 collective-permute-done.1.refs_3_
  95.2 1.6 %pass_on.1 = (f32[56,2560]{1,0:T(8,128)S(1)}, f32[56,2560]{1,0:T(8,128)S(1)}) custom-call(f32[56,2560]{1,0:T(8,128)} %get-tuple-element.30.refs_0_, f32[56,2560]{1,0:T(8,128)} %get-tuple-element.31.refs_1_, f32[56,1280]{1,0:T(8,128)S(1)} %collective-permute-done.refs_2_, f32[56,1280]{1,0:T(8,128)S(1)} %collective-permute-done.1.refs_3_, ...), custom_call_target="tpu_custom_call" | custom-call | bytes 900000 | tf_op jit(solution)/shard_map/pass_on/pallas_call | solution.py:86
  96.8 3.1 %collective-permute-start.8 = (f32[56,2560]{1,0:T(8,128)S(1)}, f32[56,2560]{1,0:T(8,128)S(1)}, u32[]{:S(2)}, u32[]{:S(2)}) collective-permute-start(f32[56,2560]{1,0:T(8,128)S(1)} %get-tuple-element.43), channel_id=1, source_target_pairs={{0,6},{2,0},{4,2},{6,4},{1,7},{3,1},{5,3},{7,5},{8,14},{10,8},{12,... | collective-permute-start | bytes 1720328 | tf_op jit(solution)/shard_map/ppermute | solution.py:388
  99.9 0.0 collective-permute-start.7
  99.9 5.4 %all-to-all-done.2 = f32[32,24,128]{2,1,0:T(8,128)S(1)} async-done(((f32[32,24,128]{2,1,0:T(8,128)}), f32[32,24,128]{2,1,0:T(8,128)S(1)}, u32[]{:S(2)}, u32[]{:S(2)}) %all-to-all-start.2) | async-done | bytes 393248 | tf_op jit(solution)/shard_map/all_to_all | solution.py:396
  105.3 1.5 scan_backward.1
  106.8 0.0 copy-start.4
  106.8 17.9 %all_to_all.55 = f32[32,24,128]{2,1,0:T(8,128)S(1)} all-to-all(f32[32,24,128]{2,1,0:T(8,128)S(1)} %bitcast.31), channel_id=1, replica_groups=mesh['ctx'=32,'tp'=4,'dp'=2] {'ctx'}, dimensions={0} | all-to-all | bytes 786432 | tf_op jit(solution)/shard_map/all_to_all | solution.py:396
  124.7 2.4 %finish.1 = f32[224,640]{1,0:T(8,128)} custom-call(f32[768,128]{1,0:T(8,128)S(1)} %bitcast.28, f32[224,128]{1,0:T(8,128)} %bitcast.42, f32[224,10]{1,0:T(8,128)S(1)} %get-tuple-element.27.refs_4_.refs_3_.refs_6_.refs_2_, f32[224,640]{1,0:T(8,128)S(1)} %local_grad.1.refs_4_.refs_3_), custom_call_target="tpu_custom_call" | custom-call | bytes 900000 | tf_op jit(solution)/shard_map/finish/pallas_call | solution.py:86
  127.1 0.0 collective-permute-done.8
  127.1 0.2 collective-permute-done.7
  127.3 0.0 reduce-scatter.2.cloned.1.call-done
  127.3 3.8 %all-to-all-start.4 = ((f32[8,40,640]{2,1,0:T(8,128)}), f32[8,40,640]{2,1,0:T(8,128)S(1)}, u32[]{:S(2)}, u32[]{:S(2)}) async-start(f32[8,40,640]{2,1,0:T(8,128)} %bitcast.43), calls=%async_computation.5 | async-start | bytes 1638400 | tf_op jit(solution)/shard_map/all_to_all | solution.py:511
  131.1 0.0 copy-done.4
  131.1 1.9 %add_bitcast_fusion = f32[1,56,2560]{2,1,0:T(8,128)} fusion(f32[56,2560]{1,0:T(8,128)S(1)} %collective-permute-done.8, f32[56,2560]{1,0:T(8,128)S(1)} %copy-done.4, f32[56,2560]{1,0:T(8,128)} %collective-permute-done.7), kind=kLoop, calls=%fused_computation | loop fusion | flops 286720 | bytes 2293760 | tf_op jit(solution)/shard_map/broadcast_in_dim | solution.py:516
  133.0 11.4 %all-to-all-done.4 = f32[8,40,640]{2,1,0:T(8,128)S(1)} async-done(((f32[8,40,640]{2,1,0:T(8,128)}), f32[8,40,640]{2,1,0:T(8,128)S(1)}, u32[]{:S(2)}, u32[]{:S(2)}) %all-to-all-start.4) | async-done | bytes 819232 | tf_op jit(solution)/shard_map/all_to_all | solution.py:511
  144.4 0.8 sum_column.1
  (1 shorter events, 0.0 us)
Async XLA Ops:
  7.2 32.5 %collective-permute-start.3 = (f32[56,2560]{1,0:T(8,128)}, f32[56,2560]{1,0:T(8,128)S(1)}, u32[]{:S(2)}, u32[]{:S(2)}) collective-permute-start(f32[56,2560]{1,0:T(8,128)} %bitcast.32), channel_id=1, source_target_pairs={{0,6},{2,0},{4,2},{6,4},{1,7},{3,1},{5,3},{7,5},{8,14},{10,8},{12,... | collective-permute-start | bytes 1720328 | tf_op jit(solution)/shard_map/ppermute | solution.py:388
  13.5 31.0 %collective-permute-start.2 = (f32[56,2560]{1,0:T(8,128)}, f32[56,2560]{1,0:T(8,128)S(1)}, u32[]{:S(2)}, u32[]{:S(2)}) collective-permute-start(f32[56,2560]{1,0:T(8,128)} %bitcast.33), channel_id=1, source_target_pairs={{0,2},{2,4},{4,6},{6,0},{1,3},{3,5},{5,7},{7,1},{8,10},{10,12},{12... | collective-permute-start | bytes 1720328 | tf_op jit(solution)/shard_map/ppermute | solution.py:388
  16.6 16.7 %all-to-all-start = ((f32[32,24,128]{2,1,0:T(8,128)}), f32[32,24,128]{2,1,0:T(8,128)S(1)}, u32[]{:S(2)}, u32[]{:S(2)}) async-start(f32[32,24,128]{2,1,0:T(8,128)} %bitcast.6), calls=%async_computation | async-start | bytes 786432 | tf_op jit(solution)/shard_map/all_to_all | solution.py:396
  24.3 0.7 copy-start.2
  24.9 20.4 %copy-start.5 = (f32[640]{0:T(1024)S(1)}, f32[640]{0:T(1024)}, u32[]{:S(2)}) copy-start(f32[640]{0:T(1024)} %param.15) | copy-start | bytes 7684
  34.6 14.2 %all-to-all-start.1 = ((f32[32,24,128]{2,1,0:T(8,128)}), f32[32,24,128]{2,1,0:T(8,128)S(1)}, u32[]{:S(2)}, u32[]{:S(2)}) async-start(f32[32,24,128]{2,1,0:T(8,128)} %bitcast.45), calls=%async_computation.1 | async-start | bytes 786432 | tf_op jit(solution)/shard_map/all_to_all | solution.py:396
  39.6 87.7 %reduce-scatter.2.cloned.1.call-start = ((), (), s32[]{:S(2)}) async-start(), calls=%async_computation.6 | async-start | bytes 4096000 | tf_op jit(solution)/shard_map/reduce_scatter | solution.py:474
  40.4 17.3 %collective-permute-start.5 = (f32[56,1280]{1,0:T(8,128)}, f32[56,1280]{1,0:T(8,128)S(1)}, u32[]{:S(2)}, u32[]{:S(2)}) collective-permute-start(f32[56,1280]{1,0:T(8,128)} %slice.9), channel_id=1, source_target_pairs={{0,6},{2,0},{4,2},{6,4},{1,7},{3,1},{5,3},{7,5},{8,14},{10,8},{12,... | collective-permute-start | bytes 860168 | tf_op jit(solution)/shard_map/ppermute | solution.py:388
  45.3 16.6 %collective-permute-start.4 = (f32[56,1280]{1,0:T(8,128)}, f32[56,1280]{1,0:T(8,128)S(1)}, u32[]{:S(2)}, u32[]{:S(2)}) collective-permute-start(f32[56,1280]{1,0:T(8,128)} %slice.8), channel_id=1, source_target_pairs={{0,2},{2,4},{4,6},{6,0},{1,3},{3,5},{5,7},{7,1},{8,10},{10,12},{12... | collective-permute-start | bytes 860168 | tf_op jit(solution)/shard_map/ppermute | solution.py:388
  48.8 13.1 %copy-start.1 = (f32[1,56,2560]{2,1,0:T(8,128)S(1)}, f32[1,56,2560]{2,1,0:T(8,128)}, u32[]{:S(2)}) copy-start(f32[1,56,2560]{2,1,0:T(8,128)} %param.17) | copy-start | bytes 1720324
  65.0 6.3 %collective-permute-start.6 = (f32[1920,256]{1,0:T(8,128)S(1)}, f32[1920,256]{1,0:T(8,128)S(1)}, u32[]{:S(2)}, u32[]{:S(2)}) collective-permute-start(f32[1920,256]{1,0:T(8,128)S(1)} %get-tuple-element.40), channel_id=1, source_target_pairs={{0,8},{8,0},{16,24},{24,16},{32,40},{40,32},{48,56},{56,48},{64,72... | collective-permute-start | bytes 5898248 | tf_op jit(solution)/shard_map/ppermute | solution.py:392
  76.8 1.0 copy-start.6
  76.8 4.3 %copy-start = (f32[1,224,128]{2,1,0:T(8,128)S(1)}, f32[1,224,128]{2,1,0:T(8,128)}, u32[]{:S(2)}) copy-start(f32[1,224,128]{2,1,0:T(8,128)} %param.13) | copy-start | bytes 344068
  76.8 18.3 %collective-permute-start = (f32[56,1280]{1,0:T(8,128)}, f32[56,1280]{1,0:T(8,128)S(1)}, u32[]{:S(2)}, u32[]{:S(2)}) collective-permute-start(f32[56,1280]{1,0:T(8,128)} %get-tuple-element.32), channel_id=1, source_target_pairs={{0,2},{2,4},{4,6},{6,0},{1,3},{3,5},{5,7},{7,1},{8,10},{10,12},{12... | collective-permute-start | bytes 860168 | tf_op jit(solution)/shard_map/ppermute | solution.py:388
  77.7 17.4 %collective-permute-start.1 = (f32[56,1280]{1,0:T(8,128)S(1)}, f32[56,1280]{1,0:T(8,128)S(1)}, u32[]{:S(2)}, u32[]{:S(2)}) collective-permute-start(f32[56,1280]{1,0:T(8,128)S(1)} %copy-done.6), channel_id=1, source_target_pairs={{0,6},{2,0},{4,2},{6,4},{1,7},{3,1},{5,3},{7,5},{8,14},{10,8},{12,... | collective-permute-start | bytes 860168 | tf_op jit(solution)/shard_map/ppermute | solution.py:388
  81.0 10.7 %copy-start.3 = (f32[10]{0:T(128)S(1)}, f32[10]{0:T(128)}, u32[]{:S(2)}) copy-start(f32[10]{0:T(128)} %refs_5_.3) | copy-start | bytes 124
  84.2 21.1 %all-to-all-start.2 = ((f32[32,24,128]{2,1,0:T(8,128)}), f32[32,24,128]{2,1,0:T(8,128)S(1)}, u32[]{:S(2)}, u32[]{:S(2)}) async-start(f32[32,24,128]{2,1,0:T(8,128)} %bitcast.14), calls=%async_computation.2 | async-start | bytes 786432 | tf_op jit(solution)/shard_map/all_to_all | solution.py:396
  96.8 30.3 %collective-permute-start.8 = (f32[56,2560]{1,0:T(8,128)S(1)}, f32[56,2560]{1,0:T(8,128)S(1)}, u32[]{:S(2)}, u32[]{:S(2)}) collective-permute-start(f32[56,2560]{1,0:T(8,128)S(1)} %get-tuple-element.43), channel_id=1, source_target_pairs={{0,6},{2,0},{4,2},{6,4},{1,7},{3,1},{5,3},{7,5},{8,14},{10,8},{12,... | collective-permute-start | bytes 1720328 | tf_op jit(solution)/shard_map/ppermute | solution.py:388
  99.9 27.4 %collective-permute-start.7 = (f32[56,2560]{1,0:T(8,128)S(1)}, f32[56,2560]{1,0:T(8,128)}, u32[]{:S(2)}, u32[]{:S(2)}) collective-permute-start(f32[56,2560]{1,0:T(8,128)S(1)} %get-tuple-element.42.refs_2_), channel_id=1, source_target_pairs={{0,2},{2,4},{4,6},{6,0},{1,3},{3,5},{5,7},{7,1},{8,10},{10,12},{12... | collective-permute-start | bytes 1720328 | tf_op jit(solution)/shard_map/ppermute | solution.py:388
  106.8 24.3 %copy-start.4 = (f32[56,2560]{1,0:T(8,128)S(1)}, f32[56,2560]{1,0:T(8,128)}, u32[]{:S(2)}) copy-start(f32[56,2560]{1,0:T(8,128)} %get-tuple-element.29) | copy-start | bytes 1720324
  127.3 17.1 %all-to-all-start.4 = ((f32[8,40,640]{2,1,0:T(8,128)}), f32[8,40,640]{2,1,0:T(8,128)S(1)}, u32[]{:S(2)}, u32[]{:S(2)}) async-start(f32[8,40,640]{2,1,0:T(8,128)} %bitcast.43), calls=%async_computation.5 | async-start | bytes 1638400 | tf_op jit(solution)/shard_map/all_to_all | solution.py:511
Sparse Core Ops, SparseCore 0:
  76.9 45.7 reduce-scatter.1

commit v6 on v5

--- a/solution.py
+++ b/solution.py
@@ -250,7 +250,7 @@
     half = far_left_ref.shape[1]
     for side, far_ref in enumerate((far_left_ref, far_right_ref)):
 
-        @pl.loop(0, half // TILE)
+        @pl.loop(0, half // TILE, unroll=5)
         def _(n):
             k = side * (half // TILE) + n
             io.tile(7, k).wait()
@@ -298,7 +298,7 @@
 def normed_grad(io, high_ref, low_ref, w_ref, dn_ref, sum_ref):
     sum_ref[...] = jnp.zeros_like(sum_ref)
 
-    @pl.loop(0, w_ref.shape[1] // TILE)
+    @pl.loop(0, w_ref.shape[1] // TILE, unroll=5)
     def _(k):
         io.tile(2, k).wait()
         here = pl.ds(pl.multiple_of(k * TILE, TILE), TILE)

time: 153 us -> 154 us (level)
  waiting for transfers between devices: 29.7 us -> 25.9 us
  Pallas kernels: 44 us -> 47.7 us
  starting transfers between devices: 41.2 us -> 43.1 us
    pallas_call x13, Pallas kernels: 44 us -> 47.7 us  [call(): pl.pallas_call(run, out_shape=[pltpu.HBM(o.shape, o.dtype) if j in far el...]
    ppermute x8, waiting for transfers between devices: 4.43 us -> 1.68 us  [shifted(): lax.ppermute(value, axis, [(i, (i + step) % count) for i in range(count)])]
    all_to_all x1, starting transfers between devices: 3.78 us -> 5.63 us  [per_device(): lax.all_to_all(grad_w, ('ctx', 'dp'), 0, 0, tiled=True, axis_index_groups...]
  transfers between devices with their start and end apart: 14 -> 14, of which waited for: 6 -> 5; matrix products, arithmetic and copies ran while one was open for 2% -> 2% of each run, Pallas kernels for 23% -> 25%
where the time goes in v6:
time: 154 us; the launch traced here: 153 us
  Pallas kernels  47.7 us (31%)
  starting transfers between devices  43.1 us (28%)
  waiting for transfers between devices  25.9 us (17%)
  blocking collectives  17.8 us (12%)
  between operations  14.3 us (9%)
  local copies, waits for them, and re-layouts  2.67 us (2%)
  other arithmetic  2.03 us (1%)
    pallas_call x13, Pallas kernels, call(): pl.pallas_call(run, out_shape=[pltpu.HBM(o.shape, o.dtype) if j in far el...  47.7 us
    all_to_all x3, starting transfers between devices, exchange(): return lax.all_to_all(value, axis, 0, 0, tiled=True)  20.1 us
    all_to_all x1, blocking collectives, exchange(): return lax.all_to_all(value, axis, 0, 0, tiled=True)  17.8 us
    ppermute x8, starting transfers between devices, shifted(): lax.ppermute(value, axis, [(i, (i + step) % count) for i in range(count)])  17.2 us
    all_to_all x3, waiting for transfers between devices, exchange(): return lax.all_to_all(value, axis, 0, 0, tiled=True)  14 us
    all_to_all x1, waiting for transfers between devices, per_device(): lax.all_to_all(grad_w, ('ctx', 'dp'), 0, 0, tiled=True, axis_index_groups...  10.2 us
    all_to_all x1, starting transfers between devices, per_device(): lax.all_to_all(grad_w, ('ctx', 'dp'), 0, 0, tiled=True, axis_index_groups...  5.63 us
  transfers between devices with their start and end apart: 14, of which 5 were waited for; matrix products, arithmetic and copies ran while one was open for 2% of the time, Pallas kernels for 25%

profile of v6, /device:TPU:2, one launch (start us, length us, event | category | flops | bytes accessed | tf_op | source)
XLA Modules:
  0.0 153.4 jit_solution(5412680971548445736)
XLA Ops:
  7.2 6.4 %collective-permute-start.3 = (f32[56,2560]{1,0:T(8,128)}, f32[56,2560]{1,0:T(8,128)S(1)}, u32[]{:S(2)}, u32[]{:S(2)}) collective-permute-start(f32[56,2560]{1,0:T(8,128)} %bitcast.32), channel_id=1, source_target_pairs={{0,6},{2,0},{4,2},{6,4},{1,7},{3,1},{5,3},{7,5},{8,14},{10,8},{12,... | collective-permute-start | bytes 1720328 | tf_op jit(solution)/shard_map/ppermute | solution.py:388
  13.5 0.0 collective-permute-start.2
  13.5 3.1 %block_state.1 = (f32[768,128]{1,0:T(8,128)}, f32[10,224]{1,0:T(8,128)S(1)}, f32[224,10]{1,0:T(8,128)S(1)}) custom-call(f32[10,1,224]{2,1,0:T(1,128)} %bitcast.46, f32[224,640]{1,0:T(8,128)} %bitcast.37, f32[224,128]{1,0:T(8,128)} %bitcast.39), custom_call_target="tpu_custom_call" | custom-call | bytes 900000 | tf_op jit(solution)/shard_map/block_state/pallas_call | solution.py:86
  16.6 7.6 %all-to-all-start = ((f32[32,24,128]{2,1,0:T(8,128)}), f32[32,24,128]{2,1,0:T(8,128)S(1)}, u32[]{:S(2)}, u32[]{:S(2)}) async-start(f32[32,24,128]{2,1,0:T(8,128)} %bitcast.6), calls=%async_computation | async-start | bytes 786432 | tf_op jit(solution)/shard_map/all_to_all | solution.py:396
  24.3 0.0 copy-start.2
  24.3 0.6 copy-done.2
  24.9 0.0 copy-start.5
  24.9 3.4 %local_output.1.refs_1_.refs_4_ = f32[224,640]{1,0:T(8,128)S(1)} custom-call(f32[224,640]{1,0:T(8,128)} %bitcast.38, f32[224,128]{1,0:T(8,128)} %bitcast.40, f32[224,128]{1,0:T(8,128)} %bitcast.23, f32[10,224]{1,0:T(8,128)S(1)} %get-tuple-element.26.refs_3_, f32[224,10]{1,0:T(8,128)S(1)} %get-tuple-element.27.refs_4_.refs_3_.refs_6_.refs_2_, f32[10]{0:T(128)S(1)} %copy-done.2), custom_call_target="tpu_custom_call" | custom-call | bytes 900000 | tf_op jit(solution)/shard_map/local_output/pallas_call | solution.py:86
  28.3 5.0 %all-to-all-done = f32[32,24,128]{2,1,0:T(8,128)S(1)} async-done(((f32[32,24,128]{2,1,0:T(8,128)}), f32[32,24,128]{2,1,0:T(8,128)S(1)}, u32[]{:S(2)}, u32[]{:S(2)}) %all-to-all-start) | async-done | bytes 393248 | tf_op jit(solution)/shard_map/all_to_all | solution.py:396
  33.3 1.3 scan_forward.1
  34.6 5.0 %all-to-all-start.1 = ((f32[32,24,128]{2,1,0:T(8,128)}), f32[32,24,128]{2,1,0:T(8,128)S(1)}, u32[]{:S(2)}, u32[]{:S(2)}) async-start(f32[32,24,128]{2,1,0:T(8,128)} %bitcast.45), calls=%async_computation.1 | async-start | bytes 786432 | tf_op jit(solution)/shard_map/all_to_all | solution.py:396
  39.6 0.0 reduce-scatter.2.cloned.1.call-start
  39.7 0.0 collective-permute-done.3.refs_3_
  39.7 0.7 slice.9
  40.4 4.1 %collective-permute-start.5 = (f32[56,1280]{1,0:T(8,128)}, f32[56,1280]{1,0:T(8,128)S(1)}, u32[]{:S(2)}, u32[]{:S(2)}) collective-permute-start(f32[56,1280]{1,0:T(8,128)} %slice.9), channel_id=1, source_target_pairs={{0,6},{2,0},{4,2},{6,4},{1,7},{3,1},{5,3},{7,5},{8,14},{10,8},{12,... | collective-permute-start | bytes 860168 | tf_op jit(solution)/shard_map/ppermute | solution.py:388
  44.6 0.0 collective-permute-done.2.refs_2_
  44.6 0.7 slice.8
  45.3 0.0 collective-permute-start.4
  45.3 0.0 copy-done.5
  45.3 0.1 pad_add_fusion.refs_0_
  45.4 3.5 %all-to-all-done.1 = f32[32,24,128]{2,1,0:T(8,128)S(1)} async-done(((f32[32,24,128]{2,1,0:T(8,128)}), f32[32,24,128]{2,1,0:T(8,128)S(1)}, u32[]{:S(2)}, u32[]{:S(2)}) %all-to-all-start.1) | async-done | bytes 393248 | tf_op jit(solution)/shard_map/all_to_all | solution.py:396
  48.8 0.0 copy-start.1
  48.8 11.4 %gate_out.1 = (f32[224,640]{1,0:T(8,128)S(1)}, f32[224,640]{1,0:T(8,128)S(1)}, f32[224,128]{1,0:T(8,128)S(1)}, f32[56,1280]{1,0:T(8,128)}, f32[56,1280]{1,0:T(8,...) custom-call(s32[3]{0:T(128)S(1)} %pad_add_fusion.refs_0_, f32[768,128]{1,0:T(8,128)S(1)} %bitcast.27, ...), custom_call_target="tpu_custom_call" | custom-call | bytes 21000000 | tf_op jit(solution)/shard_map/gate_out/pallas_call | solution.py:86
  60.2 0.0 collective-permute-done.5.refs_5_
  60.2 1.7 %collective-permute-done.4.refs_4_ = f32[56,1280]{1,0:T(8,128)S(1)} collective-permute-done((f32[56,1280]{1,0:T(8,128)}, f32[56,1280]{1,0:T(8,128)S(1)}, u32[]{:S(2)}, u32[]{:S(2)}) %collective-permute-start.4) | collective-permute-done | bytes 286752 | tf_op jit(solution)/shard_map/ppermute | solution.py:388
  61.9 0.0 copy-done.1
  61.9 3.1 %turn.1 = (f32[1280,256]{1,0:T(8,128)S(1)}, f32[1920,256]{1,0:T(8,128)S(1)}, bf16[2560,256]{1,0:T(8,128)(2,1)S(1)}, bf16[2560,256]{1,0:T(8,128)(2,1)S(1)}) custom-call(s32[3]{0:T(128)S(1)} %pad_add_fusion.refs_0_, f32[56,2560]{1,0:T(8,128)S(1)} %bitcast.34, f32[56,2560]{1,0:T(8,128)S(1)} %collective-permute-done.2.refs_2_, ...), custom_call_target="tpu_custom_call" | custom-call | bytes 900000 | tf_op jit(solution)/shard_map/turn/pallas_call | solution.py:86
  65.0 0.1 collective-permute-start.6
  65.1 7.1 %normed_grad.1.refs_3_.refs_0_ = f32[224,640]{1,0:T(8,128)S(1)} custom-call(bf16[2560,256]{1,0:T(8,128)(2,1)S(1)} %get-tuple-element.35.refs_0_, bf16[2560,256]{1,0:T(8,128)(2,1)S(1)} %get-tuple-element.36.refs_1_, f32[640,2560]{1,0:T(8,128)} %refs_2_.1), custom_call_target="tpu_custom_call" | custom-call | bytes 900000 | tf_op jit(solution)/shard_map/normed_grad/pallas_call | solution.py:86
  72.2 0.0 collective-permute-done.6.refs_1_
  72.3 5.4 %weight_grad.1.refs_7_ = f32[1280,640]{1,0:T(8,128)} custom-call(f32[1280,256]{1,0:T(8,128)S(1)} %get-tuple-element.39.refs_0_, f32[1920,256]{1,0:T(8,128)S(1)} %collective-permute-done.6.refs_1_, f32[224,640]{1,0:T(8,128)S(1)} %get-tuple-element.34.refs_6_.refs_2_, f32[224,640]{1,0:T(8,128)S(1)} %normed_grad.1.refs_3_.refs_0_), custom_call_target="tpu_custom_call" | custom-call | bytes 900000 | tf_op jit(solution)/shard_map/weight_grad/pallas_call | solution.py:86
  77.7 0.0 copy-start.6
  77.7 0.0 copy-start
  77.7 0.0 reduce-scatter.2.cloned.1.call-update
  77.7 0.4 collective-permute-start
  78.1 0.5 copy-done.6
  78.6 3.3 %collective-permute-start.1 = (f32[56,1280]{1,0:T(8,128)S(1)}, f32[56,1280]{1,0:T(8,128)S(1)}, u32[]{:S(2)}, u32[]{:S(2)}) collective-permute-start(f32[56,1280]{1,0:T(8,128)S(1)} %copy-done.6), channel_id=1, source_target_pairs={{0,6},{2,0},{4,2},{6,4},{1,7},{3,1},{5,3},{7,5},{8,14},{10,8},{12,... | collective-permute-start | bytes 860168 | tf_op jit(solution)/shard_map/ppermute | solution.py:388
  81.9 0.0 copy-done
  81.9 0.0 copy-start.3
  82.0 3.2 %norm_grad.1 = (f32[768,128]{1,0:T(8,128)}, f32[224,640]{1,0:T(8,128)S(1)}) custom-call(f32[224,640]{1,0:T(8,128)S(1)} %normed_grad.1.refs_3_.refs_0_, f32[224,640]{1,0:T(8,128)S(1)} %get-tuple-element.37.refs_1_, f32[224,128]{1,0:T(8,128)S(1)} %get-tuple-element.38.refs_2_, f32[224,640]{1,0:T(8,128)} %bitcast.36, ...), custom_call_target="tpu_custom_call" | custom-call | bytes 900000 | tf_op jit(solution)/shard_map/norm_grad/pallas_call | solution.py:86
  85.1 7.5 %all-to-all-start.2 = ((f32[32,24,128]{2,1,0:T(8,128)}), f32[32,24,128]{2,1,0:T(8,128)S(1)}, u32[]{:S(2)}, u32[]{:S(2)}) async-start(f32[32,24,128]{2,1,0:T(8,128)} %bitcast.14), calls=%async_computation.2 | async-start | bytes 786432 | tf_op jit(solution)/shard_map/all_to_all | solution.py:396
  92.6 0.0 copy-done.3
  92.7 3.4 %local_grad.1.refs_4_.refs_3_ = f32[224,640]{1,0:T(8,128)S(1)} custom-call(f32[224,640]{1,0:T(8,128)S(1)} %get-tuple-element.41.refs_0_, f32[224,128]{1,0:T(8,128)} %bitcast.41, f32[224,128]{1,0:T(8,128)} %bitcast.25, f32[10,224]{1,0:T(8,128)S(1)} %get-tuple-element.26.refs_3_, f32[224,10]{1,0:T(8,128)S(1)} %get-tuple-element.27.refs_4_.refs_3_.refs_6_.refs_2_, ...), custom_call_target="tpu_custom_call" | custom-call | bytes 900000 | tf_op jit(solution)/shard_map/local_grad/pallas_call | solution.py:86
  96.1 0.0 collective-permute-done.refs_2_
  96.1 0.0 collective-permute-done.1.refs_3_
  96.1 1.6 %pass_on.1 = (f32[56,2560]{1,0:T(8,128)S(1)}, f32[56,2560]{1,0:T(8,128)S(1)}) custom-call(f32[56,2560]{1,0:T(8,128)} %get-tuple-element.30.refs_0_, f32[56,2560]{1,0:T(8,128)} %get-tuple-element.31.refs_1_, f32[56,1280]{1,0:T(8,128)S(1)} %collective-permute-done.refs_2_, f32[56,1280]{1,0:T(8,128)S(1)} %collective-permute-done.1.refs_3_, ...), custom_call_target="tpu_custom_call" | custom-call | bytes 900000 | tf_op jit(solution)/shard_map/pass_on/pallas_call | solution.py:86
  97.7 2.3 %collective-permute-start.8 = (f32[56,2560]{1,0:T(8,128)S(1)}, f32[56,2560]{1,0:T(8,128)S(1)}, u32[]{:S(2)}, u32[]{:S(2)}) collective-permute-start(f32[56,2560]{1,0:T(8,128)S(1)} %get-tuple-element.43), channel_id=1, source_target_pairs={{0,6},{2,0},{4,2},{6,4},{1,7},{3,1},{5,3},{7,5},{8,14},{10,8},{12,... | collective-permute-start | bytes 1720328 | tf_op jit(solution)/shard_map/ppermute | solution.py:388
  100.0 0.7 collective-permute-start.7
  100.7 5.5 %all-to-all-done.2 = f32[32,24,128]{2,1,0:T(8,128)S(1)} async-done(((f32[32,24,128]{2,1,0:T(8,128)}), f32[32,24,128]{2,1,0:T(8,128)S(1)}, u32[]{:S(2)}, u32[]{:S(2)}) %all-to-all-start.2) | async-done | bytes 393248 | tf_op jit(solution)/shard_map/all_to_all | solution.py:396
  106.2 1.5 scan_backward.1
  107.7 0.0 copy-start.4
  107.7 17.8 %all_to_all.55 = f32[32,24,128]{2,1,0:T(8,128)S(1)} all-to-all(f32[32,24,128]{2,1,0:T(8,128)S(1)} %bitcast.31), channel_id=1, replica_groups=mesh['ctx'=32,'tp'=4,'dp'=2] {'ctx'}, dimensions={0} | all-to-all | bytes 786432 | tf_op jit(solution)/shard_map/all_to_all | solution.py:396
  125.5 2.4 %finish.1 = f32[224,640]{1,0:T(8,128)} custom-call(f32[768,128]{1,0:T(8,128)S(1)} %bitcast.28, f32[224,128]{1,0:T(8,128)} %bitcast.42, f32[224,10]{1,0:T(8,128)S(1)} %get-tuple-element.27.refs_4_.refs_3_.refs_6_.refs_2_, f32[224,640]{1,0:T(8,128)S(1)} %local_grad.1.refs_4_.refs_3_), custom_call_target="tpu_custom_call" | custom-call | bytes 900000 | tf_op jit(solution)/shard_map/finish/pallas_call | solution.py:86
  127.9 0.0 collective-permute-done.8
  128.0 0.0 collective-permute-done.7
  128.0 0.0 reduce-scatter.2.cloned.1.call-done
  128.0 5.6 %all-to-all-start.4 = ((f32[8,40,640]{2,1,0:T(8,128)}), f32[8,40,640]{2,1,0:T(8,128)S(1)}, u32[]{:S(2)}, u32[]{:S(2)}) async-start(f32[8,40,640]{2,1,0:T(8,128)} %bitcast.43), calls=%async_computation.5 | async-start | bytes 1638400 | tf_op jit(solution)/shard_map/all_to_all | solution.py:511
  133.6 0.0 copy-done.4
  133.6 1.9 %add_bitcast_fusion = f32[1,56,2560]{2,1,0:T(8,128)} fusion(f32[56,2560]{1,0:T(8,128)S(1)} %collective-permute-done.8, f32[56,2560]{1,0:T(8,128)S(1)} %copy-done.4, f32[56,2560]{1,0:T(8,128)} %collective-permute-done.7), kind=kLoop, calls=%fused_computation | loop fusion | flops 286720 | bytes 2293760 | tf_op jit(solution)/shard_map/broadcast_in_dim | solution.py:516
  135.6 10.2 %all-to-all-done.4 = f32[8,40,640]{2,1,0:T(8,128)S(1)} async-done(((f32[8,40,640]{2,1,0:T(8,128)}), f32[8,40,640]{2,1,0:T(8,128)S(1)}, u32[]{:S(2)}, u32[]{:S(2)}) %all-to-all-start.4) | async-done | bytes 819232 | tf_op jit(solution)/shard_map/all_to_all | solution.py:511
  145.8 0.8 sum_column.1
  (1 shorter events, 0.0 us)
Async XLA Ops:
  7.2 32.5 %collective-permute-start.3 = (f32[56,2560]{1,0:T(8,128)}, f32[56,2560]{1,0:T(8,128)S(1)}, u32[]{:S(2)}, u32[]{:S(2)}) collective-permute-start(f32[56,2560]{1,0:T(8,128)} %bitcast.32), channel_id=1, source_target_pairs={{0,6},{2,0},{4,2},{6,4},{1,7},{3,1},{5,3},{7,5},{8,14},{10,8},{12,... | collective-permute-start | bytes 1720328 | tf_op jit(solution)/shard_map/ppermute | solution.py:388
  13.5 31.0 %collective-permute-start.2 = (f32[56,2560]{1,0:T(8,128)}, f32[56,2560]{1,0:T(8,128)S(1)}, u32[]{:S(2)}, u32[]{:S(2)}) collective-permute-start(f32[56,2560]{1,0:T(8,128)} %bitcast.33), channel_id=1, source_target_pairs={{0,2},{2,4},{4,6},{6,0},{1,3},{3,5},{5,7},{7,1},{8,10},{10,12},{12... | collective-permute-start | bytes 1720328 | tf_op jit(solution)/shard_map/ppermute | solution.py:388
  16.6 16.7 %all-to-all-start = ((f32[32,24,128]{2,1,0:T(8,128)}), f32[32,24,128]{2,1,0:T(8,128)S(1)}, u32[]{:S(2)}, u32[]{:S(2)}) async-start(f32[32,24,128]{2,1,0:T(8,128)} %bitcast.6), calls=%async_computation | async-start | bytes 786432 | tf_op jit(solution)/shard_map/all_to_all | solution.py:396
  24.3 0.7 copy-start.2
  24.9 20.4 %copy-start.5 = (f32[640]{0:T(1024)S(1)}, f32[640]{0:T(1024)}, u32[]{:S(2)}) copy-start(f32[640]{0:T(1024)} %param.15) | copy-start | bytes 7684
  34.6 14.2 %all-to-all-start.1 = ((f32[32,24,128]{2,1,0:T(8,128)}), f32[32,24,128]{2,1,0:T(8,128)S(1)}, u32[]{:S(2)}, u32[]{:S(2)}) async-start(f32[32,24,128]{2,1,0:T(8,128)} %bitcast.45), calls=%async_computation.1 | async-start | bytes 786432 | tf_op jit(solution)/shard_map/all_to_all | solution.py:396
  39.6 88.3 %reduce-scatter.2.cloned.1.call-start = ((), (), s32[]{:S(2)}) async-start(), calls=%async_computation.6 | async-start | bytes 4096000 | tf_op jit(solution)/shard_map/reduce_scatter | solution.py:474
  40.4 19.8 %collective-permute-start.5 = (f32[56,1280]{1,0:T(8,128)}, f32[56,1280]{1,0:T(8,128)S(1)}, u32[]{:S(2)}, u32[]{:S(2)}) collective-permute-start(f32[56,1280]{1,0:T(8,128)} %slice.9), channel_id=1, source_target_pairs={{0,6},{2,0},{4,2},{6,4},{1,7},{3,1},{5,3},{7,5},{8,14},{10,8},{12,... | collective-permute-start | bytes 860168 | tf_op jit(solution)/shard_map/ppermute | solution.py:388
  45.3 16.6 %collective-permute-start.4 = (f32[56,1280]{1,0:T(8,128)}, f32[56,1280]{1,0:T(8,128)S(1)}, u32[]{:S(2)}, u32[]{:S(2)}) collective-permute-start(f32[56,1280]{1,0:T(8,128)} %slice.8), channel_id=1, source_target_pairs={{0,2},{2,4},{4,6},{6,0},{1,3},{3,5},{5,7},{7,1},{8,10},{10,12},{12... | collective-permute-start | bytes 860168 | tf_op jit(solution)/shard_map/ppermute | solution.py:388
  48.8 13.1 %copy-start.1 = (f32[1,56,2560]{2,1,0:T(8,128)S(1)}, f32[1,56,2560]{2,1,0:T(8,128)}, u32[]{:S(2)}) copy-start(f32[1,56,2560]{2,1,0:T(8,128)} %param.17) | copy-start | bytes 1720324
  65.0 7.2 %collective-permute-start.6 = (f32[1920,256]{1,0:T(8,128)S(1)}, f32[1920,256]{1,0:T(8,128)S(1)}, u32[]{:S(2)}, u32[]{:S(2)}) collective-permute-start(f32[1920,256]{1,0:T(8,128)S(1)} %get-tuple-element.40), channel_id=1, source_target_pairs={{0,8},{8,0},{16,24},{24,16},{32,40},{40,32},{48,56},{56,48},{64,72... | collective-permute-start | bytes 5898248 | tf_op jit(solution)/shard_map/ppermute | solution.py:392
  77.7 1.0 copy-start.6
  77.7 4.3 %copy-start = (f32[1,224,128]{2,1,0:T(8,128)S(1)}, f32[1,224,128]{2,1,0:T(8,128)}, u32[]{:S(2)}) copy-start(f32[1,224,128]{2,1,0:T(8,128)} %param.13) | copy-start | bytes 344068
  77.7 18.3 %collective-permute-start = (f32[56,1280]{1,0:T(8,128)}, f32[56,1280]{1,0:T(8,128)S(1)}, u32[]{:S(2)}, u32[]{:S(2)}) collective-permute-start(f32[56,1280]{1,0:T(8,128)} %get-tuple-element.32), channel_id=1, source_target_pairs={{0,2},{2,4},{4,6},{6,0},{1,3},{3,5},{5,7},{7,1},{8,10},{10,12},{12... | collective-permute-start | bytes 860168 | tf_op jit(solution)/shard_map/ppermute | solution.py:388
  78.6 17.4 %collective-permute-start.1 = (f32[56,1280]{1,0:T(8,128)S(1)}, f32[56,1280]{1,0:T(8,128)S(1)}, u32[]{:S(2)}, u32[]{:S(2)}) collective-permute-start(f32[56,1280]{1,0:T(8,128)S(1)} %copy-done.6), channel_id=1, source_target_pairs={{0,6},{2,0},{4,2},{6,4},{1,7},{3,1},{5,3},{7,5},{8,14},{10,8},{12,... | collective-permute-start | bytes 860168 | tf_op jit(solution)/shard_map/ppermute | solution.py:388
  81.9 10.7 %copy-start.3 = (f32[10]{0:T(128)S(1)}, f32[10]{0:T(128)}, u32[]{:S(2)}) copy-start(f32[10]{0:T(128)} %refs_5_.3) | copy-start | bytes 124
  85.1 21.1 %all-to-all-start.2 = ((f32[32,24,128]{2,1,0:T(8,128)}), f32[32,24,128]{2,1,0:T(8,128)S(1)}, u32[]{:S(2)}, u32[]{:S(2)}) async-start(f32[32,24,128]{2,1,0:T(8,128)} %bitcast.14), calls=%async_computation.2 | async-start | bytes 786432 | tf_op jit(solution)/shard_map/all_to_all | solution.py:396
  97.7 30.2 %collective-permute-start.8 = (f32[56,2560]{1,0:T(8,128)S(1)}, f32[56,2560]{1,0:T(8,128)S(1)}, u32[]{:S(2)}, u32[]{:S(2)}) collective-permute-start(f32[56,2560]{1,0:T(8,128)S(1)} %get-tuple-element.43), channel_id=1, source_target_pairs={{0,6},{2,0},{4,2},{6,4},{1,7},{3,1},{5,3},{7,5},{8,14},{10,8},{12,... | collective-permute-start | bytes 1720328 | tf_op jit(solution)/shard_map/ppermute | solution.py:388
  100.0 27.9 %collective-permute-start.7 = (f32[56,2560]{1,0:T(8,128)S(1)}, f32[56,2560]{1,0:T(8,128)}, u32[]{:S(2)}, u32[]{:S(2)}) collective-permute-start(f32[56,2560]{1,0:T(8,128)S(1)} %get-tuple-element.42.refs_2_), channel_id=1, source_target_pairs={{0,2},{2,4},{4,6},{6,0},{1,3},{3,5},{5,7},{7,1},{8,10},{10,12},{12... | collective-permute-start | bytes 1720328 | tf_op jit(solution)/shard_map/ppermute | solution.py:388
  107.7 25.9 %copy-start.4 = (f32[56,2560]{1,0:T(8,128)S(1)}, f32[56,2560]{1,0:T(8,128)}, u32[]{:S(2)}) copy-start(f32[56,2560]{1,0:T(8,128)} %get-tuple-element.29) | copy-start | bytes 1720324
  128.0 17.8 %all-to-all-start.4 = ((f32[8,40,640]{2,1,0:T(8,128)}), f32[8,40,640]{2,1,0:T(8,128)S(1)}, u32[]{:S(2)}, u32[]{:S(2)}) async-start(f32[8,40,640]{2,1,0:T(8,128)} %bitcast.43), calls=%async_computation.5 | async-start | bytes 1638400 | tf_op jit(solution)/shard_map/all_to_all | solution.py:511
Sparse Core Ops, SparseCore 0:
  77.8 45.7 reduce-scatter.1
